TPU v7x, 256 devices: a whole 4x4x8 slice. The times are simulated.
256 devices in a mesh: lat: 64 (over y_lo, z, x), lon: 4 (over y_hi, core).
Axes of the slice: x: 4, y: 4 (y_hi: 2, y_lo: 2; y = y_hi * 2 + y_lo), z: 8, core: 2. Of those that a mesh axis runs over, the one named last changes fastest.
Arguments:
- grid_latent: bfloat16 [64, 4, 256, 512], P('lat', 'lon'), may hold values from -6 to 6
- mesh_latent: bfloat16 [256, 64, 512], P('lat', 'lon'), may hold values from -6 to 6
- cotangent: bfloat16 [64, 4, 256, 227], P('lat', 'lon'), may hold values from -6 to 6
- neighbours: int32 [64, 4, 3, 256], P('lat', 'lon'), may hold values from 0 to 106, as said below
- live: int32 [64, 4], P('lat', 'lon'), may hold values from 64 to 256, as said below
- w_em: bfloat16 [512, 512], replicated, may hold values from -0.25 to 0.25
- w_eg: bfloat16 [512, 512], replicated, may hold values from -0.25 to 0.25
- w_e2: bfloat16 [512, 512], replicated, may hold values from -0.25 to 0.25
- w_node: bfloat16 [1024, 512], replicated, may hold values from -0.1875 to 0.1875
- w_out: bfloat16 [512, 227], replicated, may hold values from -0.25 to 0.25
- bias_edge: float32 [512], replicated, may hold values from -3 to 3
- bias_node: float32 [512], replicated, may hold values from -3 to 3
Outputs:
- grid_grad: float32 [64, 4, 256, 512], P('lat', 'lon')
- mesh_grad: float32 [256, 64, 512], P('lat', 'lon')
- grad_em: float32 [512, 512], P('lat')
- grad_eg: float32 [512, 512], P('lat')
- grad_e2: float32 [512, 512], P('lat')
- grad_node: float32 [1024, 512], P('lat')
- grad_out: float32 [512, 227], P('lat')
Inputs may be any that keep to these rules, and one draw needn't show every extreme that they name: `neighbours`: slots count row by row over (6) x (18) slots; a point's three slots are some slot s, s + 1 and s + 18. Points 0 to live - 1 of a tile are real, the others padding.
All inputs are finite; a program needn't handle non-finite values.
Results may differ from a plain program's by a relative error of at most 0.018.
Values may be sent and summed in bfloat16 or wider, within the bound.
No kernel may reach another device: no remote copies, remote signals or barrier semaphores. Data moves between devices by JAX's collectives and lax.ppermute only.
A program may use at most 64 MiB of HBM per device.

v0:
```python
import jax
import jax.numpy as jnp
from jax import lax
from jax.sharding import PartitionSpec as P

D = 512


def with_halo(shard, sides, width, wrap):
    for axis, dim in sides:
        size, length = (lax.axis_size(axis), shard.shape[dim])
        up = [(i, (i + 1) % size) for i in range(size if wrap else size - 1)]
        down = [(j, i) for i, j in up]
        last = lax.slice_in_dim(shard, length - width, length, axis=dim)
        first = lax.slice_in_dim(shard, 0, width, axis=dim)
        before = lax.ppermute(last, axis, up)
        after = lax.ppermute(first, axis, down)
        shard = jnp.concatenate([before, shard, after], axis=dim)
    return shard


def from_behind(value, axis, steps):
    count = lax.axis_size(axis)
    first, last = (max(0, -steps), min(count, count - steps))
    return lax.ppermute(value, axis, [(source, source + steps) for source in range(first, last)])


def passed_along(block, axis, distance):
    devices = range(lax.axis_size(axis))
    route = [((i - distance) % len(devices), i) for i in devices]
    return lax.ppermute(block, axis, route)


def silu_grad(values):
    sigma = jax.nn.sigmoid(values)
    return sigma * (1.0 + values * (1.0 - sigma))


def on_device(
    grid_latent,
    mesh_latent,
    cotangent,
    neighbours,
    live,
    w_em,
    w_eg,
    w_e2,
    w_node,
    w_out,
    bias_edge,
    bias_node,
):
    grid_rows = grid_latent[0, 0]
    points = grid_rows.shape[0]
    mesh_rows, mesh_cols, feat_width = mesh_latent.shape
    cycle_slots = (mesh_rows + 2) * (mesh_cols + 2)
    extended = with_halo(mesh_latent, (("lon", 1),), 1, True)
    extended = with_halo(extended, (("lat", 0),), 1, False)
    projected = jnp.dot(
        extended.reshape(cycle_slots, feat_width), w_em, preferred_element_type=jnp.float32
    )
    slot_ids = neighbours[0, 0]
    grid_proj = jnp.dot(grid_rows, w_eg, preferred_element_type=jnp.float32) + bias_edge
    edge_pre = jnp.take(projected, slot_ids, axis=0) + grid_proj[None]
    edge_hidden = jax.nn.silu(edge_pre).astype(jnp.bfloat16)
    aggregate = jnp.einsum(
        "kpi,ij->pj", edge_hidden, w_e2, preferred_element_type=jnp.float32
    ).astype(jnp.bfloat16)
    node_pre = (
        jnp.dot(grid_rows, w_node[:D], preferred_element_type=jnp.float32)
        + jnp.dot(aggregate, w_node[D:], preferred_element_type=jnp.float32)
        + bias_node
    )
    node_hidden = jax.nn.silu(node_pre).astype(jnp.bfloat16)
    point_mask = lax.iota(jnp.int32, points) < live[0, 0]
    out_grad = jnp.where(point_mask[:, None], cotangent[0, 0], jnp.zeros((), jnp.bfloat16))
    node_grad = (
        jnp.dot(out_grad, w_out.T, preferred_element_type=jnp.float32) * silu_grad(node_pre)
    ).astype(jnp.bfloat16)
    grad_out = jnp.dot(node_hidden.T, out_grad, preferred_element_type=jnp.float32)
    grad_node = jnp.concatenate(
        [
            jnp.dot(grid_rows.T, node_grad, preferred_element_type=jnp.float32),
            jnp.dot(aggregate.T, node_grad, preferred_element_type=jnp.float32),
        ],
        axis=0,
    )
    agg_grad = jnp.dot(node_grad, w_node[D:].T, preferred_element_type=jnp.float32).astype(
        jnp.bfloat16
    )
    grad_e2 = jnp.einsum("kpi,pj->ij", edge_hidden, agg_grad, preferred_element_type=jnp.float32)
    hidden_grad = jnp.dot(agg_grad, w_e2.T, preferred_element_type=jnp.float32)
    edge_grad = (hidden_grad[None] * silu_grad(edge_pre)).astype(jnp.bfloat16)
    edge_sum = jnp.sum(edge_grad.astype(jnp.float32), axis=0).astype(jnp.bfloat16)
    grad_eg = jnp.dot(grid_rows.T, edge_sum, preferred_element_type=jnp.float32)
    grid_grad = jnp.dot(node_grad, w_node[:D].T, preferred_element_type=jnp.float32) + jnp.dot(
        edge_sum, w_eg.T, preferred_element_type=jnp.float32
    )
    slot_total = jax.ops.segment_sum(
        edge_grad.reshape(3 * points, feat_width).astype(jnp.float32),
        slot_ids.reshape(-1),
        num_segments=cycle_slots,
    )
    slot_total = slot_total.reshape(mesh_rows + 2, mesh_cols + 2, feat_width)
    from_south = from_behind(slot_total[0].astype(jnp.bfloat16), "lat", -1).astype(jnp.float32)
    from_north = from_behind(slot_total[mesh_rows + 1].astype(jnp.bfloat16), "lat", 1).astype(
        jnp.float32
    )
    inner = slot_total[1 : mesh_rows + 1]
    inner = inner.at[mesh_rows - 1].add(from_south).at[0].add(from_north)
    from_east = passed_along(inner[:, 0], "lon", -1)
    from_west = passed_along(inner[:, mesh_cols + 1], "lon", 1)
    owned = inner[:, 1 : mesh_cols + 1]
    owned = owned.at[:, mesh_cols - 1].add(from_east).at[:, 0].add(from_west)
    node_sum = owned.reshape(mesh_rows * mesh_cols, feat_width).astype(jnp.bfloat16)
    mesh_grad = jnp.dot(node_sum, w_em.T, preferred_element_type=jnp.float32).reshape(
        mesh_rows, mesh_cols, feat_width
    )
    grad_em = jnp.dot(
        mesh_latent.reshape(mesh_rows * mesh_cols, feat_width).T,
        node_sum,
        preferred_element_type=jnp.float32,
    )
    summed = (
        lax.psum(grad_em.astype(jnp.bfloat16), "lon").astype(jnp.float32),
        lax.psum(grad_eg.astype(jnp.bfloat16), "lon").astype(jnp.float32),
        lax.psum(grad_e2.astype(jnp.bfloat16), "lon").astype(jnp.float32),
        lax.psum(grad_node.astype(jnp.bfloat16), "lon").astype(jnp.float32),
        lax.psum(grad_out.astype(jnp.bfloat16), "lon").astype(jnp.float32),
    )
    shares = (
        lax.psum_scatter(summed[0], "lat", scatter_dimension=0, tiled=True),
        lax.psum_scatter(summed[1], "lat", scatter_dimension=0, tiled=True),
        lax.psum_scatter(summed[2], "lat", scatter_dimension=0, tiled=True),
        lax.psum_scatter(summed[3], "lat", scatter_dimension=0, tiled=True),
        lax.psum_scatter(summed[4], "lat", scatter_dimension=0, tiled=True),
    )
    return (
        grid_grad.reshape(1, 1, points, feat_width),
        mesh_grad,
        shares[0],
        shares[1],
        shares[2],
        shares[3],
        shares[4],
    )


def solution(mesh):
    in_specs = (
        P("lat", "lon", None, None),
        P("lat", "lon", None),
        P("lat", "lon", None, None),
        P("lat", "lon", None, None),
        P("lat", "lon"),
        P(),
        P(),
        P(),
        P(),
        P(),
        P(),
        P(),
    )
    out_specs = (
        P("lat", "lon", None, None),
        P("lat", "lon", None),
        P("lat", None),
        P("lat", None),
        P("lat", None),
        P("lat", None),
        P("lat", None),
    )
    return jax.shard_map(
        on_device, mesh=mesh, in_specs=in_specs, out_specs=out_specs, check_vma=False
    )
```

profile of v0, /device:TPU:16, one launch (start us, length us, event | category | flops | bytes accessed | tf_op | source)
XLA Modules:
  0.0 1726.7 jit_solution(11347635139435955648)
XLA Ops:
  8.2 3.2 collective-permute-start.1
  13.6 1.5 fusion.17
  15.1 1.3 convolution_add_fusion.2
  17.1 3.4 collective-permute-start.2
  20.5 1.3 collective-permute-start.3
  22.0 4.2 collective-permute-done.3
  26.6 2.2 gather_fusion
  31.5 1.1 fusion.42
  32.9 1.1 convolution_convert_fusion.1
  34.1 1.2 fusion.5
  35.9 1.6 fusion
  37.5 7.3 scatter_custom_fusion
  44.9 1.3 collective-permute-start.4
  46.2 1.1 fusion.4
  48.4 4.5 collective-permute-start.5
  53.0 1.4 collective-permute-done.5
  54.6 1.0 pad_maximum_fusion
  56.3 4.1 collective-permute-done.7
  60.4 1.1 fusion.6
  61.6 85.5 %all-reduce.3.cloned.1.call-done = (bf16[512,512]{0,1:T(8,128)(2,1)}, bf16[512,512]{0,1:T(8,128)(2,1)}, bf16[512,512]{1,0:T(8,128)(2,1)}, bf16[1024,512]{1,0:T(8,128)(2,1)}, bf16[512,227]{1,0:T(8,128)(2,1)}) async-done(((bf16[512,512]{0,1:T(8,128)(2,1)}, bf16[512,512]{0,1:T(8,128)(2,1)}, bf16[512,512]{1,0:T(8,128)(2,1)}, bf16[1024,512]{1,0:T(8,128)(2,1)}, bf16[512,227]{1,0:T(8,128)(2,1)}), ...) | async-done | bytes 2853904 | tf_op jit(solution)/shard_map/psum | solution.py:125
  147.1 1.9 convert_element_type.96
  149.0 1.2 copy.39
  150.3 1.2 copy.41
  151.6 1.1 convert_element_type.92
  153.0 1.6 convert_element_type.93
  154.7 1.2 copy-done.3
  156.2 1.1 fusion.7
  158.3 309.6 %reduce-scatter.14.cloned.1.call-done = f32[8,227]{1,0:T(8,128)} async-done(((f32[512,227]{1,0:T(8,128)}), f32[8,227]{1,0:T(8,128)}) %reduce-scatter.14.cloned.1.call-update) | async-done | bytes 7280 | tf_op jit(solution)/shard_map/reduce_scatter | solution.py:136
  467.9 312.6 %reduce-scatter.16.cloned.1.call-done = f32[8,512]{1,0:T(8,128)} async-done(((f32[512,512]{1,0:T(8,128)}), f32[8,512]{1,0:T(8,128)}) %reduce-scatter.16.cloned.1.call-update) | async-done | bytes 16400
  780.4 312.3 %reduce-scatter.18.cloned.1.call-done = f32[8,512]{1,0:T(8,128)} async-done(((f32[512,512]{1,0:T(8,128)}), f32[8,512]{1,0:T(8,128)}) %reduce-scatter.18.cloned.1.call-update) | async-done | bytes 16400
  1092.7 312.4 %reduce-scatter.10.cloned.1.call-done = f32[8,512]{1,0:T(8,128)} async-done(((f32[512,512]{1,0:T(8,128)}), f32[8,512]{1,0:T(8,128)}) %reduce-scatter.10.cloned.1.call-update) | async-done | bytes 16400 | tf_op jit(solution)/shard_map/reduce_scatter | solution.py:134
  1405.1 314.7 %reduce-scatter.12.cloned.1.call-done = f32[16,512]{1,0:T(8,128)} async-done(((f32[1024,512]{1,0:T(8,128)}), f32[16,512]{1,0:T(8,128)}) %reduce-scatter.12.cloned.1.call-update) | async-done | bytes 32784 | tf_op jit(solution)/shard_map/reduce_scatter | solution.py:135
  (98 shorter events, 11.2 us)
Async XLA Ops:
  7.2 22.1 %copy-start = (bf16[512,512]{1,0:T(8,128)(2,1)S(1)}, bf16[512,512]{1,0:T(8,128)(2,1)}, u32[]{:S(2)}) copy-start(bf16[512,512]{1,0:T(8,128)(2,1)} %param.27) | copy-start | bytes 1572868
  7.2 9.9 copy-start.16
  7.2 7.9 copy-start.4
  7.2 139.9 %all-reduce.3.cloned.1.call-start = ((), (), s32[]{:S(2)}) async-start(), calls=%async_computation.10 | async-start | bytes 5767168 | tf_op jit(solution)/shard_map/psum | solution.py:125
  8.2 8.9 collective-permute-start
  8.2 8.8 collective-permute-start.1
  13.6 12.7 copy-start.6
  17.1 4.9 collective-permute-start.2
  20.5 5.7 collective-permute-start.3
  28.7 1.2 copy-start.2
  28.7 1.2 copy-start.17
  31.5 2.6 copy-start.1
  37.5 9.8 copy-start.15
  37.5 9.8 copy-start.20
  44.9 8.1 collective-permute-start.4
  47.3 7.3 copy-start.8
  47.3 7.3 copy-start.9
  48.4 6.1 collective-permute-start.5
  54.5 1.8 collective-permute-start.6
  55.7 4.7 collective-permute-start.7
  61.6 406.3 %reduce-scatter.14.cloned.1.call-start = ((), (), s32[]{:S(2)}) async-start(), calls=%async_computation.7 | async-start | bytes 532480 | tf_op jit(solution)/shard_map/reduce_scatter | solution.py:136
  147.1 1.9 copy-start.13
  149.0 1.4 copy-start.12
  149.0 631.5 %reduce-scatter.16.cloned.1.call-start = ((), (), s32[]{:S(2)}) async-start(), calls=%async_computation.8 | async-start | bytes 1064960
  150.3 1.4 copy-start.11
  150.3 942.4 %reduce-scatter.18.cloned.1.call-start = ((), (), s32[]{:S(2)}) async-start(), calls=%async_computation.9 | async-start | bytes 1064960
  151.6 1.5 copy-start.10
  151.6 1253.6 %reduce-scatter.10.cloned.1.call-start = ((), (), s32[]{:S(2)}) async-start(), calls=%async_computation.5 | async-start | bytes 1064960 | tf_op jit(solution)/shard_map/reduce_scatter | solution.py:134
  152.8 1567.1 %reduce-scatter.12.cloned.1.call-start = ((), (), s32[]{:S(2)}) async-start(), calls=%async_computation.6 | async-start | bytes 2129920 | tf_op jit(solution)/shard_map/reduce_scatter | solution.py:135
  154.7 1.2 copy-start.3
  154.7 1.6 copy-start.5
  155.9 1.5 copy-start.7
  (3 other events, 2.8 us)
Sparse Core Ops, SparseCore 0:
  61.7 85.3 all-reduce.2
  150.2 317.6 reduce-scatter.13
  471.1 309.3 reduce-scatter.15
  783.4 309.2 reduce-scatter.17
  1095.8 309.3 reduce-scatter.9
  1408.0 311.7 reduce-scatter.11
where the time goes:
time: 1730 us
  waiting for transfers between devices  1660 us (96%)
  other arithmetic  18 us (1%)
    unnamed x8, waiting for transfers between devices  625 us
    reduce_scatter x1, waiting for transfers between devices, on_device(): lax.psum_scatter(summed[3], 'lat', scatter_dimension=0, tiled=True)  315 us
    reduce_scatter x1, waiting for transfers between devices, on_device(): lax.psum_scatter(summed[2], 'lat', scatter_dimension=0, tiled=True)  312 us
    reduce_scatter x1, waiting for transfers between devices, on_device(): lax.psum_scatter(summed[4], 'lat', scatter_dimension=0, tiled=True)  310 us
    psum x1, waiting for transfers between devices, on_device(): lax.psum(grad_em.astype(jnp.bfloat16), 'lon').astype(jnp.float32)  85.5 us
  transfers between devices with their start and end apart: 14, of which 10 were waited for; matrix products, arithmetic and copies ran while one was open for 1% of the time, Pallas kernels for 0%

commit v1 on v0

v1 whole, which is shorter than its diff:
```python
import functools

import jax
import jax.numpy as jnp
from jax import lax
from jax.experimental import pallas as pl
from jax.experimental.pallas import tpu as pltpu
from jax.sharding import Mesh
from jax.sharding import PartitionSpec as P

D = 512
CH = 227
LAT = ("y_lo", "z", "x")
LON = ("y_hi", "core")
SIZES = {"y_lo": 2, "z": 8, "x": 4, "y_hi": 2, "core": 2}
F32 = jnp.float32
BF = jnp.bfloat16
PANELS = 11


def mm(a, b):
    return lax.dot_general(a, b, (((1,), (0,)), ((), ())), preferred_element_type=F32)


def mm_nt(a, b):
    return lax.dot_general(a, b, (((1,), (1,)), ((), ())), preferred_element_type=F32)


def mm_tn(a, b):
    return lax.dot_general(a, b, (((0,), (0,)), ((), ())), preferred_element_type=F32)


def split(value):
    high = value.astype(BF)
    return high, (value - high.astype(F32)).astype(BF)


def halves(ref, value):
    width = value.shape[1] // 2
    ref[0] = value[:, :width].astype(ref.dtype)
    ref[1] = value[:, width:].astype(ref.dtype)


def main_kernel(
    live_ref,
    core_ref,
    nbr_ref,
    g_ref,
    ext_ref,
    cot_ref,
    w_em_ref,
    w_eg_ref,
    w_e2_ref,
    w_node_ref,
    w_out_ref,
    b_edge_ref,
    b_node_ref,
    grid_ref,
    slot_ref,
    keep_ref,
    send_ref,
    og_ref,
    wo_ref,
    ng_half,
    og_half,
    ag_half,
    es_half,
    sl_half,
    slope_ref,
):
    core = core_ref[0]
    g = g_ref[...]
    ext = ext_ref[...]
    points = g.shape[0]
    og_ref[...] = jnp.zeros_like(og_ref)
    wo_ref[...] = jnp.zeros_like(wo_ref)
    row = lax.broadcasted_iota(jnp.int32, (points, CH), 0)
    cot = cot_ref[...]
    og_ref[:, :CH] = jnp.where(row < live_ref[0], cot, jnp.zeros_like(cot))
    wo_ref[:, :CH] = w_out_ref[...]
    out_grad = og_ref[...]
    halves(og_half, out_grad)

    projected = mm(ext, w_em_ref[...])
    high, low = split(projected)
    both = jnp.concatenate([high, low], axis=0)
    grid_proj = mm(g, w_eg_ref[...]) + b_edge_ref[...]
    place = lax.broadcasted_iota(jnp.int32, (128, points), 0)
    hidden_sum = None
    hots = []
    for k in range(3):
        slot = nbr_ref[k : k + 1, :]
        r = (slot * 3641) >> 16
        c = slot - r * 18
        inner = jnp.where(
            c == 0, 99 + r, jnp.where(c == 17, 103 + r, (r - 1) * 16 + c - 1)
        )
        where = jnp.where(r == 0, 64 + c, jnp.where(r == 5, 82 + c, inner))
        hot = jnp.where(place == where, 1.0, 0.0).astype(BF)
        hots.append(hot)
        pre = mm_tn(jnp.concatenate([hot, hot], axis=0), both) + grid_proj
        sigma = jax.nn.sigmoid(pre)
        hidden = (pre * sigma).astype(BF)
        slope_ref[k] = sigma * (1.0 + pre * (1.0 - sigma))
        hidden = hidden.astype(F32)
        hidden_sum = hidden if hidden_sum is None else hidden_sum + hidden
    hs_high, hs_low = split(hidden_sum)
    aggregate = (mm(hs_high, w_e2_ref[...]) + mm(hs_low, w_e2_ref[...])).astype(BF)
    node_pre = mm(g, w_node_ref[:D, :]) + mm(aggregate, w_node_ref[D:, :]) + b_node_ref[...]
    sigma = jax.nn.sigmoid(node_pre)
    node_hidden = (node_pre * sigma).astype(BF)
    node_grad = (mm_nt(out_grad, wo_ref[...]) * (sigma * (1.0 + node_pre * (1.0 - sigma)))).astype(
        BF
    )
    halves(ng_half, node_grad)
    agg_grad = mm_nt(node_grad, w_node_ref[D:, :]).astype(BF)
    halves(ag_half, agg_grad)
    hidden_grad = mm_nt(agg_grad, w_e2_ref[...])
    edge_sum = None
    slots = None
    for k in range(3):
        edge_grad = (hidden_grad * slope_ref[k]).astype(BF)
        part = mm(hots[k], edge_grad)
        slots = part if slots is None else slots + part
        edge_grad = edge_grad.astype(F32)
        edge_sum = edge_grad if edge_sum is None else edge_sum + edge_grad
    edge_sum = edge_sum.astype(BF)
    halves(es_half, edge_sum)
    slot_ref[...] = slots
    sl_high, sl_low = split(slots)
    halves(sl_half, jnp.concatenate([sl_high, sl_low], axis=0))
    grid_ref[...] = mm_nt(node_grad, w_node_ref[:D, :]) + mm_nt(edge_sum, w_eg_ref[...])

    def put(ref, panel, value):
        v = value.reshape(16, 4, 8, 128)
        for x in range(4):
            ref[panel, x] = v[:, x].reshape(128, 128).astype(BF)

    def put_wide(ref, panel, value):
        put(ref, panel, value[:, :128])
        put(ref, panel + 1, value[:, 128:])

    ext_both = jnp.concatenate([ext, ext], axis=0)
    for ref, which in ((send_ref, 1 - core), (keep_ref, core)):
        put_wide(ref, 0, mm_tn(ext_both, sl_half[which]))
        put_wide(ref, 2, mm_tn(g, es_half[which]))
        ag = ag_half[which]
        put_wide(ref, 4, mm_tn(hs_high, ag) + mm_tn(hs_low, ag))
        ng = ng_half[which]
        for half, left in enumerate((g, aggregate)):
            value = mm_tn(left, ng)
            v = value.reshape(8, 4, 2, 8, 256)
            for x in range(4):
                for eight in range(2):
                    tile = v[:, x, eight].reshape(64, 256).astype(BF)
                    for wide in range(2):
                        ref[6 + 2 * eight + wide, x, half * 64 : half * 64 + 64, :] = tile[
                            :, wide * 128 : wide * 128 + 128
                        ]
        put(ref, 10, mm_tn(node_hidden, og_half[which]))


def vmem(n):
    return [pl.BlockSpec(memory_space=pltpu.VMEM)] * n


def smem(n):
    return [pl.BlockSpec(memory_space=pltpu.SMEM)] * n


PARAMS = pltpu.CompilerParams(vmem_limit_bytes=48 * 1024 * 1024)


def main_call(live, core, nbr, g, ext, cot, *weights):
    shape = jax.ShapeDtypeStruct
    return pl.pallas_call(
        main_kernel,
        out_shape=(
            shape((256, D), F32),
            shape((128, D), F32),
            shape((PANELS, 4, 128, 128), BF),
            shape((PANELS, 4, 128, 128), BF),
        ),
        in_specs=smem(2) + vmem(11),
        out_specs=tuple(vmem(4)),
        scratch_shapes=[
            pltpu.VMEM((256, 256), BF),
            pltpu.VMEM((D, 256), BF),
            pltpu.VMEM((2, 256, 256), BF),
            pltpu.VMEM((2, 256, 128), BF),
            pltpu.VMEM((2, 256, 256), BF),
            pltpu.VMEM((2, 256, 256), BF),
            pltpu.VMEM((2, 256, 256), BF),
            pltpu.VMEM((3, 256, D), F32),
        ],
        compiler_params=PARAMS,
        name="decoder_grads",
    )(live, core, nbr, g, ext, cot, *weights)


def core_sum_kernel(x_ref, keep_ref, got_ref, own_ref, *sends):
    x = x_ref[0]
    own_ref[...] = keep_ref[:, x].astype(F32) + got_ref[:, x].astype(F32)
    for step, ref in enumerate(sends):
        to = (x + step + 1) & 3
        ref[...] = (keep_ref[:, to].astype(F32) + got_ref[:, to].astype(F32)).astype(BF)


def core_sum(x, keep, got):
    shape = jax.ShapeDtypeStruct
    part = (PANELS, 128, 128)
    return pl.pallas_call(
        core_sum_kernel,
        out_shape=(shape(part, F32),) + (shape(part, BF),) * 3,
        in_specs=smem(1) + vmem(2),
        out_specs=tuple(vmem(4)),
        compiler_params=PARAMS,
        name="sum_over_core",
    )(x, keep, got)


def x_sum_kernel(own_ref, a_ref, b_ref, c_ref, out_ref):
    total = own_ref[...] + a_ref[...].astype(F32) + b_ref[...].astype(F32) + c_ref[...].astype(F32)
    total = total.reshape(PANELS, 16, 8, 128)
    for i in range(16):
        out_ref[i] = total[:, i].reshape(PANELS * 8, 128).astype(BF)


def x_sum(own, a, b, c):
    return pl.pallas_call(
        x_sum_kernel,
        out_shape=jax.ShapeDtypeStruct((16, PANELS * 8, 128), BF),
        in_specs=vmem(4),
        out_specs=vmem(1)[0],
        compiler_params=PARAMS,
        name="sum_over_x",
    )(own, a, b, c)


def last_kernel(in_ref, em_ref, eg_ref, e2_ref, node_ref, out_ref):
    for core in range(2):
        total = in_ref[core].astype(F32) + in_ref[core + 2].astype(F32)

        def panel(i):
            return total[8 * i : 8 * i + 8, :]

        for wide in range(2):
            at = slice((2 * core + wide) * 128, (2 * core + wide) * 128 + 128)
            em_ref[:, at] = panel(wide)
            eg_ref[:, at] = panel(2 + wide)
            e2_ref[:, at] = panel(4 + wide)
            node_ref[:8, at] = panel(6 + wide)
            node_ref[8:, at] = panel(8 + wide)
        if core == 0:
            out_ref[:, :128] = panel(10)
        else:
            out_ref[:, 128:] = panel(10)[:, : CH - 128]


def last(gathered):
    shape = jax.ShapeDtypeStruct
    return pl.pallas_call(
        last_kernel,
        out_shape=(
            shape((8, D), F32),
            shape((8, D), F32),
            shape((8, D), F32),
            shape((16, D), F32),
            shape((8, CH), F32),
        ),
        in_specs=vmem(1),
        out_specs=tuple(vmem(5)),
        compiler_params=PARAMS,
        name="sum_over_lon",
    )(gathered)


def shift(value, axes, steps, wrap):
    size = 1
    for a in axes:
        size *= SIZES[a]
    pairs = [(i, (i + steps) % size) for i in range(size) if wrap or 0 <= i + steps < size]
    return lax.ppermute(value, axes, pairs)


def on_device(
    grid_latent,
    mesh_latent,
    cotangent,
    neighbours,
    live,
    w_em,
    w_eg,
    w_e2,
    w_node,
    w_out,
    bias_edge,
    bias_node,
):
    west = shift(mesh_latent[:, 15], LON, 1, True)
    east = shift(mesh_latent[:, 0], LON, -1, True)
    top = jnp.concatenate([west[:1], mesh_latent[0], east[:1]], axis=0)
    bottom = jnp.concatenate([west[3:], mesh_latent[3], east[3:]], axis=0)
    north = shift(bottom, LAT, 1, False)
    south = shift(top, LAT, -1, False)
    ext = jnp.concatenate(
        [mesh_latent.reshape(64, D), north, south, west, east, jnp.zeros((20, D), BF)], axis=0
    )
    core = lax.axis_index("core").astype(jnp.int32).reshape(1)
    x = lax.axis_index("x").astype(jnp.int32).reshape(1)
    grid_grad, slots, keep, send = main_call(
        live.reshape(1),
        core,
        neighbours[0, 0],
        grid_latent[0, 0],
        ext,
        cotangent[0, 0],
        w_em,
        w_eg,
        w_e2,
        w_node,
        w_out,
        bias_edge.reshape(1, D),
        bias_node.reshape(1, D),
    )
    got = lax.ppermute(send, "core", [(0, 1), (1, 0)])
    own, *sends = core_sum(x, keep, got)
    came = [
        lax.ppermute(part, "x", [(i, (i + step + 1) % 4) for i in range(4)])
        for step, part in enumerate(sends)
    ]
    chunks = x_sum(own, *came)
    chunks = lax.all_to_all(chunks, ("y_lo", "z"), 0, 0, tiled=True)
    part = jnp.sum(chunks.astype(F32), axis=0).astype(BF)
    gathered = lax.all_gather(part, LON, axis=0, tiled=False)
    grads = last(gathered)

    from_south = shift(slots[64:82].astype(BF), LAT, -1, False).astype(F32)
    from_north = shift(slots[82:100].astype(BF), LAT, 1, False).astype(F32)
    to_west = slots[100:104].at[3].add(from_south[0]).at[0].add(from_north[0])
    to_east = slots[104:108].at[3].add(from_south[17]).at[0].add(from_north[17])
    from_east = shift(to_west.astype(BF), LON, -1, True).astype(F32)
    from_west = shift(to_east.astype(BF), LON, 1, True).astype(F32)
    owned = slots[:64].reshape(4, 16, D)
    owned = owned.at[3].add(from_south[1:17]).at[0].add(from_north[1:17])
    owned = owned.at[:, 15].add(from_east).at[:, 0].add(from_west)
    node_sum = owned.reshape(64, D).astype(BF)
    mesh_grad = mm_nt(node_sum, w_em).reshape(4, 16, D)
    return (grid_grad.reshape(1, 1, 256, D), mesh_grad) + tuple(grads)


def solution(mesh):
    fine = Mesh(mesh.devices.reshape(tuple(SIZES.values())), tuple(SIZES))
    in_specs = (
        P(LAT, LON, None, None),
        P(LAT, LON, None),
        P(LAT, LON, None, None),
        P(LAT, LON, None, None),
        P(LAT, LON),
    ) + (P(),) * 7
    out_specs = (P(LAT, LON, None, None), P(LAT, LON, None)) + (P(LAT, None),) * 5
    return jax.shard_map(
        on_device, mesh=fine, in_specs=in_specs, out_specs=out_specs, check_vma=False
    )
```

time: 1730 us -> 103 us (0.06)
  the two profiles are of different devices: /device:TPU:16 before, /device:TPU:1 now
where the time goes in v1:
time: 103 us; the launch traced here: 102 us
  starting transfers between devices  40.3 us (39%)
  local copies, waits for them, and re-layouts  18.3 us (18%)
  waiting for transfers between devices  18.1 us (18%)
  blocking collectives  11.4 us (11%)
  Pallas kernels  7.31 us (7%)
  other arithmetic  4 us (4%)
  between operations  1.58 us (2%)
    ppermute x8, starting transfers between devices, shift(): return lax.ppermute(value, axes, pairs)  18.2 us
    all_gather x1, blocking collectives, on_device(): gathered = lax.all_gather(part, LON, axis=0, tiled=False)  11.4 us
    ppermute x3, waiting for transfers between devices, on_device(): lax.ppermute(part, 'x', [(i, (i + step + 1) % 4) for i in range(4)])  10.5 us
    all_to_all x1, starting transfers between devices, on_device(): chunks = lax.all_to_all(chunks, ('y_lo', 'z'), 0, 0, tiled=True)  10.2 us
    unnamed x25, local copies, waits for them, and re-layouts  9.11 us
    ppermute x3, starting transfers between devices, on_device(): lax.ppermute(part, 'x', [(i, (i + step + 1) % 4) for i in range(4)])  7.64 us
    all_to_all x1, waiting for transfers between devices, on_device(): chunks = lax.all_to_all(chunks, ('y_lo', 'z'), 0, 0, tiled=True)  7.2 us
    pallas_call x1, Pallas kernels, main_call(): pl.pallas_call(main_kernel, out_shape=(shape((256, D), F32), shape((128,...  4.59 us
  transfers between devices with their start and end apart: 13, of which 4 were waited for; matrix products, arithmetic and copies ran while one was open for 14% of the time, Pallas kernels for 1%

profile of v1, /device:TPU:1, one launch (start us, length us, event | category | flops | bytes accessed | tf_op | source)
XLA Modules:
  0.0 101.9 jit_solution(10206420722765774518)
XLA Ops:
  0.7 0.9 fusion.8
  1.6 3.3 %collective-permute-start.1 = (bf16[4,512]{1,0:T(4,128)(2,1)S(1)}, bf16[4,512]{1,0:T(4,128)(2,1)S(1)}, u32[]{:S(2)}, u32[]{:S(2)}) collective-permute-start(bf16[4,512]{1,0:T(4,128)(2,1)S(1)} %bitcast.44), channel_id=1, source_target_pairs={{0,3},{1,0},{2,1},{3,2},{4,7},{5,4},{6,5},{7,6},{8,11},{9,8},{10,9... | collective-permute-start | bytes 12296 | tf_op jit(solution)/shard_map/ppermute | solution.py:283
  4.9 1.2 %collective-permute-start = (bf16[4,512]{1,0:T(4,128)(2,1)S(1)}, bf16[4,512]{1,0:T(4,128)(2,1)S(1)}, u32[]{:S(2)}, u32[]{:S(2)}) collective-permute-start(bf16[4,512]{1,0:T(4,128)(2,1)S(1)} %bitcast.45), channel_id=1, source_target_pairs={{0,1},{1,2},{2,3},{3,0},{4,5},{5,6},{6,7},{7,4},{8,9},{9,10},{10,1... | collective-permute-start | bytes 12296 | tf_op jit(solution)/shard_map/ppermute | solution.py:283
  7.3 3.1 %collective-permute-start.2 = (bf16[18,512]{1,0:T(8,128)(2,1)S(1)}, bf16[18,512]{1,0:T(8,128)(2,1)S(1)}, u32[]{:S(2)}, u32[]{:S(2)}) collective-permute-start(bf16[18,512]{1,0:T(8,128)(2,1)S(1)} %pad_maximum_fusion), channel_id=1, source_target_pairs={{0,4},{4,8},{8,12},{12,16},{16,20},{20,24},{24,28},{28,32},{32,36}... | collective-permute-start | bytes 55304 | tf_op jit(solution)/shard_map/ppermute | solution.py:283
  10.4 1.3 %collective-permute-start.3 = (bf16[18,512]{1,0:T(8,128)(2,1)S(1)}, bf16[18,512]{1,0:T(8,128)(2,1)S(1)}, u32[]{:S(2)}, u32[]{:S(2)}) collective-permute-start(bf16[18,512]{1,0:T(8,128)(2,1)S(1)} %pad_maximum_fusion.1), channel_id=1, source_target_pairs={{4,0},{8,4},{12,8},{16,12},{20,16},{24,20},{28,24},{32,28},{36,32}... | collective-permute-start | bytes 55304 | tf_op jit(solution)/shard_map/ppermute | solution.py:283
  13.1 1.0 copy.27
  14.1 1.1 %copy.28.w_out_ref = bf16[512,227]{1,0:T(8,128)(2,1)S(1)} copy(bf16[512,227]{0,1:T(8,128)(2,1)} %param.37) | data formatting | bytes 464896 | tf_op args[9]
  15.2 1.2 %concatenate.27.ext_ref = bf16[128,512]{1,0:T(8,128)(2,1)S(1)} concatenate(bf16[64,512]{1,0:T(8,128)(2,1)} %bitcast.43, bf16[18,512]{1,0:T(8,128)(2,1)S(1)} %collective-permute-done.2, bf16[18,512]{1,0:T(8,128)(2,1)S(1)} %collective-permute-done.3, bf16[4,512]{1,0:T(4,128)(2,1)S(1)} %collective-permute-done, bf16[4,512]{1,0:T(4,128)(2,1)S(1)} %collective-permute-done.1, ...), dimensions={0} | concatenate | bytes 262144 | tf_op jit(solution)/shard_map/concatenate | solution.py:306
  16.4 1.2 %copy-done.1 = bf16[1024,512]{1,0:T(8,128)(2,1)S(1)} copy-done((bf16[1024,512]{1,0:T(8,128)(2,1)S(1)}, bf16[1024,512]{1,0:T(8,128)(2,1)}, u32[]{:S(2)}) %copy-start.1) | copy-done | bytes 1048600
  17.6 1.0 %copy-done.6 = bf16[512,512]{1,0:T(8,128)(2,1)S(1)} copy-done((bf16[512,512]{1,0:T(8,128)(2,1)S(1)}, bf16[512,512]{1,0:T(8,128)(2,1)}, u32[]{:S(2)}) %copy-start.6) | copy-done | bytes 524312
  20.0 4.6 %decoder_grads.1 = (f32[256,512]{1,0:T(8,128)}, f32[128,512]{1,0:T(8,128)S(1)}, bf16[11,4,128,128]{3,2,1,0:T(8,128)(2,1)S(1)}, bf16[11,4,128,128]{3,2,1,0:T(8,128)(2,1)}) custom-call(s32[1]{0:T(128)} %bitcast.35.live_ref, s32[1]{0:T(128)} %bitcast.1.core_ref, s32[3,256]{1,0:T(4,128)S(1)} %bitcast.39, bf16[256,512]{1,0:T(8,128)(2,1)S(1)} %bitcast.38, ...), custom_call_target="tpu_custom_call" | custom-call | tf_op jit(solution)/shard_map/decoder_grads/pallas_call | solution.py:176
  25.3 4.3 %collective-permute-start.8 = (bf16[11,4,128,128]{3,2,1,0:T(8,128)(2,1)}, bf16[11,4,128,128]{3,2,1,0:T(8,128)(2,1)S(1)}, u32[]{:S(2)}, u32[]{:S(2)}) collective-permute-start(bf16[11,4,128,128]{3,2,1,0:T(8,128)(2,1)} %get-tuple-element.119), channel_id=1, source_target_pairs={{0,1},{1,0},{2,3},{3,2},{4,5},{5,4},{6,7},{7,6},{8,9},{9,8},{10,11... | collective-permute-start | bytes 4325384 | tf_op jit(solution)/shard_map/ppermute | solution.py:326
  29.6 1.0 convert.11
  31.2 1.3 %collective-permute-start.4 = (bf16[18,512]{1,0:T(8,128)(2,1)S(1)}, bf16[18,512]{1,0:T(8,128)(2,1)S(1)}, u32[]{:S(2)}, u32[]{:S(2)}) collective-permute-start(bf16[18,512]{1,0:T(8,128)(2,1)S(1)} %get-tuple-element.134), channel_id=1, source_target_pairs={{4,0},{8,4},{12,8},{16,12},{20,16},{24,20},{28,24},{32,28},{36,32}... | collective-permute-start | bytes 55304 | tf_op jit(solution)/shard_map/ppermute | solution.py:283
  33.3 0.9 slice.227
  34.2 4.6 %collective-permute-start.5 = (bf16[18,512]{1,0:T(8,128)(2,1)}, bf16[18,512]{1,0:T(8,128)(2,1)}, u32[]{:S(2)}, u32[]{:S(2)}) collective-permute-start(bf16[18,512]{1,0:T(8,128)(2,1)} %get-tuple-element.133), channel_id=1, source_target_pairs={{0,4},{4,8},{8,12},{12,16},{16,20},{20,24},{24,28},{28,32},{32,36}... | collective-permute-start | bytes 55304 | tf_op jit(solution)/shard_map/ppermute | solution.py:283
  39.7 1.3 %slice_add_fusion.5 = (f32[1,512]{1,0:T(1,128)}, f32[1,512]{1,0:T(1,128)}) fusion(f32[18,512]{1,0:T(8,128)S(1)} %convert_element_type.22, f32[128,512]{1,0:T(8,128)} %copy-done.2), kind=kLoop, calls=%fused_computation.18 | loop fusion | flops 1024 | bytes 12288 | tf_op jit(solution)/shard_map/add | solution.py:341
  43.8 1.2 %sum_over_core.1 = (f32[11,128,128]{2,1,0:T(8,128)S(1)}, bf16[11,128,128]{2,1,0:T(8,128)(2,1)}, bf16[11,128,128]{2,1,0:T(8,128)(2,1)}, bf16[11,128,128]{2,1,0:T(8,128)(2,1)}) custom-call(s32[1]{0:T(128)} %bitcast.17.x_ref, bf16[11,4,128,128]{3,2,1,0:T(8,128)(2,1)S(1)} %get-tuple-element.118.keep_ref, bf16[11,4,128,128]{3,2,1,0:T(8,128)(2,1)S(1)} %collective-permute-done.8.got_ref), custom_call_target="tpu_custom_call" | custom-call | tf_op jit(solution)/shard_map/sum_over_core/pallas_call | solution.py:212
  45.0 0.9 copy-done.3
  45.9 0.8 collective-permute-start.9
  46.7 6.8 %collective-permute-start.10 = (bf16[11,128,128]{2,1,0:T(8,128)(2,1)}, bf16[11,128,128]{2,1,0:T(8,128)(2,1)S(1)}, u32[]{:S(2)}, u32[]{:S(2)}) collective-permute-start(bf16[11,128,128]{2,1,0:T(8,128)(2,1)} %get-tuple-element.122), channel_id=1, source_target_pairs={{0,8},{4,12},{8,0},{12,4},{1,9},{5,13},{9,1},{13,5},{2,10},{6,14},... | collective-permute-start | bytes 1081352 | tf_op jit(solution)/shard_map/ppermute | solution.py:329
  53.6 1.2 %collective-permute-start.6 = (bf16[4,512]{1,0:T(4,128)(2,1)S(1)}, bf16[4,512]{1,0:T(4,128)(2,1)S(1)}, u32[]{:S(2)}, u32[]{:S(2)}) collective-permute-start(bf16[4,512]{1,0:T(4,128)(2,1)S(1)} %convert_element_type.24), channel_id=1, source_target_pairs={{0,3},{1,0},{2,1},{3,2},{4,7},{5,4},{6,5},{7,6},{8,11},{9,8},{10,9... | collective-permute-start | bytes 12296 | tf_op jit(solution)/shard_map/ppermute | solution.py:283
  54.8 0.9 scatter-add.26
  56.7 2.2 %collective-permute-start.7 = (bf16[4,512]{1,0:T(4,128)(2,1)S(1)}, bf16[4,512]{1,0:T(4,128)(2,1)S(1)}, u32[]{:S(2)}, u32[]{:S(2)}) collective-permute-start(bf16[4,512]{1,0:T(4,128)(2,1)S(1)} %convert_element_type.25), channel_id=1, source_target_pairs={{0,1},{1,2},{2,3},{3,0},{4,5},{5,6},{6,7},{7,4},{8,9},{9,10},{10,1... | collective-permute-start | bytes 12296 | tf_op jit(solution)/shard_map/ppermute | solution.py:283
  58.9 2.5 %collective-permute-done.9.a_ref = bf16[11,128,128]{2,1,0:T(8,128)(2,1)S(1)} collective-permute-done((bf16[11,128,128]{2,1,0:T(8,128)(2,1)}, bf16[11,128,128]{2,1,0:T(8,128)(2,1)S(1)}, u32[]{:S(2)}, u32[]{:S(2)}) %collective-permute-start.9) | collective-permute-done | bytes 360480 | tf_op jit(solution)/shard_map/ppermute | solution.py:329
  61.4 8.0 %collective-permute-done.10.b_ref = bf16[11,128,128]{2,1,0:T(8,128)(2,1)S(1)} collective-permute-done((bf16[11,128,128]{2,1,0:T(8,128)(2,1)}, bf16[11,128,128]{2,1,0:T(8,128)(2,1)S(1)}, u32[]{:S(2)}, u32[]{:S(2)}) %collective-permute-start.10) | collective-permute-done | bytes 360480 | tf_op jit(solution)/shard_map/ppermute | solution.py:329
  69.4 1.1 %copy-done.4 = f32[11,128,128]{2,1,0:T(8,128)S(1)} copy-done((f32[11,128,128]{2,1,0:T(8,128)S(1)}, f32[11,128,128]{2,1,0:T(8,128)}, u32[]{:S(2)}) %copy-start.4) | copy-done | bytes 720920
  70.5 0.9 sum_over_x.1
  71.4 10.2 %all-to-all-start = ((bf16[16,88,128]{2,1,0:T(8,128)(2,1)}), bf16[16,88,128]{2,1,0:T(8,128)(2,1)S(1)}, u32[]{:S(2)}, u32[]{:S(2)}) async-start(bf16[16,88,128]{2,1,0:T(8,128)(2,1)} %sum_over_x.1), calls=%async_computation | async-start | bytes 720896 | tf_op jit(solution)/shard_map/all_to_all | solution.py:333
  81.7 0.9 fusion
  82.7 7.2 %all-to-all-done = bf16[16,88,128]{2,1,0:T(8,128)(2,1)S(1)} async-done(((bf16[16,88,128]{2,1,0:T(8,128)(2,1)}), bf16[16,88,128]{2,1,0:T(8,128)(2,1)S(1)}, u32[]{:S(2)}, u32[]{:S(2)}) %all-to-all-start) | async-done | bytes 360480 | tf_op jit(solution)/shard_map/all_to_all | solution.py:333
  89.9 11.4 %all-gather = bf16[352,128]{1,0:T(8,128)(2,1)S(1)} all-gather(bf16[88,128]{1,0:T(8,128)(2,1)S(1)} %reduce_sum.12), channel_id=2, replica_groups=mesh['y_lo'=2,'z'=8,'x'=4,'y_hi'=2,'core'=2] {'y_hi','core'}, dimensions={0}, use_global_device_ids=true | all-gather | bytes 112640 | tf_op jit(solution)/shard_map/all_gather | solution.py:335
  (58 shorter events, 10.9 us)
Async XLA Ops:
  0.6 15.7 %copy-start = (bf16[512,512]{1,0:T(8,128)(2,1)S(1)}, bf16[512,512]{1,0:T(8,128)(2,1)}, u32[]{:S(2)}) copy-start(bf16[512,512]{1,0:T(8,128)(2,1)} %w_em_ref.1) | copy-start | bytes 1572868
  0.6 15.7 %copy-start.5 = (bf16[512,512]{1,0:T(8,128)(2,1)S(1)}, bf16[512,512]{1,0:T(8,128)(2,1)}, u32[]{:S(2)}) copy-start(bf16[512,512]{1,0:T(8,128)(2,1)} %w_eg_ref.1) | copy-start | bytes 1572868
  0.7 15.7 %copy-start.7 = (bf16[1,1,256,512]{3,2,1,0:T(8,128)(2,1)S(1)}, bf16[1,1,256,512]{3,2,1,0:T(8,128)(2,1)}, u32[]{:S(2)}) copy-start(bf16[1,1,256,512]{3,2,1,0:T(8,128)(2,1)} %param.28) | copy-start | bytes 786436
  1.6 5.7 %collective-permute-start.1 = (bf16[4,512]{1,0:T(4,128)(2,1)S(1)}, bf16[4,512]{1,0:T(4,128)(2,1)S(1)}, u32[]{:S(2)}, u32[]{:S(2)}) collective-permute-start(bf16[4,512]{1,0:T(4,128)(2,1)S(1)} %bitcast.44), channel_id=1, source_target_pairs={{0,3},{1,0},{2,1},{3,2},{4,7},{5,4},{6,5},{7,6},{8,11},{9,8},{10,9... | collective-permute-start | bytes 12296 | tf_op jit(solution)/shard_map/ppermute | solution.py:283
  4.9 2.4 %collective-permute-start = (bf16[4,512]{1,0:T(4,128)(2,1)S(1)}, bf16[4,512]{1,0:T(4,128)(2,1)S(1)}, u32[]{:S(2)}, u32[]{:S(2)}) collective-permute-start(bf16[4,512]{1,0:T(4,128)(2,1)S(1)} %bitcast.45), channel_id=1, source_target_pairs={{0,1},{1,2},{2,3},{3,0},{4,5},{5,6},{6,7},{7,4},{8,9},{9,10},{10,1... | collective-permute-start | bytes 12296 | tf_op jit(solution)/shard_map/ppermute | solution.py:283
  7.3 7.9 %collective-permute-start.2 = (bf16[18,512]{1,0:T(8,128)(2,1)S(1)}, bf16[18,512]{1,0:T(8,128)(2,1)S(1)}, u32[]{:S(2)}, u32[]{:S(2)}) collective-permute-start(bf16[18,512]{1,0:T(8,128)(2,1)S(1)} %pad_maximum_fusion), channel_id=1, source_target_pairs={{0,4},{4,8},{8,12},{12,16},{16,20},{20,24},{24,28},{28,32},{32,36}... | collective-permute-start | bytes 55304 | tf_op jit(solution)/shard_map/ppermute | solution.py:283
  10.4 4.7 %collective-permute-start.3 = (bf16[18,512]{1,0:T(8,128)(2,1)S(1)}, bf16[18,512]{1,0:T(8,128)(2,1)S(1)}, u32[]{:S(2)}, u32[]{:S(2)}) collective-permute-start(bf16[18,512]{1,0:T(8,128)(2,1)S(1)} %pad_maximum_fusion.1), channel_id=1, source_target_pairs={{4,0},{8,4},{12,8},{16,12},{20,16},{24,20},{28,24},{32,28},{36,32}... | collective-permute-start | bytes 55304 | tf_op jit(solution)/shard_map/ppermute | solution.py:283
  16.4 1.2 %copy-start.1 = (bf16[1024,512]{1,0:T(8,128)(2,1)S(1)}, bf16[1024,512]{1,0:T(8,128)(2,1)}, u32[]{:S(2)}) copy-start(bf16[1024,512]{1,0:T(8,128)(2,1)} %w_node_ref.1) | copy-start | bytes 3145732
  17.6 1.0 %copy-start.6 = (bf16[512,512]{1,0:T(8,128)(2,1)S(1)}, bf16[512,512]{1,0:T(8,128)(2,1)}, u32[]{:S(2)}) copy-start(bf16[512,512]{1,0:T(8,128)(2,1)} %w_e2_ref.1) | copy-start | bytes 1572868
  18.7 0.7 copy-start.8
  19.4 0.7 copy-start.9
  24.6 0.7 copy-start.2
  25.3 18.5 %collective-permute-start.8 = (bf16[11,4,128,128]{3,2,1,0:T(8,128)(2,1)}, bf16[11,4,128,128]{3,2,1,0:T(8,128)(2,1)S(1)}, u32[]{:S(2)}, u32[]{:S(2)}) collective-permute-start(bf16[11,4,128,128]{3,2,1,0:T(8,128)(2,1)} %get-tuple-element.119), channel_id=1, source_target_pairs={{0,1},{1,0},{2,3},{3,2},{4,5},{5,4},{6,7},{7,6},{8,9},{9,8},{10,11... | collective-permute-start | bytes 4325384 | tf_op jit(solution)/shard_map/ppermute | solution.py:326
  31.2 7.6 %collective-permute-start.4 = (bf16[18,512]{1,0:T(8,128)(2,1)S(1)}, bf16[18,512]{1,0:T(8,128)(2,1)S(1)}, u32[]{:S(2)}, u32[]{:S(2)}) collective-permute-start(bf16[18,512]{1,0:T(8,128)(2,1)S(1)} %get-tuple-element.134), channel_id=1, source_target_pairs={{4,0},{8,4},{12,8},{16,12},{20,16},{24,20},{28,24},{32,28},{36,32}... | collective-permute-start | bytes 55304 | tf_op jit(solution)/shard_map/ppermute | solution.py:283
  34.2 8.9 %collective-permute-start.5 = (bf16[18,512]{1,0:T(8,128)(2,1)}, bf16[18,512]{1,0:T(8,128)(2,1)}, u32[]{:S(2)}, u32[]{:S(2)}) collective-permute-start(bf16[18,512]{1,0:T(8,128)(2,1)} %get-tuple-element.133), channel_id=1, source_target_pairs={{0,4},{4,8},{8,12},{12,16},{16,20},{20,24},{24,28},{28,32},{32,36}... | collective-permute-start | bytes 55304 | tf_op jit(solution)/shard_map/ppermute | solution.py:283
  45.0 0.9 copy-start.3
  45.9 15.6 %collective-permute-start.9 = (bf16[11,128,128]{2,1,0:T(8,128)(2,1)}, bf16[11,128,128]{2,1,0:T(8,128)(2,1)S(1)}, u32[]{:S(2)}, u32[]{:S(2)}) collective-permute-start(bf16[11,128,128]{2,1,0:T(8,128)(2,1)} %get-tuple-element.121), channel_id=1, source_target_pairs={{0,4},{4,8},{8,12},{12,0},{1,5},{5,9},{9,13},{13,1},{2,6},{6,10},{... | collective-permute-start | bytes 1081352 | tf_op jit(solution)/shard_map/ppermute | solution.py:329
  46.7 22.7 %collective-permute-start.10 = (bf16[11,128,128]{2,1,0:T(8,128)(2,1)}, bf16[11,128,128]{2,1,0:T(8,128)(2,1)S(1)}, u32[]{:S(2)}, u32[]{:S(2)}) collective-permute-start(bf16[11,128,128]{2,1,0:T(8,128)(2,1)} %get-tuple-element.122), channel_id=1, source_target_pairs={{0,8},{4,12},{8,0},{12,4},{1,9},{5,13},{9,1},{13,5},{2,10},{6,14},... | collective-permute-start | bytes 1081352 | tf_op jit(solution)/shard_map/ppermute | solution.py:329
  53.5 15.9 %collective-permute-start.11 = (bf16[11,128,128]{2,1,0:T(8,128)(2,1)}, bf16[11,128,128]{2,1,0:T(8,128)(2,1)S(1)}, u32[]{:S(2)}, u32[]{:S(2)}) collective-permute-start(bf16[11,128,128]{2,1,0:T(8,128)(2,1)} %get-tuple-element.123), channel_id=1, source_target_pairs={{0,12},{4,0},{8,4},{12,8},{1,13},{5,1},{9,5},{13,9},{2,14},{6,2},{... | collective-permute-start | bytes 1081352 | tf_op jit(solution)/shard_map/ppermute | solution.py:329
  53.6 28.0 %collective-permute-start.6 = (bf16[4,512]{1,0:T(4,128)(2,1)S(1)}, bf16[4,512]{1,0:T(4,128)(2,1)S(1)}, u32[]{:S(2)}, u32[]{:S(2)}) collective-permute-start(bf16[4,512]{1,0:T(4,128)(2,1)S(1)} %convert_element_type.24), channel_id=1, source_target_pairs={{0,3},{1,0},{2,1},{3,2},{4,7},{5,4},{6,5},{7,6},{8,11},{9,8},{10,9... | collective-permute-start | bytes 12296 | tf_op jit(solution)/shard_map/ppermute | solution.py:283
  56.7 24.9 %collective-permute-start.7 = (bf16[4,512]{1,0:T(4,128)(2,1)S(1)}, bf16[4,512]{1,0:T(4,128)(2,1)S(1)}, u32[]{:S(2)}, u32[]{:S(2)}) collective-permute-start(bf16[4,512]{1,0:T(4,128)(2,1)S(1)} %convert_element_type.25), channel_id=1, source_target_pairs={{0,1},{1,2},{2,3},{3,0},{4,5},{5,6},{6,7},{7,4},{8,9},{9,10},{10,1... | collective-permute-start | bytes 12296 | tf_op jit(solution)/shard_map/ppermute | solution.py:283
  69.4 1.1 %copy-start.4 = (f32[11,128,128]{2,1,0:T(8,128)S(1)}, f32[11,128,128]{2,1,0:T(8,128)}, u32[]{:S(2)}) copy-start(f32[11,128,128]{2,1,0:T(8,128)} %copy-done.3) | copy-start | bytes 2162692
  71.4 18.4 %all-to-all-start = ((bf16[16,88,128]{2,1,0:T(8,128)(2,1)}), bf16[16,88,128]{2,1,0:T(8,128)(2,1)S(1)}, u32[]{:S(2)}, u32[]{:S(2)}) async-start(bf16[16,88,128]{2,1,0:T(8,128)(2,1)} %sum_over_x.1), calls=%async_computation | async-start | bytes 720896 | tf_op jit(solution)/shard_map/all_to_all | solution.py:333

commit v2 on v1

--- a/solution.py
+++ b/solution.py
@@ -1,5 +1,3 @@
-import functools
-
 import jax
 import jax.numpy as jnp
 from jax import lax
@@ -41,77 +39,74 @@
     ref[1] = value[:, width:].astype(ref.dtype)
 
 
+W_EM, W_EG, W_E2, W_NODE, GRID, MESH, W_OUT = (0, 512, 1024, 1536, 2560, 2816, 2880)
+
+
 def main_kernel(
-    live_ref,
+    place_ref,
+    north_ref,
+    south_ref,
+    mate_ref,
+    opposite_ref,
+    pack_ref,
+    bias_ref,
+    cot_ref,
     core_ref,
-    nbr_ref,
-    g_ref,
-    ext_ref,
-    cot_ref,
-    w_em_ref,
-    w_eg_ref,
-    w_e2_ref,
-    w_node_ref,
-    w_out_ref,
-    b_edge_ref,
-    b_node_ref,
     grid_ref,
     slot_ref,
     keep_ref,
     send_ref,
-    og_ref,
-    wo_ref,
+    ext_ref,
     ng_half,
     og_half,
     ag_half,
     es_half,
     sl_half,
     slope_ref,
+    og_ref,
 ):
+    w_em_ref = pack_ref.at[W_EM:W_EG]
+    w_eg_ref = pack_ref.at[W_EG:W_E2]
+    w_e2_ref = pack_ref.at[W_E2:W_NODE]
+    w_node_ref = pack_ref.at[W_NODE:GRID]
+    g_ref = pack_ref.at[GRID:MESH]
+    mesh_ref = pack_ref.at[MESH:W_OUT]
+    wo_ref = pack_ref.at[W_OUT : W_OUT + 256]
     core = core_ref[0]
+    points = 256
+    ext_ref[:64, :] = mesh_ref[...].astype(F32)
+    ext_ref[64:, :] = jnp.zeros((64, D), F32)
+    ext_ref[64:82, :] = north_ref[...].astype(F32)
+    ext_ref[88:106, :] = south_ref[...].astype(F32)
+    ext_ref[112:116, :] = mate_ref[...].astype(F32)
+    ext_ref[120:124, :] = opposite_ref[...].astype(F32)
+    ext = ext_ref[...].astype(BF)
+    row = lax.broadcasted_iota(jnp.int32, (128, points), 0)
+    hots = [jnp.where(row == place_ref[k : k + 1, :], 1.0, 0.0).astype(BF) for k in range(3)]
     g = g_ref[...]
-    ext = ext_ref[...]
-    points = g.shape[0]
-    og_ref[...] = jnp.zeros_like(og_ref)
-    wo_ref[...] = jnp.zeros_like(wo_ref)
-    row = lax.broadcasted_iota(jnp.int32, (points, CH), 0)
-    cot = cot_ref[...]
-    og_ref[:, :CH] = jnp.where(row < live_ref[0], cot, jnp.zeros_like(cot))
-    wo_ref[:, :CH] = w_out_ref[...]
-    out_grad = og_ref[...]
-    halves(og_half, out_grad)
-
     projected = mm(ext, w_em_ref[...])
     high, low = split(projected)
     both = jnp.concatenate([high, low], axis=0)
-    grid_proj = mm(g, w_eg_ref[...]) + b_edge_ref[...]
-    place = lax.broadcasted_iota(jnp.int32, (128, points), 0)
+    grid_proj = mm(g, w_eg_ref[...]) + bias_ref[0:1, :]
     hidden_sum = None
-    hots = []
     for k in range(3):
-        slot = nbr_ref[k : k + 1, :]
-        r = (slot * 3641) >> 16
-        c = slot - r * 18
-        inner = jnp.where(
-            c == 0, 99 + r, jnp.where(c == 17, 103 + r, (r - 1) * 16 + c - 1)
-        )
-        where = jnp.where(r == 0, 64 + c, jnp.where(r == 5, 82 + c, inner))
-        hot = jnp.where(place == where, 1.0, 0.0).astype(BF)
-        hots.append(hot)
-        pre = mm_tn(jnp.concatenate([hot, hot], axis=0), both) + grid_proj
+        pre = mm_tn(jnp.concatenate([hots[k], hots[k]], axis=0), both) + grid_proj
         sigma = jax.nn.sigmoid(pre)
         hidden = (pre * sigma).astype(BF)
         slope_ref[k] = sigma * (1.0 + pre * (1.0 - sigma))
         hidden = hidden.astype(F32)
         hidden_sum = hidden if hidden_sum is None else hidden_sum + hidden
     hs_high, hs_low = split(hidden_sum)
+    og_ref[...] = jnp.zeros_like(og_ref)
+    og_ref[:CH, :] = cot_ref[...]
+    out_grad = og_ref[...].T
+    halves(og_half, out_grad)
+
     aggregate = (mm(hs_high, w_e2_ref[...]) + mm(hs_low, w_e2_ref[...])).astype(BF)
-    node_pre = mm(g, w_node_ref[:D, :]) + mm(aggregate, w_node_ref[D:, :]) + b_node_ref[...]
+    node_pre = mm(g, w_node_ref[:D, :]) + mm(aggregate, w_node_ref[D:, :]) + bias_ref[1:2, :]
     sigma = jax.nn.sigmoid(node_pre)
     node_hidden = (node_pre * sigma).astype(BF)
-    node_grad = (mm_nt(out_grad, wo_ref[...]) * (sigma * (1.0 + node_pre * (1.0 - sigma)))).astype(
-        BF
-    )
+    node_grad = (mm(out_grad, wo_ref[...]) * (sigma * (1.0 + node_pre * (1.0 - sigma)))).astype(BF)
     halves(ng_half, node_grad)
     agg_grad = mm_nt(node_grad, w_node_ref[D:, :]).astype(BF)
     halves(ag_half, agg_grad)
@@ -168,10 +163,11 @@
     return [pl.BlockSpec(memory_space=pltpu.SMEM)] * n
 
 
-PARAMS = pltpu.CompilerParams(vmem_limit_bytes=48 * 1024 * 1024)
-
-
-def main_call(live, core, nbr, g, ext, cot, *weights):
+def params(mebibytes):
+    return pltpu.CompilerParams(vmem_limit_bytes=mebibytes * 1024 * 1024)
+
+
+def main_call(*args):
     shape = jax.ShapeDtypeStruct
     return pl.pallas_call(
         main_kernel,
@@ -181,21 +177,21 @@
             shape((PANELS, 4, 128, 128), BF),
             shape((PANELS, 4, 128, 128), BF),
         ),
-        in_specs=smem(2) + vmem(11),
+        in_specs=vmem(8) + smem(1),
         out_specs=tuple(vmem(4)),
         scratch_shapes=[
-            pltpu.VMEM((256, 256), BF),
-            pltpu.VMEM((D, 256), BF),
+            pltpu.VMEM((128, D), F32),
             pltpu.VMEM((2, 256, 256), BF),
             pltpu.VMEM((2, 256, 128), BF),
             pltpu.VMEM((2, 256, 256), BF),
             pltpu.VMEM((2, 256, 256), BF),
             pltpu.VMEM((2, 256, 256), BF),
             pltpu.VMEM((3, 256, D), F32),
+            pltpu.VMEM((256, 256), BF),
         ],
-        compiler_params=PARAMS,
+        compiler_params=params(28),
         name="decoder_grads",
-    )(live, core, nbr, g, ext, cot, *weights)
+    )(*args)
 
 
 def core_sum_kernel(x_ref, keep_ref, got_ref, own_ref, *sends):
@@ -214,7 +210,7 @@
         out_shape=(shape(part, F32),) + (shape(part, BF),) * 3,
         in_specs=smem(1) + vmem(2),
         out_specs=tuple(vmem(4)),
-        compiler_params=PARAMS,
+        compiler_params=params(12),
         name="sum_over_core",
     )(x, keep, got)
 
@@ -232,7 +228,7 @@
         out_shape=jax.ShapeDtypeStruct((16, PANELS * 8, 128), BF),
         in_specs=vmem(4),
         out_specs=vmem(1)[0],
-        compiler_params=PARAMS,
+        compiler_params=params(8),
         name="sum_over_x",
     )(own, a, b, c)
 
@@ -270,17 +266,25 @@
         ),
         in_specs=vmem(1),
         out_specs=tuple(vmem(5)),
-        compiler_params=PARAMS,
+        compiler_params=params(4),
         name="sum_over_lon",
     )(gathered)
 
 
-def shift(value, axes, steps, wrap):
+def shift(value, axes, steps):
     size = 1
     for a in axes:
         size *= SIZES[a]
-    pairs = [(i, (i + steps) % size) for i in range(size) if wrap or 0 <= i + steps < size]
+    pairs = [(i, i + steps) for i in range(size) if 0 <= i + steps < size]
     return lax.ppermute(value, axes, pairs)
+
+
+def to_mate(value):
+    return lax.ppermute(value, "core", [(0, 1), (1, 0)])
+
+
+def to_opposite(value):
+    return lax.ppermute(value, LON, [(i, 3 - i) for i in range(4)])
 
 
 def on_device(
@@ -297,34 +301,41 @@
     bias_edge,
     bias_node,
 ):
-    west = shift(mesh_latent[:, 15], LON, 1, True)
-    east = shift(mesh_latent[:, 0], LON, -1, True)
+    core = lax.axis_index("core").astype(jnp.int32)
+    x = lax.axis_index("x").astype(jnp.int32).reshape(1)
+    first, final = mesh_latent[:, 0], mesh_latent[:, 15]
+    mate = to_mate(jnp.where(core == 0, final, first))
+    opposite = to_opposite(jnp.where(core == 0, first, final))
+    west = jnp.where(core == 0, opposite, mate)
+    east = jnp.where(core == 0, mate, opposite)
     top = jnp.concatenate([west[:1], mesh_latent[0], east[:1]], axis=0)
     bottom = jnp.concatenate([west[3:], mesh_latent[3], east[3:]], axis=0)
-    north = shift(bottom, LAT, 1, False)
-    south = shift(top, LAT, -1, False)
-    ext = jnp.concatenate(
-        [mesh_latent.reshape(64, D), north, south, west, east, jnp.zeros((20, D), BF)], axis=0
+    north = shift(bottom, LAT, 1)
+    south = shift(top, LAT, -1)
+    pack = jnp.concatenate(
+        [w_em, w_eg, w_e2, w_node, grid_latent[0, 0], mesh_latent.reshape(64, D), w_out.T, jnp.zeros((29, D), BF)]
     )
-    core = lax.axis_index("core").astype(jnp.int32).reshape(1)
-    x = lax.axis_index("x").astype(jnp.int32).reshape(1)
+    live_point = lax.broadcasted_iota(jnp.int32, (CH, 256), 1) < live[0, 0]
+    out_grad = jnp.where(live_point, cotangent[0, 0].T, jnp.zeros((), BF))
+    slot = neighbours[0, 0]
+    r, c = slot // 18, slot % 18
+    side = jnp.where(c == 0, 120 - 8 * core, 112 + 8 * core) + r - 1
+    inner = jnp.where((c == 0) | (c == 17), side, (r - 1) * 16 + c - 1)
+    place = jnp.where(r == 0, 64 + c, jnp.where(r == 5, 88 + c, inner))
     grid_grad, slots, keep, send = main_call(
-        live.reshape(1),
-        core,
-        neighbours[0, 0],
-        grid_latent[0, 0],
-        ext,
-        cotangent[0, 0],
-        w_em,
-        w_eg,
-        w_e2,
-        w_node,
-        w_out,
-        bias_edge.reshape(1, D),
-        bias_node.reshape(1, D),
+        place,
+        north,
+        south,
+        mate,
+        opposite,
+        pack,
+        jnp.stack([bias_edge, bias_node]),
+        out_grad,
+        core.reshape(1),
     )
     got = lax.ppermute(send, "core", [(0, 1), (1, 0)])
     own, *sends = core_sum(x, keep, got)
+    slots, sends = lax.optimization_barrier((slots, sends))
     came = [
         lax.ppermute(part, "x", [(i, (i + step + 1) % 4) for i in range(4)])
         for step, part in enumerate(sends)
@@ -335,15 +346,17 @@
     gathered = lax.all_gather(part, LON, axis=0, tiled=False)
     grads = last(gathered)
 
-    from_south = shift(slots[64:82].astype(BF), LAT, -1, False).astype(F32)
-    from_north = shift(slots[82:100].astype(BF), LAT, 1, False).astype(F32)
-    to_west = slots[100:104].at[3].add(from_south[0]).at[0].add(from_north[0])
-    to_east = slots[104:108].at[3].add(from_south[17]).at[0].add(from_north[17])
-    from_east = shift(to_west.astype(BF), LON, -1, True).astype(F32)
-    from_west = shift(to_east.astype(BF), LON, 1, True).astype(F32)
-    owned = slots[:64].reshape(4, 16, D)
-    owned = owned.at[3].add(from_south[1:17]).at[0].add(from_north[1:17])
-    owned = owned.at[:, 15].add(from_east).at[:, 0].add(from_west)
+    from_south = shift(slots[64:82].astype(BF), LAT, -1).astype(F32)
+    from_north = shift(slots[88:106].astype(BF), LAT, 1).astype(F32)
+    ends = jnp.stack([from_north, jnp.zeros_like(from_north), jnp.zeros_like(from_north), from_south])
+    mate = slots[112:116] + jnp.where(core == 0, ends[:, 17], ends[:, 0])
+    opposite = slots[120:124] + jnp.where(core == 0, ends[:, 0], ends[:, 17])
+    mate = to_mate(mate.astype(BF)).astype(F32)
+    opposite = to_opposite(opposite.astype(BF)).astype(F32)
+    west = jnp.where(core == 0, opposite, mate)
+    east = jnp.where(core == 0, mate, opposite)
+    sides = jnp.concatenate([west[:, None], jnp.zeros((4, 14, D), F32), east[:, None]], axis=1)
+    owned = slots[:64].reshape(4, 16, D) + ends[:, 1:17] + sides
     node_sum = owned.reshape(64, D).astype(BF)
     mesh_grad = mm_nt(node_sum, w_em).reshape(4, 16, D)
     return (grid_grad.reshape(1, 1, 256, D), mesh_grad) + tuple(grads)

time: 103 us -> 97.5 us (0.947)
  starting transfers between devices: 40.3 us -> 31.9 us
  waiting for transfers between devices: 18.1 us -> 25.7 us
  blocking collectives: 11.4 us -> 8.88 us
    ppermute x8 -> x4, waiting for transfers between devices: 0.47 us -> 13 us  [shift(): return lax.ppermute(value, axes, pairs)]
    concatenate x1 -> x2, local copies, waits for them, and re-layouts: 1.17 us -> 12.6 us  [the longest x1 12.6 us: on_device(): jnp.concatenate([w_em, w_eg, w_e2, w_node, grid_latent[0, 0], mesh_latent...]
    ppermute x3, waiting for transfers between devices: 10.5 us -> 0.01 us  [on_device(): lax.ppermute(part, 'x', [(i, (i + step + 1) % 4) for i in range(4)])]
    ppermute x8 -> x4, starting transfers between devices: 18.2 us -> 9.68 us  [shift(): return lax.ppermute(value, axes, pairs)]
    ppermute x0 -> x4, starting transfers between devices: none -> 6.04 us  [the longest x2 6.04 us: to_opposite(): return lax.ppermute(value, LON, [(i, 3 - i) for i in range(4)])]
    unnamed x25 -> x8, local copies, waits for them, and re-layouts: 9.11 us -> 3.38 us
    ppermute x1, starting transfers between devices: 4.29 us -> 1.07 us  [on_device(): got = lax.ppermute(send, 'core', [(0, 1), (1, 0)])]
    slice x5 -> x3, local copies, waits for them, and re-layouts: 3.91 us -> 0.81 us  [the longest x1 0.79 us: on_device(): first, final = (mesh_latent[:, 0], mesh_latent[:, 15])]
  transfers between devices with their start and end apart: 13 -> 13, of which waited for: 4 -> 3; matrix products, arithmetic and copies ran while one was open for 14% -> 18% of each run, Pallas kernels for 1% -> 1%
where the time goes in v2:
time: 97.5 us; the launch traced here: 96.6 us
  starting transfers between devices  31.9 us (33%)
  waiting for transfers between devices  25.7 us (26%)
  local copies, waits for them, and re-layouts  17.7 us (18%)
  blocking collectives  8.88 us (9%)
  Pallas kernels  6.53 us (7%)
  other arithmetic  3.35 us (3%)
  between operations  1.58 us (2%)
    ppermute x4, waiting for transfers between devices, shift(): return lax.ppermute(value, axes, pairs)  13 us
    concatenate x1, local copies, waits for them, and re-layouts, on_device(): jnp.concatenate([w_em, w_eg, w_e2, w_node, grid_latent[0, 0], mesh_latent...  12.6 us
    ppermute x4, starting transfers between devices, shift(): return lax.ppermute(value, axes, pairs)  9.68 us
    all_to_all x1, waiting for transfers between devices, on_device(): chunks = lax.all_to_all(chunks, ('y_lo', 'z'), 0, 0, tiled=True)  9.59 us
    all_to_all x1, starting transfers between devices, on_device(): chunks = lax.all_to_all(chunks, ('y_lo', 'z'), 0, 0, tiled=True)  9.06 us
    all_gather x1, blocking collectives, on_device(): gathered = lax.all_gather(part, LON, axis=0, tiled=False)  8.88 us
    ppermute x3, starting transfers between devices, on_device(): lax.ppermute(part, 'x', [(i, (i + step + 1) % 4) for i in range(4)])  6.06 us
    ppermute x2, starting transfers between devices, to_opposite(): return lax.ppermute(value, LON, [(i, 3 - i) for i in range(4)])  6.04 us
  transfers between devices with their start and end apart: 13, of which 3 were waited for; matrix products, arithmetic and copies ran while one was open for 18% of the time, Pallas kernels for 1%

profile of v2, /device:TPU:1, one launch (start us, length us, event | category | flops | bytes accessed | tf_op | source)
XLA Modules:
  0.0 96.6 jit_solution(7801210209286921572)
XLA Ops:
  0.6 0.8 fusion.14
  1.5 4.4 %collective-permute-start = (bf16[4,512]{1,0:T(4,128)(2,1)S(1)}, bf16[4,512]{1,0:T(4,128)(2,1)S(1)}, u32[]{:S(2)}, u32[]{:S(2)}) collective-permute-start(bf16[4,512]{1,0:T(4,128)(2,1)S(1)} %get-tuple-element.49), channel_id=1, source_target_pairs={{0,3},{1,2},{2,1},{3,0},{4,7},{5,6},{6,5},{7,4},{8,11},{9,10},{10,... | collective-permute-start | bytes 12296 | tf_op jit(solution)/shard_map/ppermute | solution.py:287
  5.9 0.7 slice_bitcast_fusion
  7.3 1.6 %fusion.4.cot_ref = bf16[227,256]{1,0:T(8,128)(2,1)} fusion(bf16[1,1,256,227]{2,3,1,0:T(8,128)(2,1)} %param.14, pred[256]{0:T(512)(128)(4,1)S(1)} %iota_compare_fusion), kind=kLoop, calls=%fused_computation.7 | loop fusion | flops 58112 | bytes 232704 | tf_op jit(solution)/shard_map/jit(_where)/select_n | solution.py:319
  8.8 0.7 select_select_fusion.place_ref
  9.6 1.3 %collective-permute-start.3 = (bf16[18,512]{1,0:T(8,128)(2,1)S(1)}, bf16[18,512]{1,0:T(8,128)(2,1)S(1)}, u32[]{:S(2)}, u32[]{:S(2)}) collective-permute-start(bf16[18,512]{1,0:T(8,128)(2,1)S(1)} %pad_maximum_fusion.2), channel_id=1, source_target_pairs={{4,0},{8,4},{12,8},{16,12},{20,16},{24,20},{28,24},{32,28},{36,32}... | collective-permute-start | bytes 55304 | tf_op jit(solution)/shard_map/ppermute | solution.py:279
  10.9 4.0 %collective-permute-start.2 = (bf16[18,512]{1,0:T(8,128)(2,1)S(1)}, bf16[18,512]{1,0:T(8,128)(2,1)S(1)}, u32[]{:S(2)}, u32[]{:S(2)}) collective-permute-start(bf16[18,512]{1,0:T(8,128)(2,1)S(1)} %pad_maximum_fusion.1), channel_id=1, source_target_pairs={{0,4},{4,8},{8,12},{12,16},{16,20},{20,24},{24,28},{28,32},{32,36}... | collective-permute-start | bytes 55304 | tf_op jit(solution)/shard_map/ppermute | solution.py:279
  14.9 0.7 pad_maximum_fusion.3.bias_ref
  15.6 12.6 %concatenate.14.pack_ref = bf16[3136,512]{1,0:T(8,128)(2,1)S(1)} concatenate(bf16[512,512]{1,0:T(8,128)(2,1)} %param.17, bf16[512,512]{1,0:T(8,128)(2,1)} %param.18, bf16[512,512]{1,0:T(8,128)(2,1)} %param.19, bf16[1024,512]{1,0:T(8,128)(2,1)} %param.20, bf16[256,512]{1,0:T(8,128)(2,1)} %bitcast.62, bf16[64,512]{1,0:T(8,128)(2,1)} %bitcast.64, bf16[227,512]{1,0:T(8,128)(2,1)} %bitcast.63, ...), dimensions={0} | concatenate | bytes 6422528 | tf_op jit(solution)/shard_map/concatenate | solution.py:315
  28.2 0.9 copy-done.2
  29.1 4.6 %decoder_grads.1 = (f32[256,512]{1,0:T(8,128)}, f32[128,512]{1,0:T(8,128)S(1)}, bf16[11,4,128,128]{3,2,1,0:T(8,128)(2,1)S(1)}, bf16[11,4,128,128]{3,2,1,0:T(8,128)(2,1)}) custom-call(s32[3,256]{1,0:T(4,128)S(1)} %select_select_fusion.place_ref, bf16[18,512]{1,0:T(8,128)(2,1)S(1)} %collective-permute-done.2.north_ref, ...), custom_call_target="tpu_custom_call" | custom-call | tf_op jit(solution)/shard_map/decoder_grads/pallas_call | solution.py:172
  33.7 1.1 %copy-done = bf16[11,4,128,128]{3,2,1,0:T(8,128)(2,1)} copy-done((bf16[11,4,128,128]{3,2,1,0:T(8,128)(2,1)}, bf16[11,4,128,128]{3,2,1,0:T(8,128)(2,1)S(1)}, u32[]{:S(2)}) %copy-start) | copy-done | bytes 1441816
  34.9 1.1 %collective-permute-start.4 = (bf16[11,4,128,128]{3,2,1,0:T(8,128)(2,1)}, bf16[11,4,128,128]{3,2,1,0:T(8,128)(2,1)S(1)}, u32[]{:S(2)}, u32[]{:S(2)}) collective-permute-start(bf16[11,4,128,128]{3,2,1,0:T(8,128)(2,1)} %get-tuple-element.27), channel_id=1, source_target_pairs={{0,1},{1,0},{2,3},{3,2},{4,5},{5,4},{6,7},{7,6},{8,9},{9,8},{10,11... | collective-permute-start | bytes 4325384 | tf_op jit(solution)/shard_map/ppermute | solution.py:336
  35.9 3.1 %collective-permute-done.4.got_ref = bf16[11,4,128,128]{3,2,1,0:T(8,128)(2,1)S(1)} collective-permute-done((bf16[11,4,128,128]{3,2,1,0:T(8,128)(2,1)}, bf16[11,4,128,128]{3,2,1,0:T(8,128)(2,1)S(1)}, u32[]{:S(2)}, u32[]{:S(2)}) %collective-permute-start.4) | collective-permute-done | bytes 1441824 | tf_op jit(solution)/shard_map/ppermute | solution.py:336
  39.0 1.4 %copy-done.1 = bf16[11,4,128,128]{3,2,1,0:T(8,128)(2,1)S(1)} copy-done((bf16[11,4,128,128]{3,2,1,0:T(8,128)(2,1)S(1)}, bf16[11,4,128,128]{3,2,1,0:T(8,128)(2,1)}, u32[]{:S(2)}) %copy-start.1) | copy-done | bytes 1441816
  40.3 0.4 sum_over_core.1
  40.8 3.1 %collective-permute-start.5 = (bf16[18,512]{1,0:T(8,128)(2,1)S(1)}, bf16[18,512]{1,0:T(8,128)(2,1)S(1)}, u32[]{:S(2)}, u32[]{:S(2)}) collective-permute-start(bf16[18,512]{1,0:T(8,128)(2,1)S(1)} %get-tuple-element.43), channel_id=1, source_target_pairs={{0,4},{4,8},{8,12},{12,16},{16,20},{20,24},{24,28},{28,32},{32,36}... | collective-permute-start | bytes 55304 | tf_op jit(solution)/shard_map/ppermute | solution.py:279
  43.9 0.1 pad.4.clone
  44.0 4.6 %collective-permute-start.10 = (bf16[11,128,128]{2,1,0:T(8,128)(2,1)S(1)}, bf16[11,128,128]{2,1,0:T(8,128)(2,1)S(1)}, u32[]{:S(2)}, u32[]{:S(2)}) collective-permute-start(bf16[11,128,128]{2,1,0:T(8,128)(2,1)S(1)} %get-tuple-element.34), channel_id=1, source_target_pairs={{0,8},{4,12},{8,0},{12,4},{1,9},{5,13},{9,1},{13,5},{2,10},{6,14},... | collective-permute-start | bytes 1081352 | tf_op jit(solution)/shard_map/ppermute | solution.py:340
  48.6 1.5 %collective-permute-start.9 = (bf16[11,128,128]{2,1,0:T(8,128)(2,1)S(1)}, bf16[11,128,128]{2,1,0:T(8,128)(2,1)S(1)}, u32[]{:S(2)}, u32[]{:S(2)}) collective-permute-start(bf16[11,128,128]{2,1,0:T(8,128)(2,1)S(1)} %get-tuple-element.33), channel_id=1, source_target_pairs={{0,4},{4,8},{8,12},{12,0},{1,5},{5,9},{9,13},{13,1},{2,6},{6,10},{... | collective-permute-start | bytes 1081352 | tf_op jit(solution)/shard_map/ppermute | solution.py:340
  50.0 1.3 %collective-permute-start.6 = (bf16[18,512]{1,0:T(8,128)(2,1)S(1)}, bf16[18,512]{1,0:T(8,128)(2,1)S(1)}, u32[]{:S(2)}, u32[]{:S(2)}) collective-permute-start(bf16[18,512]{1,0:T(8,128)(2,1)S(1)} %get-tuple-element.44), channel_id=1, source_target_pairs={{4,0},{8,4},{12,8},{16,12},{20,16},{24,20},{28,24},{32,28},{36,32}... | collective-permute-start | bytes 55304 | tf_op jit(solution)/shard_map/ppermute | solution.py:279
  51.4 13.0 %collective-permute-done.6 = bf16[18,512]{1,0:T(8,128)(2,1)S(1)} collective-permute-done((bf16[18,512]{1,0:T(8,128)(2,1)S(1)}, bf16[18,512]{1,0:T(8,128)(2,1)S(1)}, u32[]{:S(2)}, u32[]{:S(2)}) %collective-permute-start.6) | collective-permute-done | bytes 18464 | tf_op jit(solution)/shard_map/ppermute | solution.py:279
  64.5 0.1 pad_maximum_fusion
  64.6 1.6 %collective-permute-start.7 = (bf16[4,512]{1,0:T(4,128)(2,1)S(1)}, bf16[4,512]{1,0:T(4,128)(2,1)S(1)}, u32[]{:S(2)}, u32[]{:S(2)}) collective-permute-start(bf16[4,512]{1,0:T(4,128)(2,1)S(1)} %get-tuple-element.42), channel_id=1, source_target_pairs={{0,3},{1,2},{2,1},{3,0},{4,7},{5,6},{6,5},{7,4},{8,11},{9,10},{10,... | collective-permute-start | bytes 12296 | tf_op jit(solution)/shard_map/ppermute | solution.py:287
  66.2 0.1 pad.1.clone
  66.4 0.9 sum_over_x.1
  67.3 9.1 %all-to-all-start = ((bf16[16,88,128]{2,1,0:T(8,128)(2,1)}), bf16[16,88,128]{2,1,0:T(8,128)(2,1)S(1)}, u32[]{:S(2)}, u32[]{:S(2)}) async-start(bf16[16,88,128]{2,1,0:T(8,128)(2,1)} %sum_over_x.1), calls=%async_computation | async-start | bytes 720896 | tf_op jit(solution)/shard_map/all_to_all | solution.py:344
  76.4 0.1 fusion.3
  76.5 0.9 fusion
  77.5 9.6 %all-to-all-done = bf16[16,88,128]{2,1,0:T(8,128)(2,1)S(1)} async-done(((bf16[16,88,128]{2,1,0:T(8,128)(2,1)}), bf16[16,88,128]{2,1,0:T(8,128)(2,1)S(1)}, u32[]{:S(2)}, u32[]{:S(2)}) %all-to-all-start) | async-done | bytes 360480 | tf_op jit(solution)/shard_map/all_to_all | solution.py:344
  87.1 8.9 %all-gather = bf16[352,128]{1,0:T(8,128)(2,1)S(1)} all-gather(bf16[88,128]{1,0:T(8,128)(2,1)S(1)} %reduce_sum.12), channel_id=2, replica_groups=mesh['y_lo'=2,'z'=8,'x'=4,'y_hi'=2,'core'=2] {'y_hi','core'}, dimensions={0}, use_global_device_ids=true | all-gather | bytes 112640 | tf_op jit(solution)/shard_map/all_gather | solution.py:346
  96.0 0.6 sum_over_lon.1
  (36 shorter events, 0.3 us)
Async XLA Ops:
  1.5 8.1 %collective-permute-start = (bf16[4,512]{1,0:T(4,128)(2,1)S(1)}, bf16[4,512]{1,0:T(4,128)(2,1)S(1)}, u32[]{:S(2)}, u32[]{:S(2)}) collective-permute-start(bf16[4,512]{1,0:T(4,128)(2,1)S(1)} %get-tuple-element.49), channel_id=1, source_target_pairs={{0,3},{1,2},{2,1},{3,0},{4,7},{5,6},{6,5},{7,4},{8,11},{9,10},{10,... | collective-permute-start | bytes 12296 | tf_op jit(solution)/shard_map/ppermute | solution.py:287
  5.8 3.7 %collective-permute-start.1 = (bf16[4,512]{1,0:T(4,128)(2,1)S(1)}, bf16[4,512]{1,0:T(4,128)(2,1)S(1)}, u32[]{:S(2)}, u32[]{:S(2)}) collective-permute-start(bf16[4,512]{1,0:T(4,128)(2,1)S(1)} %get-tuple-element.50), channel_id=1, source_target_pairs={{0,1},{1,0},{2,3},{3,2},{4,5},{5,4},{6,7},{7,6},{8,9},{9,8},{10,11... | collective-permute-start | bytes 12296 | tf_op jit(solution)/shard_map/ppermute | solution.py:283
  9.6 18.6 %collective-permute-start.3 = (bf16[18,512]{1,0:T(8,128)(2,1)S(1)}, bf16[18,512]{1,0:T(8,128)(2,1)S(1)}, u32[]{:S(2)}, u32[]{:S(2)}) collective-permute-start(bf16[18,512]{1,0:T(8,128)(2,1)S(1)} %pad_maximum_fusion.2), channel_id=1, source_target_pairs={{4,0},{8,4},{12,8},{16,12},{20,16},{24,20},{28,24},{32,28},{36,32}... | collective-permute-start | bytes 55304 | tf_op jit(solution)/shard_map/ppermute | solution.py:279
  10.9 17.3 %collective-permute-start.2 = (bf16[18,512]{1,0:T(8,128)(2,1)S(1)}, bf16[18,512]{1,0:T(8,128)(2,1)S(1)}, u32[]{:S(2)}, u32[]{:S(2)}) collective-permute-start(bf16[18,512]{1,0:T(8,128)(2,1)S(1)} %pad_maximum_fusion.1), channel_id=1, source_target_pairs={{0,4},{4,8},{8,12},{12,16},{16,20},{20,24},{24,28},{28,32},{32,36}... | collective-permute-start | bytes 55304 | tf_op jit(solution)/shard_map/ppermute | solution.py:279
  28.2 0.9 copy-start.2
  33.7 1.1 %copy-start = (bf16[11,4,128,128]{3,2,1,0:T(8,128)(2,1)}, bf16[11,4,128,128]{3,2,1,0:T(8,128)(2,1)S(1)}, u32[]{:S(2)}) copy-start(bf16[11,4,128,128]{3,2,1,0:T(8,128)(2,1)S(1)} %get-tuple-element.26.keep_ref) | copy-start | bytes 4325380
  34.9 4.1 %collective-permute-start.4 = (bf16[11,4,128,128]{3,2,1,0:T(8,128)(2,1)}, bf16[11,4,128,128]{3,2,1,0:T(8,128)(2,1)S(1)}, u32[]{:S(2)}, u32[]{:S(2)}) collective-permute-start(bf16[11,4,128,128]{3,2,1,0:T(8,128)(2,1)} %get-tuple-element.27), channel_id=1, source_target_pairs={{0,1},{1,0},{2,3},{3,2},{4,5},{5,4},{6,7},{7,6},{8,9},{9,8},{10,11... | collective-permute-start | bytes 4325384 | tf_op jit(solution)/shard_map/ppermute | solution.py:336
  39.0 1.4 %copy-start.1 = (bf16[11,4,128,128]{3,2,1,0:T(8,128)(2,1)S(1)}, bf16[11,4,128,128]{3,2,1,0:T(8,128)(2,1)}, u32[]{:S(2)}) copy-start(bf16[11,4,128,128]{3,2,1,0:T(8,128)(2,1)} %copy-done) | copy-start | bytes 4325380
  40.8 10.6 %collective-permute-start.5 = (bf16[18,512]{1,0:T(8,128)(2,1)S(1)}, bf16[18,512]{1,0:T(8,128)(2,1)S(1)}, u32[]{:S(2)}, u32[]{:S(2)}) collective-permute-start(bf16[18,512]{1,0:T(8,128)(2,1)S(1)} %get-tuple-element.43), channel_id=1, source_target_pairs={{0,4},{4,8},{8,12},{12,16},{16,20},{20,24},{24,28},{28,32},{32,36}... | collective-permute-start | bytes 55304 | tf_op jit(solution)/shard_map/ppermute | solution.py:279
  44.0 22.3 %collective-permute-start.10 = (bf16[11,128,128]{2,1,0:T(8,128)(2,1)S(1)}, bf16[11,128,128]{2,1,0:T(8,128)(2,1)S(1)}, u32[]{:S(2)}, u32[]{:S(2)}) collective-permute-start(bf16[11,128,128]{2,1,0:T(8,128)(2,1)S(1)} %get-tuple-element.34), channel_id=1, source_target_pairs={{0,8},{4,12},{8,0},{12,4},{1,9},{5,13},{9,1},{13,5},{2,10},{6,14},... | collective-permute-start | bytes 1081352 | tf_op jit(solution)/shard_map/ppermute | solution.py:340
  48.6 17.8 %collective-permute-start.11 = (bf16[11,128,128]{2,1,0:T(8,128)(2,1)S(1)}, bf16[11,128,128]{2,1,0:T(8,128)(2,1)S(1)}, u32[]{:S(2)}, u32[]{:S(2)}) collective-permute-start(bf16[11,128,128]{2,1,0:T(8,128)(2,1)S(1)} %get-tuple-element.35), channel_id=1, source_target_pairs={{0,12},{4,0},{8,4},{12,8},{1,13},{5,1},{9,5},{13,9},{2,14},{6,2},{... | collective-permute-start | bytes 1081352 | tf_op jit(solution)/shard_map/ppermute | solution.py:340
  48.6 17.8 %collective-permute-start.9 = (bf16[11,128,128]{2,1,0:T(8,128)(2,1)S(1)}, bf16[11,128,128]{2,1,0:T(8,128)(2,1)S(1)}, u32[]{:S(2)}, u32[]{:S(2)}) collective-permute-start(bf16[11,128,128]{2,1,0:T(8,128)(2,1)S(1)} %get-tuple-element.33), channel_id=1, source_target_pairs={{0,4},{4,8},{8,12},{12,0},{1,5},{5,9},{9,13},{13,1},{2,6},{6,10},{... | collective-permute-start | bytes 1081352 | tf_op jit(solution)/shard_map/ppermute | solution.py:340
  50.0 14.4 %collective-permute-start.6 = (bf16[18,512]{1,0:T(8,128)(2,1)S(1)}, bf16[18,512]{1,0:T(8,128)(2,1)S(1)}, u32[]{:S(2)}, u32[]{:S(2)}) collective-permute-start(bf16[18,512]{1,0:T(8,128)(2,1)S(1)} %get-tuple-element.44), channel_id=1, source_target_pairs={{4,0},{8,4},{12,8},{16,12},{20,16},{24,20},{28,24},{32,28},{36,32}... | collective-permute-start | bytes 55304 | tf_op jit(solution)/shard_map/ppermute | solution.py:279
  64.6 11.8 %collective-permute-start.7 = (bf16[4,512]{1,0:T(4,128)(2,1)S(1)}, bf16[4,512]{1,0:T(4,128)(2,1)S(1)}, u32[]{:S(2)}, u32[]{:S(2)}) collective-permute-start(bf16[4,512]{1,0:T(4,128)(2,1)S(1)} %get-tuple-element.42), channel_id=1, source_target_pairs={{0,3},{1,2},{2,1},{3,0},{4,7},{5,6},{6,5},{7,4},{8,11},{9,10},{10,... | collective-permute-start | bytes 12296 | tf_op jit(solution)/shard_map/ppermute | solution.py:287
  66.2 10.1 %collective-permute-start.8 = (bf16[4,512]{1,0:T(4,128)(2,1)S(1)}, bf16[4,512]{1,0:T(4,128)(2,1)S(1)}, u32[]{:S(2)}, u32[]{:S(2)}) collective-permute-start(bf16[4,512]{1,0:T(4,128)(2,1)S(1)} %get-tuple-element.41), channel_id=1, source_target_pairs={{0,1},{1,0},{2,3},{3,2},{4,5},{5,4},{6,7},{7,6},{8,9},{9,8},{10,11... | collective-permute-start | bytes 12296 | tf_op jit(solution)/shard_map/ppermute | solution.py:283
  66.4 10.2 %copy-start.3 = (bf16[512,512]{1,0:T(8,128)(2,1)S(1)}, bf16[512,512]{1,0:T(8,128)(2,1)}, u32[]{:S(2)}) copy-start(bf16[512,512]{1,0:T(8,128)(2,1)} %param.17) | copy-start | bytes 1572868
  67.3 19.8 %all-to-all-start = ((bf16[16,88,128]{2,1,0:T(8,128)(2,1)}), bf16[16,88,128]{2,1,0:T(8,128)(2,1)S(1)}, u32[]{:S(2)}, u32[]{:S(2)}) async-start(bf16[16,88,128]{2,1,0:T(8,128)(2,1)} %sum_over_x.1), calls=%async_computation | async-start | bytes 720896 | tf_op jit(solution)/shard_map/all_to_all | solution.py:344

commit v3 on v2

--- a/solution.py
+++ b/solution.py
@@ -8,9 +8,11 @@
 
 D = 512
 CH = 227
-LAT = ("y_lo", "z", "x")
+LAT = ("y_lo", "z_hi", "z_lo", "x_hi", "x_lo")
 LON = ("y_hi", "core")
-SIZES = {"y_lo": 2, "z": 8, "x": 4, "y_hi": 2, "core": 2}
+NEAR = ("y_lo", "z_lo", "x_lo")
+FAR = ("z_hi", "x_hi")
+SIZES = {"y_lo": 2, "z_hi": 4, "z_lo": 2, "x_hi": 2, "x_lo": 2, "y_hi": 2, "core": 2}
 F32 = jnp.float32
 BF = jnp.bfloat16
 PANELS = 11
@@ -39,23 +41,40 @@
     ref[1] = value[:, width:].astype(ref.dtype)
 
 
-W_EM, W_EG, W_E2, W_NODE, GRID, MESH, W_OUT = (0, 512, 1024, 1536, 2560, 2816, 2880)
-
-
 def main_kernel(
+    core_ref,
+    live_ref,
+    bias_ref,
     place_ref,
-    north_ref,
-    south_ref,
-    mate_ref,
-    opposite_ref,
-    pack_ref,
-    bias_ref,
-    cot_ref,
-    core_ref,
+    pair_hbm,
+    other_hbm,
+    mate_hbm,
+    opposite_hbm,
+    mesh_hbm,
+    w_em_hbm,
+    g_hbm,
+    w_eg_hbm,
+    w_e2_hbm,
+    w_node_hbm,
+    cot_hbm,
+    w_out_hbm,
     grid_ref,
     slot_ref,
     keep_ref,
     send_ref,
+    pair_ref,
+    other_ref,
+    mate_ref,
+    opposite_ref,
+    mesh_ref,
+    w_em_ref,
+    g_ref,
+    w_eg_ref,
+    w_e2_ref,
+    w_node_ref,
+    cot_ref,
+    w_out_ref,
+    sems,
     ext_ref,
     ng_half,
     og_half,
@@ -64,29 +83,45 @@
     sl_half,
     slope_ref,
     og_ref,
+    wo_ref,
 ):
-    w_em_ref = pack_ref.at[W_EM:W_EG]
-    w_eg_ref = pack_ref.at[W_EG:W_E2]
-    w_e2_ref = pack_ref.at[W_E2:W_NODE]
-    w_node_ref = pack_ref.at[W_NODE:GRID]
-    g_ref = pack_ref.at[GRID:MESH]
-    mesh_ref = pack_ref.at[MESH:W_OUT]
-    wo_ref = pack_ref.at[W_OUT : W_OUT + 256]
+    ways = (
+        (mesh_hbm, mesh_ref),
+        (pair_hbm, pair_ref),
+        (other_hbm, other_ref),
+        (mate_hbm, mate_ref),
+        (opposite_hbm, opposite_ref),
+        (w_em_hbm, w_em_ref),
+        (g_hbm, g_ref),
+        (w_eg_hbm, w_eg_ref),
+        (w_e2_hbm, w_e2_ref),
+        (w_node_hbm, w_node_ref),
+        (cot_hbm, cot_ref),
+        (w_out_hbm, w_out_ref),
+    )
+    copies = [pltpu.make_async_copy(a, b, sems.at[i]) for i, (a, b) in enumerate(ways)]
+    for copy in copies:
+        copy.start()
     core = core_ref[0]
     points = 256
+    ext_ref[64:, :] = jnp.zeros((64, D), F32)
+    for copy in copies[:5]:
+        copy.wait()
     ext_ref[:64, :] = mesh_ref[...].astype(F32)
-    ext_ref[64:, :] = jnp.zeros((64, D), F32)
-    ext_ref[64:82, :] = north_ref[...].astype(F32)
-    ext_ref[88:106, :] = south_ref[...].astype(F32)
+    ext_ref[64:82, :] = pair_ref[...].astype(F32)
+    ext_ref[88:106, :] = other_ref[...].astype(F32)
     ext_ref[112:116, :] = mate_ref[...].astype(F32)
     ext_ref[120:124, :] = opposite_ref[...].astype(F32)
     ext = ext_ref[...].astype(BF)
     row = lax.broadcasted_iota(jnp.int32, (128, points), 0)
     hots = [jnp.where(row == place_ref[k : k + 1, :], 1.0, 0.0).astype(BF) for k in range(3)]
-    g = g_ref[...]
+    copies[5].wait()
     projected = mm(ext, w_em_ref[...])
     high, low = split(projected)
     both = jnp.concatenate([high, low], axis=0)
+    copies[6].wait()
+    copies[7].wait()
+    g = g_ref[...]
     grid_proj = mm(g, w_eg_ref[...]) + bias_ref[0:1, :]
     hidden_sum = None
     for k in range(3):
@@ -97,8 +132,14 @@
         hidden = hidden.astype(F32)
         hidden_sum = hidden if hidden_sum is None else hidden_sum + hidden
     hs_high, hs_low = split(hidden_sum)
+    for copy in copies[8:]:
+        copy.wait()
     og_ref[...] = jnp.zeros_like(og_ref)
-    og_ref[:CH, :] = cot_ref[...]
+    wo_ref[...] = jnp.zeros_like(wo_ref)
+    column = lax.broadcasted_iota(jnp.int32, (CH, points), 1)
+    cot = cot_ref[...]
+    og_ref[:CH, :] = jnp.where(column < live_ref[0], cot, jnp.zeros_like(cot))
+    wo_ref[:CH, :] = w_out_ref[...]
     out_grad = og_ref[...].T
     halves(og_half, out_grad)
 
@@ -127,9 +168,10 @@
     grid_ref[...] = mm_nt(node_grad, w_node_ref[:D, :]) + mm_nt(edge_sum, w_eg_ref[...])
 
     def put(ref, panel, value):
-        v = value.reshape(16, 4, 8, 128)
-        for x in range(4):
-            ref[panel, x] = v[:, x].reshape(128, 128).astype(BF)
+        v = value.reshape(2, 4, 2, 2, 2, 8, 128)
+        for i in range(8):
+            tile = v[i >> 2, :, (i >> 1) & 1, :, i & 1]
+            ref[panel, i] = tile.reshape(64, 128).astype(BF)
 
     def put_wide(ref, panel, value):
         put(ref, panel, value[:, :128])
@@ -143,15 +185,12 @@
         put_wide(ref, 4, mm_tn(hs_high, ag) + mm_tn(hs_low, ag))
         ng = ng_half[which]
         for half, left in enumerate((g, aggregate)):
-            value = mm_tn(left, ng)
-            v = value.reshape(8, 4, 2, 8, 256)
-            for x in range(4):
+            v = mm_tn(left, ng).reshape(4, 2, 2, 2, 2, 8, 256)
+            for i in range(4):
                 for eight in range(2):
-                    tile = v[:, x, eight].reshape(64, 256).astype(BF)
+                    tile = v[:, i >> 1, :, i & 1, eight].reshape(64, 256).astype(BF)
                     for wide in range(2):
-                        ref[6 + 2 * eight + wide, x, half * 64 : half * 64 + 64, :] = tile[
-                            :, wide * 128 : wide * 128 + 128
-                        ]
+                        ref[6 + 2 * eight + wide, 4 * half + i] = tile[:, wide * 128 : wide * 128 + 128]
         put(ref, 10, mm_tn(node_hidden, og_half[which]))
 
 
@@ -169,17 +208,20 @@
 
 def main_call(*args):
     shape = jax.ShapeDtypeStruct
+    inputs = args[4:]
     return pl.pallas_call(
         main_kernel,
         out_shape=(
             shape((256, D), F32),
             shape((128, D), F32),
-            shape((PANELS, 4, 128, 128), BF),
-            shape((PANELS, 4, 128, 128), BF),
+            shape((PANELS, 8, 64, 128), BF),
+            shape((PANELS, 8, 64, 128), BF),
         ),
-        in_specs=vmem(8) + smem(1),
+        in_specs=smem(2) + vmem(2) + [pl.BlockSpec(memory_space=pltpu.HBM)] * len(inputs),
         out_specs=tuple(vmem(4)),
-        scratch_shapes=[
+        scratch_shapes=[pltpu.VMEM(a.shape, a.dtype) for a in inputs]
+        + [
+            pltpu.SemaphoreType.DMA((len(inputs),)),
             pltpu.VMEM((128, D), F32),
             pltpu.VMEM((2, 256, 256), BF),
             pltpu.VMEM((2, 256, 128), BF),
@@ -188,49 +230,68 @@
             pltpu.VMEM((2, 256, 256), BF),
             pltpu.VMEM((3, 256, D), F32),
             pltpu.VMEM((256, 256), BF),
+            pltpu.VMEM((256, D), BF),
         ],
-        compiler_params=params(28),
+        compiler_params=params(56),
         name="decoder_grads",
     )(*args)
 
 
-def core_sum_kernel(x_ref, keep_ref, got_ref, own_ref, *sends):
-    x = x_ref[0]
-    own_ref[...] = keep_ref[:, x].astype(F32) + got_ref[:, x].astype(F32)
+def core_sum_kernel(mine_ref, keep_ref, got_ref, own_ref, *sends):
+    mine = mine_ref[0]
+    own_ref[...] = keep_ref[:, mine].astype(F32) + got_ref[:, mine].astype(F32)
     for step, ref in enumerate(sends):
-        to = (x + step + 1) & 3
+        to = mine ^ (step + 1)
         ref[...] = (keep_ref[:, to].astype(F32) + got_ref[:, to].astype(F32)).astype(BF)
 
 
-def core_sum(x, keep, got):
+def core_sum(mine, keep, got):
     shape = jax.ShapeDtypeStruct
-    part = (PANELS, 128, 128)
+    part = (PANELS, 64, 128)
     return pl.pallas_call(
         core_sum_kernel,
-        out_shape=(shape(part, F32),) + (shape(part, BF),) * 3,
+        out_shape=(shape(part, F32),) + (shape(part, BF),) * 7,
         in_specs=smem(1) + vmem(2),
-        out_specs=tuple(vmem(4)),
+        out_specs=tuple(vmem(8)),
         compiler_params=params(12),
         name="sum_over_core",
-    )(x, keep, got)
-
-
-def x_sum_kernel(own_ref, a_ref, b_ref, c_ref, out_ref):
-    total = own_ref[...] + a_ref[...].astype(F32) + b_ref[...].astype(F32) + c_ref[...].astype(F32)
-    total = total.reshape(PANELS, 16, 8, 128)
-    for i in range(16):
+    )(mine, keep, got)
+
+
+def near_sum_kernel(own_ref, *refs):
+    out_ref = refs[-1]
+    total = own_ref[...]
+    for ref in refs[:-1]:
+        total = total + ref[...].astype(F32)
+    total = total.reshape(PANELS, 8, 8, 128)
+    for i in range(8):
         out_ref[i] = total[:, i].reshape(PANELS * 8, 128).astype(BF)
 
 
-def x_sum(own, a, b, c):
+def near_sum(own, *came):
     return pl.pallas_call(
-        x_sum_kernel,
-        out_shape=jax.ShapeDtypeStruct((16, PANELS * 8, 128), BF),
-        in_specs=vmem(4),
+        near_sum_kernel,
+        out_shape=jax.ShapeDtypeStruct((8, PANELS * 8, 128), BF),
+        in_specs=vmem(8),
         out_specs=vmem(1)[0],
         compiler_params=params(8),
-        name="sum_over_x",
-    )(own, a, b, c)
+        name="sum_over_near",
+    )(own, *came)
+
+
+def far_sum_kernel(in_ref, out_ref):
+    out_ref[...] = jnp.sum(in_ref[...].astype(F32), axis=0).astype(BF)
+
+
+def far_sum(chunks):
+    return pl.pallas_call(
+        far_sum_kernel,
+        out_shape=jax.ShapeDtypeStruct((PANELS * 8, 128), BF),
+        in_specs=vmem(1),
+        out_specs=vmem(1)[0],
+        compiler_params=params(4),
+        name="sum_over_far",
+    )(chunks)
 
 
 def last_kernel(in_ref, em_ref, eg_ref, e2_ref, node_ref, out_ref):
@@ -271,12 +332,13 @@
     )(gathered)
 
 
-def shift(value, axes, steps):
-    size = 1
-    for a in axes:
-        size *= SIZES[a]
-    pairs = [(i, i + steps) for i in range(size) if 0 <= i + steps < size]
-    return lax.ppermute(value, axes, pairs)
+def to_pair(value):
+    return lax.ppermute(value, "x_lo", [(0, 1), (1, 0)])
+
+
+def to_other(value):
+    odd = [(i, i + 1) for i in range(1, 63, 2)]
+    return lax.ppermute(value, LAT, odd + [(j, i) for i, j in odd])
 
 
 def to_mate(value):
@@ -302,7 +364,8 @@
     bias_node,
 ):
     core = lax.axis_index("core").astype(jnp.int32)
-    x = lax.axis_index("x").astype(jnp.int32).reshape(1)
+    odd = lax.axis_index("x_lo").astype(jnp.int32)
+    near = lax.axis_index(NEAR).astype(jnp.int32).reshape(1)
     first, final = mesh_latent[:, 0], mesh_latent[:, 15]
     mate = to_mate(jnp.where(core == 0, final, first))
     opposite = to_opposite(jnp.where(core == 0, first, final))
@@ -310,45 +373,49 @@
     east = jnp.where(core == 0, mate, opposite)
     top = jnp.concatenate([west[:1], mesh_latent[0], east[:1]], axis=0)
     bottom = jnp.concatenate([west[3:], mesh_latent[3], east[3:]], axis=0)
-    north = shift(bottom, LAT, 1)
-    south = shift(top, LAT, -1)
-    pack = jnp.concatenate(
-        [w_em, w_eg, w_e2, w_node, grid_latent[0, 0], mesh_latent.reshape(64, D), w_out.T, jnp.zeros((29, D), BF)]
-    )
-    live_point = lax.broadcasted_iota(jnp.int32, (CH, 256), 1) < live[0, 0]
-    out_grad = jnp.where(live_point, cotangent[0, 0].T, jnp.zeros((), BF))
+    pair = to_pair(jnp.where(odd == 1, top, bottom))
+    other = to_other(jnp.where(odd == 1, bottom, top))
     slot = neighbours[0, 0]
     r, c = slot // 18, slot % 18
     side = jnp.where(c == 0, 120 - 8 * core, 112 + 8 * core) + r - 1
     inner = jnp.where((c == 0) | (c == 17), side, (r - 1) * 16 + c - 1)
-    place = jnp.where(r == 0, 64 + c, jnp.where(r == 5, 88 + c, inner))
+    place = jnp.where(r == 0, 88 - 24 * odd + c, jnp.where(r == 5, 64 + 24 * odd + c, inner))
     grid_grad, slots, keep, send = main_call(
+        core.reshape(1),
+        live.reshape(1),
+        jnp.stack([bias_edge, bias_node]),
         place,
-        north,
-        south,
+        pair,
+        other,
         mate,
         opposite,
-        pack,
-        jnp.stack([bias_edge, bias_node]),
-        out_grad,
-        core.reshape(1),
+        mesh_latent.reshape(64, D),
+        w_em,
+        grid_latent[0, 0],
+        w_eg,
+        w_e2,
+        w_node,
+        cotangent[0, 0].T,
+        w_out.T,
     )
-    got = lax.ppermute(send, "core", [(0, 1), (1, 0)])
-    own, *sends = core_sum(x, keep, got)
-    slots, sends = lax.optimization_barrier((slots, sends))
+    got = to_mate(send)
+    own, *sends = core_sum(near, keep, got)
     came = [
-        lax.ppermute(part, "x", [(i, (i + step + 1) % 4) for i in range(4)])
+        lax.ppermute(part, NEAR, [(i, i ^ (step + 1)) for i in range(8)])
         for step, part in enumerate(sends)
     ]
-    chunks = x_sum(own, *came)
-    chunks = lax.all_to_all(chunks, ("y_lo", "z"), 0, 0, tiled=True)
-    part = jnp.sum(chunks.astype(F32), axis=0).astype(BF)
+    slots, came[0] = lax.optimization_barrier((slots, came[0]))
+    chunks = near_sum(own, *came)
+    chunks = lax.all_to_all(chunks, FAR, 0, 0, tiled=True)
+    part = far_sum(chunks)
     gathered = lax.all_gather(part, LON, axis=0, tiled=False)
     grads = last(gathered)
 
-    from_south = shift(slots[64:82].astype(BF), LAT, -1).astype(F32)
-    from_north = shift(slots[88:106].astype(BF), LAT, 1).astype(F32)
-    ends = jnp.stack([from_north, jnp.zeros_like(from_north), jnp.zeros_like(from_north), from_south])
+    pair = to_pair(slots[64:82].astype(BF)).astype(F32)
+    other = to_other(slots[88:106].astype(BF)).astype(F32)
+    top = jnp.where(odd == 1, pair, other)
+    bottom = jnp.where(odd == 1, other, pair)
+    ends = jnp.stack([top, jnp.zeros_like(top), jnp.zeros_like(top), bottom])
     mate = slots[112:116] + jnp.where(core == 0, ends[:, 17], ends[:, 0])
     opposite = slots[120:124] + jnp.where(core == 0, ends[:, 0], ends[:, 17])
     mate = to_mate(mate.astype(BF)).astype(F32)

time: 97.5 us -> 92.3 us (0.947)
  local copies, waits for them, and re-layouts: 17.7 us -> 3.75 us
  starting transfers between devices: 31.9 us -> 44.1 us
  blocking collectives: 8.88 us -> 5.67 us
  Pallas kernels: 6.53 us -> 9.28 us
  waiting for transfers between devices: 25.7 us -> 23.5 us
    concatenate x1 -> x0, local copies, waits for them, and re-layouts: 12.6 us -> none  [on_device(): jnp.concatenate([w_em, w_eg, w_e2, w_node, grid_latent[0, 0], mesh_latent...]
    ppermute x8 -> x11, starting transfers between devices: 16.8 us -> 26.1 us  [the longest x7 18.6 us: on_device(): lax.ppermute(part, NEAR, [(i, i ^ step + 1) for i in range(8)])]
    all_to_all x1, starting transfers between devices: 9.06 us -> 3.39 us  [on_device(): chunks = lax.all_to_all(chunks, FAR, 0, 0, tiled=True)]
    ppermute x2 -> x3, starting transfers between devices: 0.01 us -> 5.49 us  [to_mate(): return lax.ppermute(value, 'core', [(0, 1), (1, 0)])]
    ppermute x8 -> x11, waiting for transfers between devices: 16.1 us -> 11.9 us  [the longest x7 11.9 us: on_device(): lax.ppermute(part, NEAR, [(i, i ^ step + 1) for i in range(8)])]
    all_gather x1, blocking collectives: 8.88 us -> 5.67 us  [on_device(): gathered = lax.all_gather(part, LON, axis=0, tiled=False)]
    ppermute x2, starting transfers between devices: 6.04 us -> 9.11 us  [to_opposite(): return lax.ppermute(value, LON, [(i, 3 - i) for i in range(4)])]
    ppermute x2 -> x3, waiting for transfers between devices: 0.01 us -> 3.06 us  [to_mate(): return lax.ppermute(value, 'core', [(0, 1), (1, 0)])]
  transfers between devices with their start and end apart: 13 -> 17, of which waited for: 3 -> 4; matrix products, arithmetic and copies ran while one was open for 18% -> 5% of each run, Pallas kernels for 1% -> 1%
where the time goes in v3:
time: 92.3 us; the launch traced here: 91.8 us
  starting transfers between devices  44.1 us (48%)
  waiting for transfers between devices  23.5 us (25%)
  Pallas kernels  9.28 us (10%)
  blocking collectives  5.67 us (6%)
  local copies, waits for them, and re-layouts  3.75 us (4%)
  other arithmetic  2.91 us (3%)
  between operations  1.57 us (2%)
  matrix products  0.94 us (1%)
    ppermute x7, starting transfers between devices, on_device(): lax.ppermute(part, NEAR, [(i, i ^ step + 1) for i in range(8)])  18.6 us
    ppermute x7, waiting for transfers between devices, on_device(): lax.ppermute(part, NEAR, [(i, i ^ step + 1) for i in range(8)])  11.9 us
    ppermute x2, starting transfers between devices, to_opposite(): return lax.ppermute(value, LON, [(i, 3 - i) for i in range(4)])  9.11 us
    all_to_all x1, waiting for transfers between devices, on_device(): chunks = lax.all_to_all(chunks, FAR, 0, 0, tiled=True)  8.55 us
    pallas_call x1, Pallas kernels, main_call(): pl.pallas_call(main_kernel, out_shape=(shape((256, D), F32), shape((128,...  7.39 us
    ppermute x2, starting transfers between devices, to_pair(): return lax.ppermute(value, 'x_lo', [(0, 1), (1, 0)])  6.25 us
    all_gather x1, blocking collectives, on_device(): gathered = lax.all_gather(part, LON, axis=0, tiled=False)  5.67 us
    ppermute x3, starting transfers between devices, to_mate(): return lax.ppermute(value, 'core', [(0, 1), (1, 0)])  5.49 us
  transfers between devices with their start and end apart: 17, of which 4 were waited for; matrix products, arithmetic and copies ran while one was open for 5% of the time, Pallas kernels for 1%

profile of v3, /device:TPU:1, one launch (start us, length us, event | category | flops | bytes accessed | tf_op | source)
XLA Modules:
  0.0 91.8 jit_solution(9897940571416677260)
XLA Ops:
  0.6 0.8 fusion.14
  1.5 4.4 %collective-permute-start = (bf16[4,512]{1,0:T(4,128)(2,1)S(1)}, bf16[4,512]{1,0:T(4,128)(2,1)S(1)}, u32[]{:S(2)}, u32[]{:S(2)}) collective-permute-start(bf16[4,512]{1,0:T(4,128)(2,1)S(1)} %get-tuple-element.57), channel_id=1, source_target_pairs={{0,3},{1,2},{2,1},{3,0},{4,7},{5,6},{6,5},{7,4},{8,11},{9,10},{10,... | collective-permute-start | bytes 12296 | tf_op jit(solution)/shard_map/ppermute | solution.py:349
  5.9 0.7 slice_bitcast_fusion.1
  6.6 1.3 %select_select_fusion.place_ref = s32[3,256]{1,0:T(4,128)} fusion(s32[1,1,3,256]{3,1,2,0:T(1,128)} %param.15, s32[]{:T(128)S(6)} %add_shard_map.7, s32[]{:T(128)S(6)} %sub.23, s32[]{:T(128)S(6)} %add_shard_map.6, s32[]{:T(128)S(6)} %sub.22), kind=kLoop, calls=%fused_computation.35 | loop fusion | flops 22272 | bytes 6160 | tf_op jit(solution)/shard_map/jit(_where)/select_n | solution.py:382
  8.0 1.3 %collective-permute-start.2 = (bf16[18,512]{1,0:T(8,128)(2,1)S(1)}, bf16[18,512]{1,0:T(8,128)(2,1)S(1)}, u32[]{:S(2)}, u32[]{:S(2)}) collective-permute-start(bf16[18,512]{1,0:T(8,128)(2,1)S(1)} %get-tuple-element.56), channel_id=1, source_target_pairs={{0,4},{4,0},{1,5},{5,1},{2,6},{6,2},{3,7},{7,3},{8,12},{12,8},{9,1... | collective-permute-start | bytes 55304 | tf_op jit(solution)/shard_map/ppermute | solution.py:336
  9.3 0.7 collective-permute-start.3
  9.9 1.3 %pad_maximum_fusion.3.bias_ref = f32[2,512]{1,0:T(2,128)} fusion(f32[1,512]{1,0:T(1,128)} %bitcast.62, f32[1,512]{1,0:T(1,128)} %bitcast.63), kind=kLoop, calls=%fused_computation.32 | loop fusion | flops 1024 | bytes 8192 | tf_op jit(solution)/shard_map/stack | solution.py:386
  12.0 0.6 copy-done.3
  12.5 7.4 %decoder_grads.1 = (f32[256,512]{1,0:T(8,128)}, f32[128,512]{1,0:T(8,128)}, bf16[11,8,64,128]{3,2,1,0:T(8,128)(2,1)}, bf16[11,8,64,128]{3,2,1,0:T(8,128)(2,1)}) custom-call(s32[1]{0:T(128)} %bitcast.core_ref, s32[1]{0:T(128)} %bitcast.55.live_ref, f32[2,512]{1,0:T(2,128)} %pad_maximum_fusion.3.bias_ref, s32[3,256]{1,0:T(4,128)} %select_select_fusion.place_ref, ...), custom_call_target="tpu_custom_call" | custom-call | tf_op jit(solution)/shard_map/decoder_grads/pallas_call | solution.py:212
  19.9 1.5 %collective-permute-start.4 = (bf16[11,8,64,128]{3,2,1,0:T(8,128)(2,1)}, bf16[11,8,64,128]{3,2,1,0:T(8,128)(2,1)S(1)}, u32[]{:S(2)}, u32[]{:S(2)}) collective-permute-start(bf16[11,8,64,128]{3,2,1,0:T(8,128)(2,1)} %get-tuple-element.29), channel_id=1, source_target_pairs={{0,1},{1,0},{2,3},{3,2},{4,5},{5,4},{6,7},{7,6},{8,9},{9,8},{10,11... | collective-permute-start | bytes 4325384 | tf_op jit(solution)/shard_map/ppermute | solution.py:345
  21.4 3.1 %collective-permute-done.4.got_ref = bf16[11,8,64,128]{3,2,1,0:T(8,128)(2,1)S(1)} collective-permute-done((bf16[11,8,64,128]{3,2,1,0:T(8,128)(2,1)}, bf16[11,8,64,128]{3,2,1,0:T(8,128)(2,1)S(1)}, u32[]{:S(2)}, u32[]{:S(2)}) %collective-permute-start.4) | collective-permute-done | bytes 1441824 | tf_op jit(solution)/shard_map/ppermute | solution.py:345
  24.5 1.4 %copy-done = bf16[11,8,64,128]{3,2,1,0:T(8,128)(2,1)S(1)} copy-done((bf16[11,8,64,128]{3,2,1,0:T(8,128)(2,1)S(1)}, bf16[11,8,64,128]{3,2,1,0:T(8,128)(2,1)}, u32[]{:S(2)}) %copy-start) | copy-done | bytes 1441816
  25.8 0.3 sum_over_core.1
  26.2 3.7 %collective-permute-start.5 = (bf16[11,64,128]{2,1,0:T(8,128)(2,1)S(1)}, bf16[11,64,128]{2,1,0:T(8,128)(2,1)S(1)}, u32[]{:S(2)}, u32[]{:S(2)}) collective-permute-start(bf16[11,64,128]{2,1,0:T(8,128)(2,1)S(1)} %get-tuple-element.30), channel_id=1, source_target_pairs={{0,4},{4,0},{16,20},{20,16},{128,132},{132,128},{144,148},{148,144... | collective-permute-start | bytes 540680 | tf_op jit(solution)/shard_map/ppermute | solution.py:404
  29.9 4.6 %collective-permute-done.5.refs_0_ = bf16[11,64,128]{2,1,0:T(8,128)(2,1)S(1)} collective-permute-done((bf16[11,64,128]{2,1,0:T(8,128)(2,1)S(1)}, bf16[11,64,128]{2,1,0:T(8,128)(2,1)S(1)}, u32[]{:S(2)}, u32[]{:S(2)}) %collective-permute-start.5) | collective-permute-done | bytes 180256 | tf_op jit(solution)/shard_map/ppermute | solution.py:404
  34.5 0.7 collective-permute-start.7
  35.2 5.0 %collective-permute-start.6 = (bf16[18,512]{1,0:T(8,128)(2,1)S(1)}, bf16[18,512]{1,0:T(8,128)(2,1)S(1)}, u32[]{:S(2)}, u32[]{:S(2)}) collective-permute-start(bf16[18,512]{1,0:T(8,128)(2,1)S(1)} %get-tuple-element.47), channel_id=1, source_target_pairs={{0,4},{4,0},{1,5},{5,1},{2,6},{6,2},{3,7},{7,3},{8,12},{12,8},{9,1... | collective-permute-start | bytes 55304 | tf_op jit(solution)/shard_map/ppermute | solution.py:336
  40.2 1.7 %collective-permute-start.10 = (bf16[11,64,128]{2,1,0:T(8,128)(2,1)S(1)}, bf16[11,64,128]{2,1,0:T(8,128)(2,1)S(1)}, u32[]{:S(2)}, u32[]{:S(2)}) collective-permute-start(bf16[11,64,128]{2,1,0:T(8,128)(2,1)S(1)} %get-tuple-element.34), channel_id=1, source_target_pairs={{0,16},{4,20},{16,0},{20,4},{128,144},{132,148},{144,128},{148,132... | collective-permute-start | bytes 540680 | tf_op jit(solution)/shard_map/ppermute | solution.py:404
  41.9 1.1 %collective-permute-start.11 = (bf16[11,64,128]{2,1,0:T(8,128)(2,1)S(1)}, bf16[11,64,128]{2,1,0:T(8,128)(2,1)S(1)}, u32[]{:S(2)}, u32[]{:S(2)}) collective-permute-start(bf16[11,64,128]{2,1,0:T(8,128)(2,1)S(1)} %get-tuple-element.35), channel_id=1, source_target_pairs={{0,20},{4,16},{16,4},{20,0},{128,148},{132,144},{144,132},{148,128... | collective-permute-start | bytes 540680 | tf_op jit(solution)/shard_map/ppermute | solution.py:404
  43.0 8.8 %collective-permute-start.12 = (bf16[11,64,128]{2,1,0:T(8,128)(2,1)S(1)}, bf16[11,64,128]{2,1,0:T(8,128)(2,1)S(1)}, u32[]{:S(2)}, u32[]{:S(2)}) collective-permute-start(bf16[11,64,128]{2,1,0:T(8,128)(2,1)S(1)} %get-tuple-element.36), channel_id=1, source_target_pairs={{0,128},{4,132},{16,144},{20,148},{128,0},{132,4},{144,16},{148,20... | collective-permute-start | bytes 540680 | tf_op jit(solution)/shard_map/ppermute | solution.py:404
  51.8 1.2 %collective-permute-start.14 = (bf16[11,64,128]{2,1,0:T(8,128)(2,1)S(1)}, bf16[11,64,128]{2,1,0:T(8,128)(2,1)S(1)}, u32[]{:S(2)}, u32[]{:S(2)}) collective-permute-start(bf16[11,64,128]{2,1,0:T(8,128)(2,1)S(1)} %get-tuple-element.38), channel_id=1, source_target_pairs={{0,144},{4,148},{16,128},{20,132},{128,16},{132,20},{144,0},{148,4... | collective-permute-start | bytes 540680 | tf_op jit(solution)/shard_map/ppermute | solution.py:404
  53.2 2.2 %collective-permute-start.15 = (bf16[11,64,128]{2,1,0:T(8,128)(2,1)S(1)}, bf16[11,64,128]{2,1,0:T(8,128)(2,1)S(1)}, u32[]{:S(2)}, u32[]{:S(2)}) collective-permute-start(bf16[11,64,128]{2,1,0:T(8,128)(2,1)S(1)} %get-tuple-element.39), channel_id=1, source_target_pairs={{0,148},{4,144},{16,132},{20,128},{128,20},{132,16},{144,4},{148,0... | collective-permute-start | bytes 540680 | tf_op jit(solution)/shard_map/ppermute | solution.py:404
  55.4 4.0 %collective-permute-start.9 = (bf16[4,512]{1,0:T(4,128)(2,1)S(1)}, bf16[4,512]{1,0:T(4,128)(2,1)S(1)}, u32[]{:S(2)}, u32[]{:S(2)}) collective-permute-start(bf16[4,512]{1,0:T(4,128)(2,1)S(1)} %get-tuple-element.45), channel_id=1, source_target_pairs={{0,1},{1,0},{2,3},{3,2},{4,5},{5,4},{6,7},{7,6},{8,9},{9,8},{10,11... | collective-permute-start | bytes 12296 | tf_op jit(solution)/shard_map/ppermute | solution.py:345
  59.4 7.3 %collective-permute-done.12.refs_3_ = bf16[11,64,128]{2,1,0:T(8,128)(2,1)S(1)} collective-permute-done((bf16[11,64,128]{2,1,0:T(8,128)(2,1)S(1)}, bf16[11,64,128]{2,1,0:T(8,128)(2,1)S(1)}, u32[]{:S(2)}, u32[]{:S(2)}) %collective-permute-start.12) | collective-permute-done | bytes 180256 | tf_op jit(solution)/shard_map/ppermute | solution.py:404
  66.6 4.7 %collective-permute-start.8 = (bf16[4,512]{1,0:T(4,128)(2,1)S(1)}, bf16[4,512]{1,0:T(4,128)(2,1)S(1)}, u32[]{:S(2)}, u32[]{:S(2)}) collective-permute-start(bf16[4,512]{1,0:T(4,128)(2,1)S(1)} %get-tuple-element.46), channel_id=1, source_target_pairs={{0,3},{1,2},{2,1},{3,0},{4,7},{5,6},{6,5},{7,4},{8,11},{9,10},{10,... | collective-permute-start | bytes 12296 | tf_op jit(solution)/shard_map/ppermute | solution.py:349
  71.5 0.9 sum_over_near.1
  72.4 3.4 %all-to-all-start = ((bf16[8,88,128]{2,1,0:T(8,128)(2,1)}), bf16[8,88,128]{2,1,0:T(8,128)(2,1)S(1)}, u32[]{:S(2)}, u32[]{:S(2)}) async-start(bf16[8,88,128]{2,1,0:T(8,128)(2,1)} %sum_over_near.1), calls=%async_computation | async-start | bytes 360448 | tf_op jit(solution)/shard_map/all_to_all | solution.py:409
  75.8 0.1 fusion.3
  76.0 0.9 %fusion = f32[4,16,512]{2,1,0:T(8,128)} fusion(bf16[512,512]{1,0:T(8,128)(2,1)S(1)} %copy-done.1, bf16[4,16,512]{2,0,1:T(4,128)(2,1)S(1)} %fusion.3), kind=kOutput, calls=%fused_computation | convolution fusion | flops 33554432 | bytes 720896 | tf_op jit(solution)/shard_map/dot_general | solution.py:26
  76.9 8.6 %all-to-all-done.in_ref = bf16[8,88,128]{2,1,0:T(8,128)(2,1)S(1)} async-done(((bf16[8,88,128]{2,1,0:T(8,128)(2,1)}), bf16[8,88,128]{2,1,0:T(8,128)(2,1)S(1)}, u32[]{:S(2)}, u32[]{:S(2)}) %all-to-all-start) | async-done | bytes 180256 | tf_op jit(solution)/shard_map/all_to_all | solution.py:409
  85.5 5.7 %all-gather = bf16[352,128]{1,0:T(8,128)(2,1)S(1)} all-gather(bf16[88,128]{1,0:T(8,128)(2,1)S(1)} %sum_over_far.1), channel_id=2, replica_groups=mesh['y_lo'=2,'z_hi'=4,'z_lo'=2,'x_hi'=2,'x_lo'=2,'y_hi'=2,'core'=2] {'y..., dimensions={0}, use_global_device_ids=true | all-gather | bytes 112640 | tf_op jit(solution)/shard_map/all_gather | solution.py:411
  91.1 0.6 sum_over_lon.1
  (45 shorter events, 0.6 us)
Async XLA Ops:
  1.5 6.4 %collective-permute-start = (bf16[4,512]{1,0:T(4,128)(2,1)S(1)}, bf16[4,512]{1,0:T(4,128)(2,1)S(1)}, u32[]{:S(2)}, u32[]{:S(2)}) collective-permute-start(bf16[4,512]{1,0:T(4,128)(2,1)S(1)} %get-tuple-element.57), channel_id=1, source_target_pairs={{0,3},{1,2},{2,1},{3,0},{4,7},{5,6},{6,5},{7,4},{8,11},{9,10},{10,... | collective-permute-start | bytes 12296 | tf_op jit(solution)/shard_map/ppermute | solution.py:349
  5.8 2.0 %collective-permute-start.1 = (bf16[4,512]{1,0:T(4,128)(2,1)S(1)}, bf16[4,512]{1,0:T(4,128)(2,1)S(1)}, u32[]{:S(2)}, u32[]{:S(2)}) collective-permute-start(bf16[4,512]{1,0:T(4,128)(2,1)S(1)} %get-tuple-element.58), channel_id=1, source_target_pairs={{0,1},{1,0},{2,3},{3,2},{4,5},{5,4},{6,7},{7,6},{8,9},{9,8},{10,11... | collective-permute-start | bytes 12296 | tf_op jit(solution)/shard_map/ppermute | solution.py:345
  7.9 4.1 %copy-start.5 = (bf16[4,512]{1,0:T(4,128)(2,1)}, bf16[4,512]{1,0:T(4,128)(2,1)S(1)}, u32[]{:S(2)}) copy-start(bf16[4,512]{1,0:T(4,128)(2,1)S(1)} %collective-permute-done.opposite_hbm) | copy-start | bytes 12292
  7.9 4.1 %copy-start.6 = (bf16[4,512]{1,0:T(4,128)(2,1)}, bf16[4,512]{1,0:T(4,128)(2,1)S(1)}, u32[]{:S(2)}) copy-start(bf16[4,512]{1,0:T(4,128)(2,1)S(1)} %collective-permute-done.1.mate_hbm) | copy-start | bytes 12292
  8.0 3.9 %collective-permute-start.2 = (bf16[18,512]{1,0:T(8,128)(2,1)S(1)}, bf16[18,512]{1,0:T(8,128)(2,1)S(1)}, u32[]{:S(2)}, u32[]{:S(2)}) collective-permute-start(bf16[18,512]{1,0:T(8,128)(2,1)S(1)} %get-tuple-element.56), channel_id=1, source_target_pairs={{0,4},{4,0},{1,5},{5,1},{2,6},{6,2},{3,7},{7,3},{8,12},{12,8},{9,1... | collective-permute-start | bytes 55304 | tf_op jit(solution)/shard_map/ppermute | solution.py:336
  9.3 2.6 %collective-permute-start.3 = (bf16[18,512]{1,0:T(8,128)(2,1)S(1)}, bf16[18,512]{1,0:T(8,128)(2,1)S(1)}, u32[]{:S(2)}, u32[]{:S(2)}) collective-permute-start(bf16[18,512]{1,0:T(8,128)(2,1)S(1)} %get-tuple-element.55), channel_id=1, source_target_pairs={{4,8},{12,16},{20,24},{28,32},{36,40},{44,48},{52,56},{60,64},{68,... | collective-permute-start | bytes 55304 | tf_op jit(solution)/shard_map/ppermute | solution.py:341
  11.9 0.6 copy-start.3
  11.9 0.6 copy-start.4
  19.9 4.5 %collective-permute-start.4 = (bf16[11,8,64,128]{3,2,1,0:T(8,128)(2,1)}, bf16[11,8,64,128]{3,2,1,0:T(8,128)(2,1)S(1)}, u32[]{:S(2)}, u32[]{:S(2)}) collective-permute-start(bf16[11,8,64,128]{3,2,1,0:T(8,128)(2,1)} %get-tuple-element.29), channel_id=1, source_target_pairs={{0,1},{1,0},{2,3},{3,2},{4,5},{5,4},{6,7},{7,6},{8,9},{9,8},{10,11... | collective-permute-start | bytes 4325384 | tf_op jit(solution)/shard_map/ppermute | solution.py:345
  24.5 1.4 %copy-start = (bf16[11,8,64,128]{3,2,1,0:T(8,128)(2,1)S(1)}, bf16[11,8,64,128]{3,2,1,0:T(8,128)(2,1)}, u32[]{:S(2)}) copy-start(bf16[11,8,64,128]{3,2,1,0:T(8,128)(2,1)} %get-tuple-element.28.keep_ref) | copy-start | bytes 4325380
  25.8 8.7 %copy-start.2 = (f32[128,512]{1,0:T(8,128)S(1)}, f32[128,512]{1,0:T(8,128)}, u32[]{:S(2)}) copy-start(f32[128,512]{1,0:T(8,128)} %get-tuple-element.31) | copy-start | bytes 786436
  26.2 8.3 %collective-permute-start.5 = (bf16[11,64,128]{2,1,0:T(8,128)(2,1)S(1)}, bf16[11,64,128]{2,1,0:T(8,128)(2,1)S(1)}, u32[]{:S(2)}, u32[]{:S(2)}) collective-permute-start(bf16[11,64,128]{2,1,0:T(8,128)(2,1)S(1)} %get-tuple-element.30), channel_id=1, source_target_pairs={{0,4},{4,0},{16,20},{20,16},{128,132},{132,128},{144,148},{148,144... | collective-permute-start | bytes 540680 | tf_op jit(solution)/shard_map/ppermute | solution.py:404
  34.5 17.2 %collective-permute-start.7 = (bf16[18,512]{1,0:T(8,128)(2,1)S(1)}, bf16[18,512]{1,0:T(8,128)(2,1)S(1)}, u32[]{:S(2)}, u32[]{:S(2)}) collective-permute-start(bf16[18,512]{1,0:T(8,128)(2,1)S(1)} %get-tuple-element.48), channel_id=1, source_target_pairs={{4,8},{12,16},{20,24},{28,32},{36,40},{44,48},{52,56},{60,64},{68,... | collective-permute-start | bytes 55304 | tf_op jit(solution)/shard_map/ppermute | solution.py:341
  35.2 16.6 %collective-permute-start.6 = (bf16[18,512]{1,0:T(8,128)(2,1)S(1)}, bf16[18,512]{1,0:T(8,128)(2,1)S(1)}, u32[]{:S(2)}, u32[]{:S(2)}) collective-permute-start(bf16[18,512]{1,0:T(8,128)(2,1)S(1)} %get-tuple-element.47), channel_id=1, source_target_pairs={{0,4},{4,0},{1,5},{5,1},{2,6},{6,2},{3,7},{7,3},{8,12},{12,8},{9,1... | collective-permute-start | bytes 55304 | tf_op jit(solution)/shard_map/ppermute | solution.py:336
  40.2 12.9 %collective-permute-start.10 = (bf16[11,64,128]{2,1,0:T(8,128)(2,1)S(1)}, bf16[11,64,128]{2,1,0:T(8,128)(2,1)S(1)}, u32[]{:S(2)}, u32[]{:S(2)}) collective-permute-start(bf16[11,64,128]{2,1,0:T(8,128)(2,1)S(1)} %get-tuple-element.34), channel_id=1, source_target_pairs={{0,16},{4,20},{16,0},{20,4},{128,144},{132,148},{144,128},{148,132... | collective-permute-start | bytes 540680 | tf_op jit(solution)/shard_map/ppermute | solution.py:404
  41.9 13.5 %collective-permute-start.11 = (bf16[11,64,128]{2,1,0:T(8,128)(2,1)S(1)}, bf16[11,64,128]{2,1,0:T(8,128)(2,1)S(1)}, u32[]{:S(2)}, u32[]{:S(2)}) collective-permute-start(bf16[11,64,128]{2,1,0:T(8,128)(2,1)S(1)} %get-tuple-element.35), channel_id=1, source_target_pairs={{0,20},{4,16},{16,4},{20,0},{128,148},{132,144},{144,132},{148,128... | collective-permute-start | bytes 540680 | tf_op jit(solution)/shard_map/ppermute | solution.py:404
  43.0 23.6 %collective-permute-start.12 = (bf16[11,64,128]{2,1,0:T(8,128)(2,1)S(1)}, bf16[11,64,128]{2,1,0:T(8,128)(2,1)S(1)}, u32[]{:S(2)}, u32[]{:S(2)}) collective-permute-start(bf16[11,64,128]{2,1,0:T(8,128)(2,1)S(1)} %get-tuple-element.36), channel_id=1, source_target_pairs={{0,128},{4,132},{16,144},{20,148},{128,0},{132,4},{144,16},{148,20... | collective-permute-start | bytes 540680 | tf_op jit(solution)/shard_map/ppermute | solution.py:404
  51.8 19.7 %collective-permute-start.13 = (bf16[11,64,128]{2,1,0:T(8,128)(2,1)S(1)}, bf16[11,64,128]{2,1,0:T(8,128)(2,1)S(1)}, u32[]{:S(2)}, u32[]{:S(2)}) collective-permute-start(bf16[11,64,128]{2,1,0:T(8,128)(2,1)S(1)} %get-tuple-element.37), channel_id=1, source_target_pairs={{0,132},{4,128},{16,148},{20,144},{128,4},{132,0},{144,20},{148,16... | collective-permute-start | bytes 540680 | tf_op jit(solution)/shard_map/ppermute | solution.py:404
  51.8 19.7 %collective-permute-start.14 = (bf16[11,64,128]{2,1,0:T(8,128)(2,1)S(1)}, bf16[11,64,128]{2,1,0:T(8,128)(2,1)S(1)}, u32[]{:S(2)}, u32[]{:S(2)}) collective-permute-start(bf16[11,64,128]{2,1,0:T(8,128)(2,1)S(1)} %get-tuple-element.38), channel_id=1, source_target_pairs={{0,144},{4,148},{16,128},{20,132},{128,16},{132,20},{144,0},{148,4... | collective-permute-start | bytes 540680 | tf_op jit(solution)/shard_map/ppermute | solution.py:404
  53.1 22.8 %copy-start.1 = (bf16[512,512]{1,0:T(8,128)(2,1)S(1)}, bf16[512,512]{1,0:T(8,128)(2,1)}, u32[]{:S(2)}) copy-start(bf16[512,512]{1,0:T(8,128)(2,1)} %w_em_hbm.1) | copy-start | bytes 1572868
  53.2 18.3 %collective-permute-start.15 = (bf16[11,64,128]{2,1,0:T(8,128)(2,1)S(1)}, bf16[11,64,128]{2,1,0:T(8,128)(2,1)S(1)}, u32[]{:S(2)}, u32[]{:S(2)}) collective-permute-start(bf16[11,64,128]{2,1,0:T(8,128)(2,1)S(1)} %get-tuple-element.39), channel_id=1, source_target_pairs={{0,148},{4,144},{16,132},{20,128},{128,20},{132,16},{144,4},{148,0... | collective-permute-start | bytes 540680 | tf_op jit(solution)/shard_map/ppermute | solution.py:404
  55.4 20.4 %collective-permute-start.9 = (bf16[4,512]{1,0:T(4,128)(2,1)S(1)}, bf16[4,512]{1,0:T(4,128)(2,1)S(1)}, u32[]{:S(2)}, u32[]{:S(2)}) collective-permute-start(bf16[4,512]{1,0:T(4,128)(2,1)S(1)} %get-tuple-element.45), channel_id=1, source_target_pairs={{0,1},{1,0},{2,3},{3,2},{4,5},{5,4},{6,7},{7,6},{8,9},{9,8},{10,11... | collective-permute-start | bytes 12296 | tf_op jit(solution)/shard_map/ppermute | solution.py:345
  66.6 9.2 %collective-permute-start.8 = (bf16[4,512]{1,0:T(4,128)(2,1)S(1)}, bf16[4,512]{1,0:T(4,128)(2,1)S(1)}, u32[]{:S(2)}, u32[]{:S(2)}) collective-permute-start(bf16[4,512]{1,0:T(4,128)(2,1)S(1)} %get-tuple-element.46), channel_id=1, source_target_pairs={{0,3},{1,2},{2,1},{3,0},{4,7},{5,6},{6,5},{7,4},{8,11},{9,10},{10,... | collective-permute-start | bytes 12296 | tf_op jit(solution)/shard_map/ppermute | solution.py:349
  72.4 13.1 %all-to-all-start = ((bf16[8,88,128]{2,1,0:T(8,128)(2,1)}), bf16[8,88,128]{2,1,0:T(8,128)(2,1)S(1)}, u32[]{:S(2)}, u32[]{:S(2)}) async-start(bf16[8,88,128]{2,1,0:T(8,128)(2,1)} %sum_over_near.1), calls=%async_computation | async-start | bytes 360448 | tf_op jit(solution)/shard_map/all_to_all | solution.py:409

commit v4 on v3

--- a/solution.py
+++ b/solution.py
@@ -10,11 +10,11 @@
 CH = 227
 LAT = ("y_lo", "z_hi", "z_lo", "x_hi", "x_lo")
 LON = ("y_hi", "core")
-NEAR = ("y_lo", "z_lo", "x_lo")
-FAR = ("z_hi", "x_hi")
+NEAR = ("y_lo", "z_lo", "x_hi", "x_lo")
 SIZES = {"y_lo": 2, "z_hi": 4, "z_lo": 2, "x_hi": 2, "x_lo": 2, "y_hi": 2, "core": 2}
 F32 = jnp.float32
 BF = jnp.bfloat16
+VMEM_MAIN = 56
 PANELS = 11
 
 
@@ -43,8 +43,6 @@
 
 def main_kernel(
     core_ref,
-    live_ref,
-    bias_ref,
     place_ref,
     pair_hbm,
     other_hbm,
@@ -58,10 +56,16 @@
     w_node_hbm,
     cot_hbm,
     w_out_hbm,
-    grid_ref,
+    b_edge_hbm,
+    b_node_hbm,
     slot_ref,
-    keep_ref,
-    send_ref,
+    pair_out,
+    other_out,
+    mate_out,
+    opposite_out,
+    grid_hbm,
+    send_hbm,
+    keep_hbm,
     pair_ref,
     other_ref,
     mate_ref,
@@ -74,7 +78,13 @@
     w_node_ref,
     cot_ref,
     w_out_ref,
+    b_edge_ref,
+    b_node_ref,
+    grid_ref,
+    send_ref,
+    keep_ref,
     sems,
+    out_sems,
     ext_ref,
     ng_half,
     og_half,
@@ -94,6 +104,8 @@
         (w_em_hbm, w_em_ref),
         (g_hbm, g_ref),
         (w_eg_hbm, w_eg_ref),
+        (b_edge_hbm, b_edge_ref),
+        (b_node_hbm, b_node_ref),
         (w_e2_hbm, w_e2_ref),
         (w_node_hbm, w_node_ref),
         (cot_hbm, cot_ref),
@@ -114,15 +126,16 @@
     ext_ref[120:124, :] = opposite_ref[...].astype(F32)
     ext = ext_ref[...].astype(BF)
     row = lax.broadcasted_iota(jnp.int32, (128, points), 0)
-    hots = [jnp.where(row == place_ref[k : k + 1, :], 1.0, 0.0).astype(BF) for k in range(3)]
+    hots = [jnp.where(row == (place_ref[k : k + 1, :] & 1023), 1.0, 0.0).astype(BF) for k in range(3)]
     copies[5].wait()
     projected = mm(ext, w_em_ref[...])
     high, low = split(projected)
     both = jnp.concatenate([high, low], axis=0)
     copies[6].wait()
-    copies[7].wait()
+    for copy in copies[7:10]:
+        copy.wait()
     g = g_ref[...]
-    grid_proj = mm(g, w_eg_ref[...]) + bias_ref[0:1, :]
+    grid_proj = mm(g, w_eg_ref[...]) + b_edge_ref[...]
     hidden_sum = None
     for k in range(3):
         pre = mm_tn(jnp.concatenate([hots[k], hots[k]], axis=0), both) + grid_proj
@@ -132,19 +145,18 @@
         hidden = hidden.astype(F32)
         hidden_sum = hidden if hidden_sum is None else hidden_sum + hidden
     hs_high, hs_low = split(hidden_sum)
-    for copy in copies[8:]:
+    for copy in copies[10:]:
         copy.wait()
     og_ref[...] = jnp.zeros_like(og_ref)
     wo_ref[...] = jnp.zeros_like(wo_ref)
-    column = lax.broadcasted_iota(jnp.int32, (CH, points), 1)
     cot = cot_ref[...]
-    og_ref[:CH, :] = jnp.where(column < live_ref[0], cot, jnp.zeros_like(cot))
+    og_ref[:CH, :] = jnp.where(place_ref[0:1, :] < 1024, cot, jnp.zeros_like(cot))
     wo_ref[:CH, :] = w_out_ref[...]
     out_grad = og_ref[...].T
     halves(og_half, out_grad)
 
     aggregate = (mm(hs_high, w_e2_ref[...]) + mm(hs_low, w_e2_ref[...])).astype(BF)
-    node_pre = mm(g, w_node_ref[:D, :]) + mm(aggregate, w_node_ref[D:, :]) + bias_ref[1:2, :]
+    node_pre = mm(g, w_node_ref[:D, :]) + mm(aggregate, w_node_ref[D:, :]) + b_node_ref[...]
     sigma = jax.nn.sigmoid(node_pre)
     node_hidden = (node_pre * sigma).astype(BF)
     node_grad = (mm(out_grad, wo_ref[...]) * (sigma * (1.0 + node_pre * (1.0 - sigma)))).astype(BF)
@@ -162,36 +174,50 @@
         edge_sum = edge_grad if edge_sum is None else edge_sum + edge_grad
     edge_sum = edge_sum.astype(BF)
     halves(es_half, edge_sum)
-    slot_ref[...] = slots
+    slot_ref[...] = slots[:64]
+    pair_out[...] = slots[64:82].astype(BF)
+    other_out[...] = slots[88:106].astype(BF)
+    mate_out[...] = slots[112:116]
+    opposite_out[...] = slots[120:124]
     sl_high, sl_low = split(slots)
     halves(sl_half, jnp.concatenate([sl_high, sl_low], axis=0))
     grid_ref[...] = mm_nt(node_grad, w_node_ref[:D, :]) + mm_nt(edge_sum, w_eg_ref[...])
 
+    grid_copy = pltpu.make_async_copy(grid_ref, grid_hbm, out_sems.at[0])
+    grid_copy.start()
+
     def put(ref, panel, value):
-        v = value.reshape(2, 4, 2, 2, 2, 8, 128)
-        for i in range(8):
-            tile = v[i >> 2, :, (i >> 1) & 1, :, i & 1]
-            ref[panel, i] = tile.reshape(64, 128).astype(BF)
+        v = value.reshape(2, 4, 2, 4, 8, 128)
+        for i in range(16):
+            tile = v[i >> 3, :, (i >> 2) & 1, i & 3]
+            ref[i, panel * 32 : panel * 32 + 32, :] = tile.reshape(32, 128).astype(BF)
 
     def put_wide(ref, panel, value):
         put(ref, panel, value[:, :128])
         put(ref, panel + 1, value[:, 128:])
 
     ext_both = jnp.concatenate([ext, ext], axis=0)
-    for ref, which in ((send_ref, 1 - core), (keep_ref, core)):
+    out_copies = [grid_copy]
+    for ref, out, which in ((send_ref, send_hbm, 1 - core), (keep_ref, keep_hbm, core)):
         put_wide(ref, 0, mm_tn(ext_both, sl_half[which]))
         put_wide(ref, 2, mm_tn(g, es_half[which]))
         ag = ag_half[which]
         put_wide(ref, 4, mm_tn(hs_high, ag) + mm_tn(hs_low, ag))
         ng = ng_half[which]
         for half, left in enumerate((g, aggregate)):
-            v = mm_tn(left, ng).reshape(4, 2, 2, 2, 2, 8, 256)
-            for i in range(4):
+            v = mm_tn(left, ng).reshape(4, 2, 4, 2, 8, 256)
+            for i in range(8):
                 for eight in range(2):
-                    tile = v[:, i >> 1, :, i & 1, eight].reshape(64, 256).astype(BF)
+                    tile = v[:, i >> 2, i & 3, eight].reshape(32, 256).astype(BF)
                     for wide in range(2):
-                        ref[6 + 2 * eight + wide, 4 * half + i] = tile[:, wide * 128 : wide * 128 + 128]
+                        at = (6 + 2 * eight + wide) * 32
+                        ref[8 * half + i, at : at + 32, :] = tile[:, wide * 128 : wide * 128 + 128]
         put(ref, 10, mm_tn(node_hidden, og_half[which]))
+        copy = pltpu.make_async_copy(ref, out, out_sems.at[len(out_copies)])
+        copy.start()
+        out_copies.append(copy)
+    for copy in out_copies:
+        copy.wait()
 
 
 def vmem(n):
@@ -206,22 +232,34 @@
     return pltpu.CompilerParams(vmem_limit_bytes=mebibytes * 1024 * 1024)
 
 
+ROWS = PANELS * 32
+
+
 def main_call(*args):
     shape = jax.ShapeDtypeStruct
-    inputs = args[4:]
+    inputs = args[2:]
+    hbm = pl.BlockSpec(memory_space=pltpu.HBM)
     return pl.pallas_call(
         main_kernel,
         out_shape=(
+            shape((64, D), F32),
+            shape((18, D), BF),
+            shape((18, D), BF),
+            shape((4, D), F32),
+            shape((4, D), F32),
             shape((256, D), F32),
-            shape((128, D), F32),
-            shape((PANELS, 8, 64, 128), BF),
-            shape((PANELS, 8, 64, 128), BF),
+            shape((16, ROWS, 128), BF),
+            shape((16, ROWS, 128), BF),
         ),
-        in_specs=smem(2) + vmem(2) + [pl.BlockSpec(memory_space=pltpu.HBM)] * len(inputs),
-        out_specs=tuple(vmem(4)),
+        in_specs=smem(1) + vmem(1) + [hbm] * len(inputs),
+        out_specs=tuple(vmem(5) + [hbm] * 3),
         scratch_shapes=[pltpu.VMEM(a.shape, a.dtype) for a in inputs]
         + [
+            pltpu.VMEM((256, D), F32),
+            pltpu.VMEM((16, ROWS, 128), BF),
+            pltpu.VMEM((16, ROWS, 128), BF),
             pltpu.SemaphoreType.DMA((len(inputs),)),
+            pltpu.SemaphoreType.DMA((3,)),
             pltpu.VMEM((128, D), F32),
             pltpu.VMEM((2, 256, 256), BF),
             pltpu.VMEM((2, 256, 128), BF),
@@ -232,51 +270,29 @@
             pltpu.VMEM((256, 256), BF),
             pltpu.VMEM((256, D), BF),
         ],
-        compiler_params=params(56),
+        compiler_params=params(VMEM_MAIN),
         name="decoder_grads",
     )(*args)
 
 
-def core_sum_kernel(mine_ref, keep_ref, got_ref, own_ref, *sends):
-    mine = mine_ref[0]
-    own_ref[...] = keep_ref[:, mine].astype(F32) + got_ref[:, mine].astype(F32)
-    for step, ref in enumerate(sends):
-        to = mine ^ (step + 1)
-        ref[...] = (keep_ref[:, to].astype(F32) + got_ref[:, to].astype(F32)).astype(BF)
-
-
-def core_sum(mine, keep, got):
-    shape = jax.ShapeDtypeStruct
-    part = (PANELS, 64, 128)
-    return pl.pallas_call(
-        core_sum_kernel,
-        out_shape=(shape(part, F32),) + (shape(part, BF),) * 7,
-        in_specs=smem(1) + vmem(2),
-        out_specs=tuple(vmem(8)),
-        compiler_params=params(12),
-        name="sum_over_core",
-    )(mine, keep, got)
-
-
-def near_sum_kernel(own_ref, *refs):
-    out_ref = refs[-1]
-    total = own_ref[...]
-    for ref in refs[:-1]:
-        total = total + ref[...].astype(F32)
-    total = total.reshape(PANELS, 8, 8, 128)
-    for i in range(8):
+def near_sum_kernel(in_ref, out_ref):
+    total = in_ref[0].astype(F32)
+    for i in range(1, 16):
+        total = total + in_ref[i].astype(F32)
+    total = total.reshape(PANELS, 4, 8, 128)
+    for i in range(4):
         out_ref[i] = total[:, i].reshape(PANELS * 8, 128).astype(BF)
 
 
-def near_sum(own, *came):
+def near_sum(chunks):
     return pl.pallas_call(
         near_sum_kernel,
-        out_shape=jax.ShapeDtypeStruct((8, PANELS * 8, 128), BF),
-        in_specs=vmem(8),
+        out_shape=jax.ShapeDtypeStruct((4, PANELS * 8, 128), BF),
+        in_specs=vmem(1),
         out_specs=vmem(1)[0],
-        compiler_params=params(8),
+        compiler_params=params(6),
         name="sum_over_near",
-    )(own, *came)
+    )(chunks)
 
 
 def far_sum_kernel(in_ref, out_ref):
@@ -365,7 +381,6 @@
 ):
     core = lax.axis_index("core").astype(jnp.int32)
     odd = lax.axis_index("x_lo").astype(jnp.int32)
-    near = lax.axis_index(NEAR).astype(jnp.int32).reshape(1)
     first, final = mesh_latent[:, 0], mesh_latent[:, 15]
     mate = to_mate(jnp.where(core == 0, final, first))
     opposite = to_opposite(jnp.where(core == 0, first, final))
@@ -373,17 +388,18 @@
     east = jnp.where(core == 0, mate, opposite)
     top = jnp.concatenate([west[:1], mesh_latent[0], east[:1]], axis=0)
     bottom = jnp.concatenate([west[3:], mesh_latent[3], east[3:]], axis=0)
-    pair = to_pair(jnp.where(odd == 1, top, bottom))
-    other = to_other(jnp.where(odd == 1, bottom, top))
+    pair, other = jnp.where(odd == 1, top, bottom), jnp.where(odd == 1, bottom, top)
     slot = neighbours[0, 0]
     r, c = slot // 18, slot % 18
     side = jnp.where(c == 0, 120 - 8 * core, 112 + 8 * core) + r - 1
     inner = jnp.where((c == 0) | (c == 17), side, (r - 1) * 16 + c - 1)
     place = jnp.where(r == 0, 88 - 24 * odd + c, jnp.where(r == 5, 64 + 24 * odd + c, inner))
-    grid_grad, slots, keep, send = main_call(
+    place = jnp.where(lax.broadcasted_iota(jnp.int32, (3, 256), 1) < live[0, 0], place, place + 1024)
+    pair, other, place = lax.optimization_barrier((pair, other, place))
+    pair = to_pair(pair)
+    other = to_other(other)
+    slots, pair, other, mate, opposite, grid_grad, send, keep = main_call(
         core.reshape(1),
-        live.reshape(1),
-        jnp.stack([bias_edge, bias_node]),
         place,
         pair,
         other,
@@ -397,33 +413,31 @@
         w_node,
         cotangent[0, 0].T,
         w_out.T,
+        bias_edge.reshape(1, D),
+        bias_node.reshape(1, D),
     )
     got = to_mate(send)
-    own, *sends = core_sum(near, keep, got)
-    came = [
-        lax.ppermute(part, NEAR, [(i, i ^ (step + 1)) for i in range(8)])
-        for step, part in enumerate(sends)
-    ]
-    slots, came[0] = lax.optimization_barrier((slots, came[0]))
-    chunks = near_sum(own, *came)
-    chunks = lax.all_to_all(chunks, FAR, 0, 0, tiled=True)
+    chunks = (keep.astype(F32) + got.astype(F32)).astype(BF)
+    chunks, pair, other = lax.optimization_barrier((chunks, pair, other))
+    chunks = lax.all_to_all(chunks, NEAR, 0, 0, tiled=True)
+    chunks = lax.all_to_all(near_sum(chunks), "z_hi", 0, 0, tiled=True)
     part = far_sum(chunks)
     gathered = lax.all_gather(part, LON, axis=0, tiled=False)
     grads = last(gathered)
 
-    pair = to_pair(slots[64:82].astype(BF)).astype(F32)
-    other = to_other(slots[88:106].astype(BF)).astype(F32)
+    pair = to_pair(pair).astype(F32)
+    other = to_other(other).astype(F32)
     top = jnp.where(odd == 1, pair, other)
     bottom = jnp.where(odd == 1, other, pair)
     ends = jnp.stack([top, jnp.zeros_like(top), jnp.zeros_like(top), bottom])
-    mate = slots[112:116] + jnp.where(core == 0, ends[:, 17], ends[:, 0])
-    opposite = slots[120:124] + jnp.where(core == 0, ends[:, 0], ends[:, 17])
+    mate = mate + jnp.where(core == 0, ends[:, 17], ends[:, 0])
+    opposite = opposite + jnp.where(core == 0, ends[:, 0], ends[:, 17])
     mate = to_mate(mate.astype(BF)).astype(F32)
     opposite = to_opposite(opposite.astype(BF)).astype(F32)
     west = jnp.where(core == 0, opposite, mate)
     east = jnp.where(core == 0, mate, opposite)
     sides = jnp.concatenate([west[:, None], jnp.zeros((4, 14, D), F32), east[:, None]], axis=1)
-    owned = slots[:64].reshape(4, 16, D) + ends[:, 1:17] + sides
+    owned = slots.reshape(4, 16, D) + ends[:, 1:17] + sides
     node_sum = owned.reshape(64, D).astype(BF)
     mesh_grad = mm_nt(node_sum, w_em).reshape(4, 16, D)
     return (grid_grad.reshape(1, 1, 256, D), mesh_grad) + tuple(grads)

time: 92.3 us -> 88.2 us (0.956)
  starting transfers between devices: 44.1 us -> 32.9 us
  blocking collectives: 5.67 us -> 9.91 us
  waiting for transfers between devices: 23.5 us -> 25.8 us
  other arithmetic: 2.91 us -> 4.53 us
  local copies, waits for them, and re-layouts: 3.75 us -> 2.39 us
    ppermute x7 -> x0, starting transfers between devices: 18.6 us -> none  [on_device(): lax.ppermute(part, NEAR, [(i, i ^ step + 1) for i in range(8)])]
    ppermute x2, waiting for transfers between devices: 0.01 us -> 15.4 us  [to_pair(): return lax.ppermute(value, 'x_lo', [(0, 1), (1, 0)])]
    all_to_all x1 -> x2, starting transfers between devices: 3.39 us -> 18.7 us  [the longest x1 11.2 us: on_device(): chunks = lax.all_to_all(chunks, NEAR, 0, 0, tiled=True)]
    ppermute x7 -> x0, waiting for transfers between devices: 11.9 us -> none  [on_device(): lax.ppermute(part, NEAR, [(i, i ^ step + 1) for i in range(8)])]
    all_gather x1, blocking collectives: 5.67 us -> 9.91 us  [on_device(): gathered = lax.all_gather(part, LON, axis=0, tiled=False)]
    ppermute x2, starting transfers between devices: 6.25 us -> 2.75 us  [to_pair(): return lax.ppermute(value, 'x_lo', [(0, 1), (1, 0)])]
    ppermute x3, starting transfers between devices: 5.49 us -> 1.99 us  [to_mate(): return lax.ppermute(value, 'core', [(0, 1), (1, 0)])]
    convert_element_type x0 -> x1, other arithmetic: none -> 2.93 us  [on_device(): chunks = (keep.astype(F32) + got.astype(F32)).astype(BF)]
  transfers between devices with their start and end apart: 17 -> 11, of which waited for: 4 -> 5; matrix products, arithmetic and copies ran while one was open for 5% -> 4% of each run, Pallas kernels for 1% -> 0%
where the time goes in v4:
time: 88.2 us; the launch traced here: 87.5 us
  starting transfers between devices  32.9 us (37%)
  waiting for transfers between devices  25.8 us (29%)
  blocking collectives  9.91 us (11%)
  Pallas kernels  9.51 us (11%)
  other arithmetic  4.53 us (5%)
  local copies, waits for them, and re-layouts  2.39 us (3%)
  between operations  1.51 us (2%)
  matrix products  0.94 us (1%)
    ppermute x2, waiting for transfers between devices, to_pair(): return lax.ppermute(value, 'x_lo', [(0, 1), (1, 0)])  15.4 us
    all_to_all x1, starting transfers between devices, on_device(): chunks = lax.all_to_all(chunks, NEAR, 0, 0, tiled=True)  11.2 us
    all_gather x1, blocking collectives, on_device(): gathered = lax.all_gather(part, LON, axis=0, tiled=False)  9.91 us
    ppermute x2, starting transfers between devices, to_opposite(): return lax.ppermute(value, LON, [(i, 3 - i) for i in range(4)])  8.15 us
    pallas_call x1, Pallas kernels, main_call(): pl.pallas_call(main_kernel, out_shape=(shape((64, D), F32), shape((18, D)...  8.03 us
    all_to_all x1, starting transfers between devices, on_device(): chunks = lax.all_to_all(near_sum(chunks), 'z_hi', 0, 0, tiled=True)  7.54 us
    all_to_all x1, waiting for transfers between devices, on_device(): chunks = lax.all_to_all(near_sum(chunks), 'z_hi', 0, 0, tiled=True)  6.08 us
    ppermute x3, waiting for transfers between devices, to_mate(): return lax.ppermute(value, 'core', [(0, 1), (1, 0)])  3.06 us
  transfers between devices with their start and end apart: 11, of which 5 were waited for; matrix products, arithmetic and copies ran while one was open for 4% of the time, Pallas kernels for 0%

profile of v4, /device:TPU:1, one launch (start us, length us, event | category | flops | bytes accessed | tf_op | source)
XLA Modules:
  0.0 87.5 jit_solution(16247046326245943150)
XLA Ops:
  0.6 0.8 fusion.13
  1.5 4.4 %collective-permute-start = (bf16[4,512]{1,0:T(4,128)(2,1)S(1)}, bf16[4,512]{1,0:T(4,128)(2,1)S(1)}, u32[]{:S(2)}, u32[]{:S(2)}) collective-permute-start(bf16[4,512]{1,0:T(4,128)(2,1)S(1)} %get-tuple-element.55), channel_id=1, source_target_pairs={{0,3},{1,2},{2,1},{3,0},{4,7},{5,6},{6,5},{7,4},{8,11},{9,10},{10,... | collective-permute-start | bytes 12296 | tf_op jit(solution)/shard_map/ppermute | solution.py:365
  5.9 0.7 slice_bitcast_fusion.1
  7.3 1.3 %add_select_fusion.place_ref = s32[3,256]{1,0:T(4,128)} fusion(s32[1,1,3,256]{3,1,2,0:T(1,128)} %param.15, s32[]{:T(128)S(6)} %add_shard_map.7, s32[]{:T(128)S(6)} %sub.23, s32[]{:T(128)S(6)} %add_shard_map.6, s32[]{:T(128)S(6)} %sub.22, pred[256]{0:T(512)(128)(4,1)S(1)} %iota_compare_fusion), kind=kLoop, calls=%fused_computation.25 | loop fusion | flops 23808 | bytes 6416 | tf_op jit(solution)/shard_map/jit(_where)/select_n | solution.py:397
  8.6 0.0 collective-permute-done.opposite_hbm
  8.6 0.0 copy-start.5
  8.7 1.3 %collective-permute-start.2 = (bf16[18,512]{1,0:T(8,128)(2,1)S(1)}, bf16[18,512]{1,0:T(8,128)(2,1)S(1)}, u32[]{:S(2)}, u32[]{:S(2)}) collective-permute-start(bf16[18,512]{1,0:T(8,128)(2,1)S(1)} %get-tuple-element.27), channel_id=1, source_target_pairs={{0,4},{4,0},{1,5},{5,1},{2,6},{6,2},{3,7},{7,3},{8,12},{12,8},{9,1... | collective-permute-start | bytes 55304 | tf_op jit(solution)/shard_map/ppermute | solution.py:352
  9.9 0.7 collective-permute-start.3
  10.6 0.8 collective-permute-done.2.pair_hbm
  11.4 0.6 copy-done.2
  12.0 8.0 %decoder_grads.1 = (f32[64,512]{1,0:T(8,128)}, bf16[18,512]{1,0:T(8,128)(2,1)}, bf16[18,512]{1,0:T(8,128)(2,1)}, f32[4,512]{1,0:T(4,128)}, f32[4,512]{1,0:T(4,12...) custom-call(s32[1]{0:T(128)} %bitcast.core_ref, ...), custom_call_target="tpu_custom_call" | custom-call | tf_op jit(solution)/shard_map/decoder_grads/pallas_call | solution.py:242
  20.1 2.0 %collective-permute-start.4 = (bf16[16,352,128]{2,1,0:T(8,128)(2,1)}, bf16[16,352,128]{2,1,0:T(8,128)(2,1)S(1)}, u32[]{:S(2)}, u32[]{:S(2)}) collective-permute-start(bf16[16,352,128]{2,1,0:T(8,128)(2,1)} %get-tuple-element.32), channel_id=1, source_target_pairs={{0,1},{1,0},{2,3},{3,2},{4,5},{5,4},{6,7},{7,6},{8,9},{9,8},{10,11... | collective-permute-start | bytes 4325384 | tf_op jit(solution)/shard_map/ppermute | solution.py:361
  22.0 3.1 %collective-permute-done.4 = bf16[16,352,128]{2,1,0:T(8,128)(2,1)S(1)} collective-permute-done((bf16[16,352,128]{2,1,0:T(8,128)(2,1)}, bf16[16,352,128]{2,1,0:T(8,128)(2,1)S(1)}, u32[]{:S(2)}, u32[]{:S(2)}) %collective-permute-start.4) | collective-permute-done | bytes 1441824 | tf_op jit(solution)/shard_map/ppermute | solution.py:361
  25.1 2.9 %add_convert_fusion = bf16[16,352,128]{2,1,0:T(8,128)(2,1)} fusion(bf16[16,352,128]{2,1,0:T(8,128)(2,1)S(1)} %collective-permute-done.4, bf16[16,352,128]{2,1,0:T(8,128)(2,1)} %get-tuple-element.31), kind=kLoop, calls=%fused_computation | loop fusion | flops 2883584 | bytes 4325376 | tf_op jit(solution)/shard_map/convert_element_type | solution.py:420
  28.0 0.0 copy-start.1
  28.1 11.2 %all-to-all-start = ((bf16[16,352,128]{2,1,0:T(8,128)(2,1)}), bf16[16,352,128]{2,1,0:T(8,128)(2,1)S(1)}, u32[]{:S(2)}, u32[]{:S(2)}) async-start(bf16[16,352,128]{2,1,0:T(8,128)(2,1)} %add_convert_fusion), calls=%async_computation | async-start | bytes 2883584 | tf_op jit(solution)/shard_map/all_to_all | solution.py:422
  39.3 0.0 copy-start
  39.3 1.4 %collective-permute-start.5 = (bf16[18,512]{1,0:T(8,128)(2,1)S(1)}, bf16[18,512]{1,0:T(8,128)(2,1)S(1)}, u32[]{:S(2)}, u32[]{:S(2)}) collective-permute-start(bf16[18,512]{1,0:T(8,128)(2,1)S(1)} %copy-done.9), channel_id=1, source_target_pairs={{0,4},{4,0},{1,5},{5,1},{2,6},{6,2},{3,7},{7,3},{8,12},{12,8},{9,1... | collective-permute-start | bytes 55304 | tf_op jit(solution)/shard_map/ppermute | solution.py:352
  40.7 0.7 collective-permute-start.6
  41.4 0.1 pad.4.clone
  41.5 14.6 %collective-permute-done.5 = bf16[18,512]{1,0:T(8,128)(2,1)S(1)} collective-permute-done((bf16[18,512]{1,0:T(8,128)(2,1)S(1)}, bf16[18,512]{1,0:T(8,128)(2,1)S(1)}, u32[]{:S(2)}, u32[]{:S(2)}) %collective-permute-start.5) | collective-permute-done | bytes 18464 | tf_op jit(solution)/shard_map/ppermute | solution.py:352
  56.2 0.1 pad_maximum_fusion
  56.4 3.8 %collective-permute-start.7 = (bf16[4,512]{1,0:T(4,128)(2,1)S(1)}, bf16[4,512]{1,0:T(4,128)(2,1)S(1)}, u32[]{:S(2)}, u32[]{:S(2)}) collective-permute-start(bf16[4,512]{1,0:T(4,128)(2,1)S(1)} %get-tuple-element.46), channel_id=1, source_target_pairs={{0,3},{1,2},{2,1},{3,0},{4,7},{5,6},{6,5},{7,4},{8,11},{9,10},{10,... | collective-permute-start | bytes 12296 | tf_op jit(solution)/shard_map/ppermute | solution.py:365
  60.1 0.1 pad.1.clone
  60.2 1.2 %collective-permute-done.7 = bf16[4,512]{1,0:T(4,128)(2,1)S(1)} collective-permute-done((bf16[4,512]{1,0:T(4,128)(2,1)S(1)}, bf16[4,512]{1,0:T(4,128)(2,1)S(1)}, u32[]{:S(2)}, u32[]{:S(2)}) %collective-permute-start.7) | collective-permute-done | bytes 4128 | tf_op jit(solution)/shard_map/ppermute | solution.py:365
  61.4 0.1 fusion.3
  61.6 0.8 sum_over_near.1
  62.4 7.5 %all-to-all-start.1 = ((bf16[4,88,128]{2,1,0:T(8,128)(2,1)}), bf16[4,88,128]{2,1,0:T(8,128)(2,1)S(1)}, u32[]{:S(2)}, u32[]{:S(2)}) async-start(bf16[4,88,128]{2,1,0:T(8,128)(2,1)} %sum_over_near.1), calls=%async_computation.1 | async-start | bytes 180224 | tf_op jit(solution)/shard_map/all_to_all | solution.py:423
  69.9 0.9 %fusion = f32[4,16,512]{2,1,0:T(8,128)} fusion(bf16[512,512]{1,0:T(8,128)(2,1)S(1)} %copy-done, bf16[4,16,512]{2,0,1:T(4,128)(2,1)S(1)} %fusion.3), kind=kOutput, calls=%fused_computation.1 | convolution fusion | flops 33554432 | bytes 720896 | tf_op jit(solution)/shard_map/dot_general | solution.py:26
  70.9 6.1 %all-to-all-done.1.in_ref = bf16[4,88,128]{2,1,0:T(8,128)(2,1)S(1)} async-done(((bf16[4,88,128]{2,1,0:T(8,128)(2,1)}), bf16[4,88,128]{2,1,0:T(8,128)(2,1)S(1)}, u32[]{:S(2)}, u32[]{:S(2)}) %all-to-all-start.1) | async-done | bytes 90144 | tf_op jit(solution)/shard_map/all_to_all | solution.py:423
  77.0 9.9 %all-gather = bf16[352,128]{1,0:T(8,128)(2,1)S(1)} all-gather(bf16[88,128]{1,0:T(8,128)(2,1)S(1)} %sum_over_far.1), channel_id=2, replica_groups=mesh['y_lo'=2,'z_hi'=4,'z_lo'=2,'x_hi'=2,'x_lo'=2,'y_hi'=2,'core'=2] {'y..., dimensions={0}, use_global_device_ids=true | all-gather | bytes 112640 | tf_op jit(solution)/shard_map/all_gather | solution.py:425
  86.9 0.6 sum_over_lon.1
  (36 shorter events, 0.2 us)
Async XLA Ops:
  1.5 7.1 %collective-permute-start = (bf16[4,512]{1,0:T(4,128)(2,1)S(1)}, bf16[4,512]{1,0:T(4,128)(2,1)S(1)}, u32[]{:S(2)}, u32[]{:S(2)}) collective-permute-start(bf16[4,512]{1,0:T(4,128)(2,1)S(1)} %get-tuple-element.55), channel_id=1, source_target_pairs={{0,3},{1,2},{2,1},{3,0},{4,7},{5,6},{6,5},{7,4},{8,11},{9,10},{10,... | collective-permute-start | bytes 12296 | tf_op jit(solution)/shard_map/ppermute | solution.py:365
  5.8 2.7 %collective-permute-start.1 = (bf16[4,512]{1,0:T(4,128)(2,1)S(1)}, bf16[4,512]{1,0:T(4,128)(2,1)S(1)}, u32[]{:S(2)}, u32[]{:S(2)}) collective-permute-start(bf16[4,512]{1,0:T(4,128)(2,1)S(1)} %get-tuple-element.56), channel_id=1, source_target_pairs={{0,1},{1,0},{2,3},{3,2},{4,5},{5,4},{6,7},{7,6},{8,9},{9,8},{10,11... | collective-permute-start | bytes 12296 | tf_op jit(solution)/shard_map/ppermute | solution.py:361
  8.6 2.9 %copy-start.4 = (bf16[4,512]{1,0:T(4,128)(2,1)}, bf16[4,512]{1,0:T(4,128)(2,1)S(1)}, u32[]{:S(2)}) copy-start(bf16[4,512]{1,0:T(4,128)(2,1)S(1)} %collective-permute-done.opposite_hbm) | copy-start | bytes 12292
  8.6 2.9 %copy-start.5 = (bf16[4,512]{1,0:T(4,128)(2,1)}, bf16[4,512]{1,0:T(4,128)(2,1)S(1)}, u32[]{:S(2)}) copy-start(bf16[4,512]{1,0:T(4,128)(2,1)S(1)} %collective-permute-done.1.mate_hbm) | copy-start | bytes 12292
  8.7 2.8 %collective-permute-start.2 = (bf16[18,512]{1,0:T(8,128)(2,1)S(1)}, bf16[18,512]{1,0:T(8,128)(2,1)S(1)}, u32[]{:S(2)}, u32[]{:S(2)}) collective-permute-start(bf16[18,512]{1,0:T(8,128)(2,1)S(1)} %get-tuple-element.27), channel_id=1, source_target_pairs={{0,4},{4,0},{1,5},{5,1},{2,6},{6,2},{3,7},{7,3},{8,12},{12,8},{9,1... | collective-permute-start | bytes 55304 | tf_op jit(solution)/shard_map/ppermute | solution.py:352
  9.9 1.5 %collective-permute-start.3 = (bf16[18,512]{1,0:T(8,128)(2,1)S(1)}, bf16[18,512]{1,0:T(8,128)(2,1)S(1)}, u32[]{:S(2)}, u32[]{:S(2)}) collective-permute-start(bf16[18,512]{1,0:T(8,128)(2,1)S(1)} %get-tuple-element.28), channel_id=1, source_target_pairs={{4,8},{12,16},{20,24},{28,32},{36,40},{44,48},{52,56},{60,64},{68,... | collective-permute-start | bytes 55304 | tf_op jit(solution)/shard_map/ppermute | solution.py:357
  11.4 0.6 copy-start.2
  11.4 0.6 copy-start.3
  20.1 5.0 %collective-permute-start.4 = (bf16[16,352,128]{2,1,0:T(8,128)(2,1)}, bf16[16,352,128]{2,1,0:T(8,128)(2,1)S(1)}, u32[]{:S(2)}, u32[]{:S(2)}) collective-permute-start(bf16[16,352,128]{2,1,0:T(8,128)(2,1)} %get-tuple-element.32), channel_id=1, source_target_pairs={{0,1},{1,0},{2,3},{3,2},{4,5},{5,4},{6,7},{7,6},{8,9},{9,8},{10,11... | collective-permute-start | bytes 4325384 | tf_op jit(solution)/shard_map/ppermute | solution.py:361
  28.0 11.2 %copy-start.9 = (bf16[18,512]{1,0:T(8,128)(2,1)S(1)}, bf16[18,512]{1,0:T(8,128)(2,1)}, u32[]{:S(2)}) copy-start(bf16[18,512]{1,0:T(8,128)(2,1)} %get-tuple-element.35) | copy-start | bytes 55300
  28.0 12.7 %copy-start.8 = (bf16[18,512]{1,0:T(8,128)(2,1)S(1)}, bf16[18,512]{1,0:T(8,128)(2,1)}, u32[]{:S(2)}) copy-start(bf16[18,512]{1,0:T(8,128)(2,1)} %get-tuple-element.36) | copy-start | bytes 55300
  28.0 28.3 %copy-start.6 = (f32[4,512]{1,0:T(4,128)S(1)}, f32[4,512]{1,0:T(4,128)}, u32[]{:S(2)}) copy-start(f32[4,512]{1,0:T(4,128)} %get-tuple-element.38) | copy-start | bytes 24580
  28.0 28.3 %copy-start.7 = (f32[4,512]{1,0:T(4,128)S(1)}, f32[4,512]{1,0:T(4,128)}, u32[]{:S(2)}) copy-start(f32[4,512]{1,0:T(4,128)} %get-tuple-element.37) | copy-start | bytes 24580
  28.0 33.4 %copy-start.1 = (f32[64,512]{1,0:T(8,128)S(1)}, f32[64,512]{1,0:T(8,128)}, u32[]{:S(2)}) copy-start(f32[64,512]{1,0:T(8,128)} %get-tuple-element.30) | copy-start | bytes 393220
  28.1 33.5 %all-to-all-start = ((bf16[16,352,128]{2,1,0:T(8,128)(2,1)}), bf16[16,352,128]{2,1,0:T(8,128)(2,1)S(1)}, u32[]{:S(2)}, u32[]{:S(2)}) async-start(bf16[16,352,128]{2,1,0:T(8,128)(2,1)} %add_convert_fusion), calls=%async_computation | async-start | bytes 2883584 | tf_op jit(solution)/shard_map/all_to_all | solution.py:422
  39.3 30.6 %copy-start = (bf16[512,512]{1,0:T(8,128)(2,1)S(1)}, bf16[512,512]{1,0:T(8,128)(2,1)}, u32[]{:S(2)}) copy-start(bf16[512,512]{1,0:T(8,128)(2,1)} %w_em_hbm.1) | copy-start | bytes 1572868
  39.3 16.8 %collective-permute-start.5 = (bf16[18,512]{1,0:T(8,128)(2,1)S(1)}, bf16[18,512]{1,0:T(8,128)(2,1)S(1)}, u32[]{:S(2)}, u32[]{:S(2)}) collective-permute-start(bf16[18,512]{1,0:T(8,128)(2,1)S(1)} %copy-done.9), channel_id=1, source_target_pairs={{0,4},{4,0},{1,5},{5,1},{2,6},{6,2},{3,7},{7,3},{8,12},{12,8},{9,1... | collective-permute-start | bytes 55304 | tf_op jit(solution)/shard_map/ppermute | solution.py:352
  40.7 15.4 %collective-permute-start.6 = (bf16[18,512]{1,0:T(8,128)(2,1)S(1)}, bf16[18,512]{1,0:T(8,128)(2,1)S(1)}, u32[]{:S(2)}, u32[]{:S(2)}) collective-permute-start(bf16[18,512]{1,0:T(8,128)(2,1)S(1)} %copy-done.8), channel_id=1, source_target_pairs={{4,8},{12,16},{20,24},{28,32},{36,40},{44,48},{52,56},{60,64},{68,... | collective-permute-start | bytes 55304 | tf_op jit(solution)/shard_map/ppermute | solution.py:357
  56.4 5.0 %collective-permute-start.7 = (bf16[4,512]{1,0:T(4,128)(2,1)S(1)}, bf16[4,512]{1,0:T(4,128)(2,1)S(1)}, u32[]{:S(2)}, u32[]{:S(2)}) collective-permute-start(bf16[4,512]{1,0:T(4,128)(2,1)S(1)} %get-tuple-element.46), channel_id=1, source_target_pairs={{0,3},{1,2},{2,1},{3,0},{4,7},{5,6},{6,5},{7,4},{8,11},{9,10},{10,... | collective-permute-start | bytes 12296 | tf_op jit(solution)/shard_map/ppermute | solution.py:365
  60.1 1.3 %collective-permute-start.8 = (bf16[4,512]{1,0:T(4,128)(2,1)S(1)}, bf16[4,512]{1,0:T(4,128)(2,1)S(1)}, u32[]{:S(2)}, u32[]{:S(2)}) collective-permute-start(bf16[4,512]{1,0:T(4,128)(2,1)S(1)} %get-tuple-element.45), channel_id=1, source_target_pairs={{0,1},{1,0},{2,3},{3,2},{4,5},{5,4},{6,7},{7,6},{8,9},{9,8},{10,11... | collective-permute-start | bytes 12296 | tf_op jit(solution)/shard_map/ppermute | solution.py:361
  62.4 14.6 %all-to-all-start.1 = ((bf16[4,88,128]{2,1,0:T(8,128)(2,1)}), bf16[4,88,128]{2,1,0:T(8,128)(2,1)S(1)}, u32[]{:S(2)}, u32[]{:S(2)}) async-start(bf16[4,88,128]{2,1,0:T(8,128)(2,1)} %sum_over_near.1), calls=%async_computation.1 | async-start | bytes 180224 | tf_op jit(solution)/shard_map/all_to_all | solution.py:423

commit v5 on v4

--- a/solution.py
+++ b/solution.py
@@ -11,6 +11,7 @@
 LAT = ("y_lo", "z_hi", "z_lo", "x_hi", "x_lo")
 LON = ("y_hi", "core")
 NEAR = ("y_lo", "z_lo", "x_hi", "x_lo")
+FAR = ("z_hi", "y_hi")
 SIZES = {"y_lo": 2, "z_hi": 4, "z_lo": 2, "x_hi": 2, "x_lo": 2, "y_hi": 2, "core": 2}
 F32 = jnp.float32
 BF = jnp.bfloat16
@@ -43,7 +44,9 @@
 
 def main_kernel(
     core_ref,
-    place_ref,
+    odd_ref,
+    live_ref,
+    nbr_hbm,
     pair_hbm,
     other_hbm,
     mate_hbm,
@@ -66,6 +69,7 @@
     grid_hbm,
     send_hbm,
     keep_hbm,
+    nbr_ref,
     pair_ref,
     other_ref,
     mate_ref,
@@ -96,6 +100,7 @@
     wo_ref,
 ):
     ways = (
+        (nbr_hbm, nbr_ref),
         (mesh_hbm, mesh_ref),
         (pair_hbm, pair_ref),
         (other_hbm, other_ref),
@@ -105,19 +110,20 @@
         (g_hbm, g_ref),
         (w_eg_hbm, w_eg_ref),
         (b_edge_hbm, b_edge_ref),
-        (b_node_hbm, b_node_ref),
         (w_e2_hbm, w_e2_ref),
         (w_node_hbm, w_node_ref),
         (cot_hbm, cot_ref),
         (w_out_hbm, w_out_ref),
+        (b_node_hbm, b_node_ref),
     )
     copies = [pltpu.make_async_copy(a, b, sems.at[i]) for i, (a, b) in enumerate(ways)]
-    for copy in copies:
+    for copy in copies[:10]:
         copy.start()
     core = core_ref[0]
+    odd = odd_ref[0]
     points = 256
     ext_ref[64:, :] = jnp.zeros((64, D), F32)
-    for copy in copies[:5]:
+    for copy in copies[:6]:
         copy.wait()
     ext_ref[:64, :] = mesh_ref[...].astype(F32)
     ext_ref[64:82, :] = pair_ref[...].astype(F32)
@@ -126,12 +132,21 @@
     ext_ref[120:124, :] = opposite_ref[...].astype(F32)
     ext = ext_ref[...].astype(BF)
     row = lax.broadcasted_iota(jnp.int32, (128, points), 0)
-    hots = [jnp.where(row == (place_ref[k : k + 1, :] & 1023), 1.0, 0.0).astype(BF) for k in range(3)]
-    copies[5].wait()
+    hots = []
+    for k in range(3):
+        slot = nbr_ref[k]
+        r = (slot * 3641) >> 16
+        c = slot - r * 18
+        side = jnp.where(c == 0, 119 - 8 * core, 111 + 8 * core) + r
+        inner = jnp.where((c == 0) | (c == 17), side, (r - 1) * 16 + c - 1)
+        place = jnp.where(r == 0, 88 - 24 * odd + c, jnp.where(r == 5, 64 + 24 * odd + c, inner))
+        hots.append(jnp.where(row == place, 1.0, 0.0).astype(BF))
+    copies[6].wait()
+    for copy in copies[10:]:
+        copy.start()
     projected = mm(ext, w_em_ref[...])
     high, low = split(projected)
     both = jnp.concatenate([high, low], axis=0)
-    copies[6].wait()
     for copy in copies[7:10]:
         copy.wait()
     g = g_ref[...]
@@ -149,8 +164,9 @@
         copy.wait()
     og_ref[...] = jnp.zeros_like(og_ref)
     wo_ref[...] = jnp.zeros_like(wo_ref)
+    column = lax.broadcasted_iota(jnp.int32, (CH, points), 1)
     cot = cot_ref[...]
-    og_ref[:CH, :] = jnp.where(place_ref[0:1, :] < 1024, cot, jnp.zeros_like(cot))
+    og_ref[:CH, :] = jnp.where(column < live_ref[0], cot, jnp.zeros_like(cot))
     wo_ref[:CH, :] = w_out_ref[...]
     out_grad = og_ref[...].T
     halves(og_half, out_grad)
@@ -198,11 +214,19 @@
 
     ext_both = jnp.concatenate([ext, ext], axis=0)
     out_copies = [grid_copy]
+
+    def leave(ref, out, first, end):
+        rows = slice(first * 32, end * 32)
+        copy = pltpu.make_async_copy(ref.at[:, rows], out.at[:, rows], out_sems.at[len(out_copies)])
+        copy.start()
+        out_copies.append(copy)
+
     for ref, out, which in ((send_ref, send_hbm, 1 - core), (keep_ref, keep_hbm, core)):
         put_wide(ref, 0, mm_tn(ext_both, sl_half[which]))
         put_wide(ref, 2, mm_tn(g, es_half[which]))
         ag = ag_half[which]
         put_wide(ref, 4, mm_tn(hs_high, ag) + mm_tn(hs_low, ag))
+        leave(ref, out, 0, 6)
         ng = ng_half[which]
         for half, left in enumerate((g, aggregate)):
             v = mm_tn(left, ng).reshape(4, 2, 4, 2, 8, 256)
@@ -212,10 +236,9 @@
                     for wide in range(2):
                         at = (6 + 2 * eight + wide) * 32
                         ref[8 * half + i, at : at + 32, :] = tile[:, wide * 128 : wide * 128 + 128]
+        leave(ref, out, 6, 10)
         put(ref, 10, mm_tn(node_hidden, og_half[which]))
-        copy = pltpu.make_async_copy(ref, out, out_sems.at[len(out_copies)])
-        copy.start()
-        out_copies.append(copy)
+        leave(ref, out, 10, 11)
     for copy in out_copies:
         copy.wait()
 
@@ -237,7 +260,7 @@
 
 def main_call(*args):
     shape = jax.ShapeDtypeStruct
-    inputs = args[2:]
+    inputs = args[3:]
     hbm = pl.BlockSpec(memory_space=pltpu.HBM)
     return pl.pallas_call(
         main_kernel,
@@ -251,7 +274,7 @@
             shape((16, ROWS, 128), BF),
             shape((16, ROWS, 128), BF),
         ),
-        in_specs=smem(1) + vmem(1) + [hbm] * len(inputs),
+        in_specs=smem(3) + [hbm] * len(inputs),
         out_specs=tuple(vmem(5) + [hbm] * 3),
         scratch_shapes=[pltpu.VMEM(a.shape, a.dtype) for a in inputs]
         + [
@@ -259,7 +282,7 @@
             pltpu.VMEM((16, ROWS, 128), BF),
             pltpu.VMEM((16, ROWS, 128), BF),
             pltpu.SemaphoreType.DMA((len(inputs),)),
-            pltpu.SemaphoreType.DMA((3,)),
+            pltpu.SemaphoreType.DMA((7,)),
             pltpu.VMEM((128, D), F32),
             pltpu.VMEM((2, 256, 256), BF),
             pltpu.VMEM((2, 256, 128), BF),
@@ -281,13 +304,15 @@
         total = total + in_ref[i].astype(F32)
     total = total.reshape(PANELS, 4, 8, 128)
     for i in range(4):
-        out_ref[i] = total[:, i].reshape(PANELS * 8, 128).astype(BF)
+        chunk = total[:, i].reshape(PANELS * 8, 128).astype(BF)
+        out_ref[2 * i] = chunk
+        out_ref[2 * i + 1] = chunk
 
 
 def near_sum(chunks):
     return pl.pallas_call(
         near_sum_kernel,
-        out_shape=jax.ShapeDtypeStruct((4, PANELS * 8, 128), BF),
+        out_shape=jax.ShapeDtypeStruct((8, PANELS * 8, 128), BF),
         in_specs=vmem(1),
         out_specs=vmem(1)[0],
         compiler_params=params(6),
@@ -312,7 +337,7 @@
 
 def last_kernel(in_ref, em_ref, eg_ref, e2_ref, node_ref, out_ref):
     for core in range(2):
-        total = in_ref[core].astype(F32) + in_ref[core + 2].astype(F32)
+        total = in_ref[core].astype(F32)
 
         def panel(i):
             return total[8 * i : 8 * i + 8, :]
@@ -344,7 +369,7 @@
         in_specs=vmem(1),
         out_specs=tuple(vmem(5)),
         compiler_params=params(4),
-        name="sum_over_lon",
+        name="share_over_core",
     )(gathered)
 
 
@@ -389,18 +414,13 @@
     top = jnp.concatenate([west[:1], mesh_latent[0], east[:1]], axis=0)
     bottom = jnp.concatenate([west[3:], mesh_latent[3], east[3:]], axis=0)
     pair, other = jnp.where(odd == 1, top, bottom), jnp.where(odd == 1, bottom, top)
-    slot = neighbours[0, 0]
-    r, c = slot // 18, slot % 18
-    side = jnp.where(c == 0, 120 - 8 * core, 112 + 8 * core) + r - 1
-    inner = jnp.where((c == 0) | (c == 17), side, (r - 1) * 16 + c - 1)
-    place = jnp.where(r == 0, 88 - 24 * odd + c, jnp.where(r == 5, 64 + 24 * odd + c, inner))
-    place = jnp.where(lax.broadcasted_iota(jnp.int32, (3, 256), 1) < live[0, 0], place, place + 1024)
-    pair, other, place = lax.optimization_barrier((pair, other, place))
     pair = to_pair(pair)
     other = to_other(other)
     slots, pair, other, mate, opposite, grid_grad, send, keep = main_call(
         core.reshape(1),
-        place,
+        odd.reshape(1),
+        live.reshape(1),
+        jnp.swapaxes(neighbours, 1, 2).reshape(3, 1, 256),
         pair,
         other,
         mate,
@@ -420,11 +440,6 @@
     chunks = (keep.astype(F32) + got.astype(F32)).astype(BF)
     chunks, pair, other = lax.optimization_barrier((chunks, pair, other))
     chunks = lax.all_to_all(chunks, NEAR, 0, 0, tiled=True)
-    chunks = lax.all_to_all(near_sum(chunks), "z_hi", 0, 0, tiled=True)
-    part = far_sum(chunks)
-    gathered = lax.all_gather(part, LON, axis=0, tiled=False)
-    grads = last(gathered)
-
     pair = to_pair(pair).astype(F32)
     other = to_other(other).astype(F32)
     top = jnp.where(odd == 1, pair, other)
@@ -432,8 +447,12 @@
     ends = jnp.stack([top, jnp.zeros_like(top), jnp.zeros_like(top), bottom])
     mate = mate + jnp.where(core == 0, ends[:, 17], ends[:, 0])
     opposite = opposite + jnp.where(core == 0, ends[:, 0], ends[:, 17])
-    mate = to_mate(mate.astype(BF)).astype(F32)
-    opposite = to_opposite(opposite.astype(BF)).astype(F32)
+    mate, opposite = mate.astype(BF), opposite.astype(BF)
+    chunks, mate, opposite = lax.optimization_barrier((near_sum(chunks), mate, opposite))
+    chunks = lax.all_to_all(chunks, FAR, 0, 0, tiled=True)
+    grads = last(lax.all_gather(far_sum(chunks), "core", axis=0, tiled=False))
+    mate = to_mate(mate).astype(F32)
+    opposite = to_opposite(opposite).astype(F32)
     west = jnp.where(core == 0, opposite, mate)
     east = jnp.where(core == 0, mate, opposite)
     sides = jnp.concatenate([west[:, None], jnp.zeros((4, 14, D), F32), east[:, None]], axis=1)

time: 88.2 us -> 84.6 us (0.959)
  blocking collectives: 9.91 us -> 3.59 us
  waiting for transfers between devices: 25.8 us -> 29.7 us
  other arithmetic: 4.53 us -> 3.22 us
    all_gather x1, blocking collectives: 9.91 us -> 3.59 us  [on_device(): grads = last(lax.all_gather(far_sum(chunks), 'core', axis=0, tiled=False))]
    all_to_all x1, waiting for transfers between devices: 0.01 us -> 3.12 us  [on_device(): chunks = lax.all_to_all(chunks, NEAR, 0, 0, tiled=True)]
    all_to_all x1, waiting for transfers between devices: 6.08 us -> 8.26 us  [on_device(): chunks = lax.all_to_all(chunks, FAR, 0, 0, tiled=True)]
    all_to_all x1, starting transfers between devices: 11.2 us -> 9.71 us  [on_device(): chunks = lax.all_to_all(chunks, NEAR, 0, 0, tiled=True)]
    ppermute x3, starting transfers between devices: 1.99 us -> 3.42 us  [to_mate(): return lax.ppermute(value, 'core', [(0, 1), (1, 0)])]
    select_n x1 -> x0, other arithmetic: 1.3 us -> none  [on_device(): jnp.where(lax.broadcasted_iota(jnp.int32, (3, 256), 1) < live[0, 0], plac...]
    ppermute x2, starting transfers between devices: 8.15 us -> 9.03 us  [to_opposite(): return lax.ppermute(value, LON, [(i, 3 - i) for i in range(4)])]
  transfers between devices with their start and end apart: 11 -> 11, of which waited for: 5 -> 6; matrix products, arithmetic and copies ran while one was open for 4% -> 3% of each run, Pallas kernels for 0% -> 0%
where the time goes in v5:
time: 84.6 us; the launch traced here: 84.1 us
  starting transfers between devices  33.6 us (40%)
  waiting for transfers between devices  29.7 us (35%)
  Pallas kernels  9.07 us (11%)
  blocking collectives  3.59 us (4%)
  other arithmetic  3.22 us (4%)
  local copies, waits for them, and re-layouts  2.39 us (3%)
  between operations  1.5 us (2%)
  matrix products  0.94 us (1%)
    ppermute x2, waiting for transfers between devices, to_pair(): return lax.ppermute(value, 'x_lo', [(0, 1), (1, 0)])  14.7 us
    all_to_all x1, starting transfers between devices, on_device(): chunks = lax.all_to_all(chunks, NEAR, 0, 0, tiled=True)  9.71 us
    ppermute x2, starting transfers between devices, to_opposite(): return lax.ppermute(value, LON, [(i, 3 - i) for i in range(4)])  9.03 us
    all_to_all x1, waiting for transfers between devices, on_device(): chunks = lax.all_to_all(chunks, FAR, 0, 0, tiled=True)  8.26 us
    pallas_call x1, Pallas kernels, main_call(): pl.pallas_call(main_kernel, out_shape=(shape((64, D), F32), shape((18, D)...  7.54 us
    all_to_all x1, starting transfers between devices, on_device(): chunks = lax.all_to_all(chunks, FAR, 0, 0, tiled=True)  7.34 us
    all_gather x1, blocking collectives, on_device(): grads = last(lax.all_gather(far_sum(chunks), 'core', axis=0, tiled=False))  3.59 us
    ppermute x3, starting transfers between devices, to_mate(): return lax.ppermute(value, 'core', [(0, 1), (1, 0)])  3.42 us
  transfers between devices with their start and end apart: 11, of which 6 were waited for; matrix products, arithmetic and copies ran while one was open for 3% of the time, Pallas kernels for 0%

profile of v5, /device:TPU:1, one launch (start us, length us, event | category | flops | bytes accessed | tf_op | source)
XLA Modules:
  0.0 84.1 jit_solution(5831780885887928944)
XLA Ops:
  0.6 0.8 fusion.10
  1.5 4.4 %collective-permute-start = (bf16[4,512]{1,0:T(4,128)(2,1)S(1)}, bf16[4,512]{1,0:T(4,128)(2,1)S(1)}, u32[]{:S(2)}, u32[]{:S(2)}) collective-permute-start(bf16[4,512]{1,0:T(4,128)(2,1)S(1)} %get-tuple-element.55), channel_id=1, source_target_pairs={{0,3},{1,2},{2,1},{3,0},{4,7},{5,6},{6,5},{7,4},{8,11},{9,10},{10,... | collective-permute-start | bytes 12296 | tf_op jit(solution)/shard_map/ppermute | solution.py:390
  5.9 0.7 slice_bitcast_fusion.1
  6.6 0.6 collective-permute-done.opposite_hbm
  7.2 1.3 %collective-permute-start.2 = (bf16[18,512]{1,0:T(8,128)(2,1)S(1)}, bf16[18,512]{1,0:T(8,128)(2,1)S(1)}, u32[]{:S(2)}, u32[]{:S(2)}) collective-permute-start(bf16[18,512]{1,0:T(8,128)(2,1)S(1)} %get-tuple-element.54), channel_id=1, source_target_pairs={{0,4},{4,0},{1,5},{5,1},{2,6},{6,2},{3,7},{7,3},{8,12},{12,8},{9,1... | collective-permute-start | bytes 55304 | tf_op jit(solution)/shard_map/ppermute | solution.py:377
  8.6 0.7 collective-permute-start.3
  9.9 0.1 collective-permute-done.2.pair_hbm
  10.0 0.6 copy-done.2
  10.6 7.5 %decoder_grads.1 = (f32[64,512]{1,0:T(8,128)}, bf16[18,512]{1,0:T(8,128)(2,1)}, bf16[18,512]{1,0:T(8,128)(2,1)}, f32[4,512]{1,0:T(4,128)}, f32[4,512]{1,0:T(4,12...) custom-call(s32[1]{0:T(128)} %bitcast.core_ref, s32[1]{0:T(128)} %bitcast.1.odd_ref, ...), custom_call_target="tpu_custom_call" | custom-call | tf_op jit(solution)/shard_map/decoder_grads/pallas_call | solution.py:265
  18.1 3.4 %collective-permute-start.4 = (bf16[16,352,128]{2,1,0:T(8,128)(2,1)}, bf16[16,352,128]{2,1,0:T(8,128)(2,1)S(1)}, u32[]{:S(2)}, u32[]{:S(2)}) collective-permute-start(bf16[16,352,128]{2,1,0:T(8,128)(2,1)} %get-tuple-element.29), channel_id=1, source_target_pairs={{0,1},{1,0},{2,3},{3,2},{4,5},{5,4},{6,7},{7,6},{8,9},{9,8},{10,11... | collective-permute-start | bytes 4325384 | tf_op jit(solution)/shard_map/ppermute | solution.py:386
  21.6 3.1 %collective-permute-done.4 = bf16[16,352,128]{2,1,0:T(8,128)(2,1)S(1)} collective-permute-done((bf16[16,352,128]{2,1,0:T(8,128)(2,1)}, bf16[16,352,128]{2,1,0:T(8,128)(2,1)S(1)}, u32[]{:S(2)}, u32[]{:S(2)}) %collective-permute-start.4) | collective-permute-done | bytes 1441824 | tf_op jit(solution)/shard_map/ppermute | solution.py:386
  24.6 2.9 %add_convert_fusion = bf16[16,352,128]{2,1,0:T(8,128)(2,1)} fusion(bf16[16,352,128]{2,1,0:T(8,128)(2,1)S(1)} %collective-permute-done.4, bf16[16,352,128]{2,1,0:T(8,128)(2,1)} %get-tuple-element.28), kind=kLoop, calls=%fused_computation | loop fusion | flops 2883584 | bytes 4325376 | tf_op jit(solution)/shard_map/convert_element_type | solution.py:440
  27.6 9.7 %all-to-all-start = ((bf16[16,352,128]{2,1,0:T(8,128)(2,1)}), bf16[16,352,128]{2,1,0:T(8,128)(2,1)S(1)}, u32[]{:S(2)}, u32[]{:S(2)}) async-start(bf16[16,352,128]{2,1,0:T(8,128)(2,1)} %add_convert_fusion), calls=%async_computation | async-start | bytes 2883584 | tf_op jit(solution)/shard_map/all_to_all | solution.py:442
  37.3 0.0 copy-start.1
  37.3 1.4 %collective-permute-start.5 = (bf16[18,512]{1,0:T(8,128)(2,1)S(1)}, bf16[18,512]{1,0:T(8,128)(2,1)S(1)}, u32[]{:S(2)}, u32[]{:S(2)}) collective-permute-start(bf16[18,512]{1,0:T(8,128)(2,1)S(1)} %copy-done.9), channel_id=1, source_target_pairs={{0,4},{4,0},{1,5},{5,1},{2,6},{6,2},{3,7},{7,3},{8,12},{12,8},{9,1... | collective-permute-start | bytes 55304 | tf_op jit(solution)/shard_map/ppermute | solution.py:377
  38.7 0.7 collective-permute-start.6
  39.4 0.1 pad.4.clone
  39.5 14.6 %collective-permute-done.5 = bf16[18,512]{1,0:T(8,128)(2,1)S(1)} collective-permute-done((bf16[18,512]{1,0:T(8,128)(2,1)S(1)}, bf16[18,512]{1,0:T(8,128)(2,1)S(1)}, u32[]{:S(2)}, u32[]{:S(2)}) %collective-permute-start.5) | collective-permute-done | bytes 18464 | tf_op jit(solution)/shard_map/ppermute | solution.py:377
  54.1 0.0 collective-permute-done.6
  54.1 0.0 copy-start
  54.2 0.1 pad_maximum_fusion
  54.4 3.1 %all-to-all-done.in_ref = bf16[16,352,128]{2,1,0:T(8,128)(2,1)S(1)} async-done(((bf16[16,352,128]{2,1,0:T(8,128)(2,1)}), bf16[16,352,128]{2,1,0:T(8,128)(2,1)S(1)}, u32[]{:S(2)}, u32[]{:S(2)}) %all-to-all-start) | async-done | bytes 1441824 | tf_op jit(solution)/shard_map/all_to_all | solution.py:442
  57.5 0.9 %sum_over_near.1 = bf16[8,88,128]{2,1,0:T(8,128)(2,1)} custom-call(bf16[16,352,128]{2,1,0:T(8,128)(2,1)S(1)} %all-to-all-done.in_ref), custom_call_target="tpu_custom_call" | custom-call | tf_op jit(solution)/shard_map/sum_over_near/pallas_call | solution.py:313
  58.4 4.6 %collective-permute-start.7 = (bf16[4,512]{1,0:T(4,128)(2,1)S(1)}, bf16[4,512]{1,0:T(4,128)(2,1)S(1)}, u32[]{:S(2)}, u32[]{:S(2)}) collective-permute-start(bf16[4,512]{1,0:T(4,128)(2,1)S(1)} %get-tuple-element.37), channel_id=1, source_target_pairs={{0,3},{1,2},{2,1},{3,0},{4,7},{5,6},{6,5},{7,4},{8,11},{9,10},{10,... | collective-permute-start | bytes 12296 | tf_op jit(solution)/shard_map/ppermute | solution.py:390
  63.0 0.1 pad.1.clone
  63.1 7.3 %all-to-all-start.1 = ((bf16[8,88,128]{2,1,0:T(8,128)(2,1)}), bf16[8,88,128]{2,1,0:T(8,128)(2,1)S(1)}, u32[]{:S(2)}, u32[]{:S(2)}) async-start(bf16[8,88,128]{2,1,0:T(8,128)(2,1)} %sum_over_near.1), calls=%async_computation.1 | async-start | bytes 360448 | tf_op jit(solution)/shard_map/all_to_all | solution.py:452
  70.4 0.0 collective-permute-done.7
  70.5 0.1 fusion.3
  70.6 0.9 %fusion = f32[4,16,512]{2,1,0:T(8,128)} fusion(bf16[512,512]{1,0:T(8,128)(2,1)S(1)} %copy-done, bf16[4,16,512]{2,0,1:T(4,128)(2,1)S(1)} %fusion.3), kind=kOutput, calls=%fused_computation.1 | convolution fusion | flops 33554432 | bytes 720896 | tf_op jit(solution)/shard_map/dot_general | solution.py:27
  71.5 8.3 %all-to-all-done.1.in_ref = bf16[8,88,128]{2,1,0:T(8,128)(2,1)S(1)} async-done(((bf16[8,88,128]{2,1,0:T(8,128)(2,1)}), bf16[8,88,128]{2,1,0:T(8,128)(2,1)S(1)}, u32[]{:S(2)}, u32[]{:S(2)}) %all-to-all-start.1) | async-done | bytes 180256 | tf_op jit(solution)/shard_map/all_to_all | solution.py:452
  79.8 3.6 %all-gather = bf16[176,128]{1,0:T(8,128)(2,1)S(1)} all-gather(bf16[88,128]{1,0:T(8,128)(2,1)S(1)} %sum_over_far.1), channel_id=2, replica_groups=mesh['y_lo'=2,'z_hi'=4,'z_lo'=2,'x_hi'=2,'x_lo'=2,'y_hi'=2,'core'=2] {'c..., dimensions={0}, use_global_device_ids=true | all-gather | bytes 67584 | tf_op jit(solution)/shard_map/all_gather | solution.py:453
  83.4 0.6 share_over_core.1
  (34 shorter events, 0.2 us)
Async XLA Ops:
  1.5 5.7 %collective-permute-start = (bf16[4,512]{1,0:T(4,128)(2,1)S(1)}, bf16[4,512]{1,0:T(4,128)(2,1)S(1)}, u32[]{:S(2)}, u32[]{:S(2)}) collective-permute-start(bf16[4,512]{1,0:T(4,128)(2,1)S(1)} %get-tuple-element.55), channel_id=1, source_target_pairs={{0,3},{1,2},{2,1},{3,0},{4,7},{5,6},{6,5},{7,4},{8,11},{9,10},{10,... | collective-permute-start | bytes 12296 | tf_op jit(solution)/shard_map/ppermute | solution.py:390
  5.8 1.3 %collective-permute-start.1 = (bf16[4,512]{1,0:T(4,128)(2,1)S(1)}, bf16[4,512]{1,0:T(4,128)(2,1)S(1)}, u32[]{:S(2)}, u32[]{:S(2)}) collective-permute-start(bf16[4,512]{1,0:T(4,128)(2,1)S(1)} %get-tuple-element.56), channel_id=1, source_target_pairs={{0,1},{1,0},{2,3},{3,2},{4,5},{5,4},{6,7},{7,6},{8,9},{9,8},{10,11... | collective-permute-start | bytes 12296 | tf_op jit(solution)/shard_map/ppermute | solution.py:386
  7.1 2.9 %copy-start.4 = (bf16[4,512]{1,0:T(4,128)(2,1)}, bf16[4,512]{1,0:T(4,128)(2,1)S(1)}, u32[]{:S(2)}) copy-start(bf16[4,512]{1,0:T(4,128)(2,1)S(1)} %collective-permute-done.opposite_hbm) | copy-start | bytes 12292
  7.1 2.9 %copy-start.5 = (bf16[4,512]{1,0:T(4,128)(2,1)}, bf16[4,512]{1,0:T(4,128)(2,1)S(1)}, u32[]{:S(2)}) copy-start(bf16[4,512]{1,0:T(4,128)(2,1)S(1)} %collective-permute-done.1.mate_hbm) | copy-start | bytes 12292
  7.2 2.8 %collective-permute-start.2 = (bf16[18,512]{1,0:T(8,128)(2,1)S(1)}, bf16[18,512]{1,0:T(8,128)(2,1)S(1)}, u32[]{:S(2)}, u32[]{:S(2)}) collective-permute-start(bf16[18,512]{1,0:T(8,128)(2,1)S(1)} %get-tuple-element.54), channel_id=1, source_target_pairs={{0,4},{4,0},{1,5},{5,1},{2,6},{6,2},{3,7},{7,3},{8,12},{12,8},{9,1... | collective-permute-start | bytes 55304 | tf_op jit(solution)/shard_map/ppermute | solution.py:377
  8.6 1.4 %collective-permute-start.3 = (bf16[18,512]{1,0:T(8,128)(2,1)S(1)}, bf16[18,512]{1,0:T(8,128)(2,1)S(1)}, u32[]{:S(2)}, u32[]{:S(2)}) collective-permute-start(bf16[18,512]{1,0:T(8,128)(2,1)S(1)} %get-tuple-element.53), channel_id=1, source_target_pairs={{4,8},{12,16},{20,24},{28,32},{36,40},{44,48},{52,56},{60,64},{68,... | collective-permute-start | bytes 55304 | tf_op jit(solution)/shard_map/ppermute | solution.py:382
  10.0 0.6 copy-start.2
  10.0 0.6 copy-start.3
  18.1 6.5 %collective-permute-start.4 = (bf16[16,352,128]{2,1,0:T(8,128)(2,1)}, bf16[16,352,128]{2,1,0:T(8,128)(2,1)S(1)}, u32[]{:S(2)}, u32[]{:S(2)}) collective-permute-start(bf16[16,352,128]{2,1,0:T(8,128)(2,1)} %get-tuple-element.29), channel_id=1, source_target_pairs={{0,1},{1,0},{2,3},{3,2},{4,5},{5,4},{6,7},{7,6},{8,9},{9,8},{10,11... | collective-permute-start | bytes 4325384 | tf_op jit(solution)/shard_map/ppermute | solution.py:386
  27.5 9.7 %copy-start.9 = (bf16[18,512]{1,0:T(8,128)(2,1)S(1)}, bf16[18,512]{1,0:T(8,128)(2,1)}, u32[]{:S(2)}) copy-start(bf16[18,512]{1,0:T(8,128)(2,1)} %get-tuple-element.32) | copy-start | bytes 55300
  27.5 11.2 %copy-start.8 = (bf16[18,512]{1,0:T(8,128)(2,1)S(1)}, bf16[18,512]{1,0:T(8,128)(2,1)}, u32[]{:S(2)}) copy-start(bf16[18,512]{1,0:T(8,128)(2,1)} %get-tuple-element.33) | copy-start | bytes 55300
  27.5 26.8 %copy-start.6 = (f32[4,512]{1,0:T(4,128)S(1)}, f32[4,512]{1,0:T(4,128)}, u32[]{:S(2)}) copy-start(f32[4,512]{1,0:T(4,128)} %get-tuple-element.35) | copy-start | bytes 24580
  27.5 26.8 %copy-start.7 = (f32[4,512]{1,0:T(4,128)S(1)}, f32[4,512]{1,0:T(4,128)}, u32[]{:S(2)}) copy-start(f32[4,512]{1,0:T(4,128)} %get-tuple-element.36) | copy-start | bytes 24580
  27.6 29.9 %all-to-all-start = ((bf16[16,352,128]{2,1,0:T(8,128)(2,1)}), bf16[16,352,128]{2,1,0:T(8,128)(2,1)S(1)}, u32[]{:S(2)}, u32[]{:S(2)}) async-start(bf16[16,352,128]{2,1,0:T(8,128)(2,1)} %add_convert_fusion), calls=%async_computation | async-start | bytes 2883584 | tf_op jit(solution)/shard_map/all_to_all | solution.py:442
  37.3 33.2 %copy-start.1 = (f32[64,512]{1,0:T(8,128)S(1)}, f32[64,512]{1,0:T(8,128)}, u32[]{:S(2)}) copy-start(f32[64,512]{1,0:T(8,128)} %get-tuple-element.27) | copy-start | bytes 393220
  37.3 16.8 %collective-permute-start.5 = (bf16[18,512]{1,0:T(8,128)(2,1)S(1)}, bf16[18,512]{1,0:T(8,128)(2,1)S(1)}, u32[]{:S(2)}, u32[]{:S(2)}) collective-permute-start(bf16[18,512]{1,0:T(8,128)(2,1)S(1)} %copy-done.9), channel_id=1, source_target_pairs={{0,4},{4,0},{1,5},{5,1},{2,6},{6,2},{3,7},{7,3},{8,12},{12,8},{9,1... | collective-permute-start | bytes 55304 | tf_op jit(solution)/shard_map/ppermute | solution.py:377
  38.7 15.4 %collective-permute-start.6 = (bf16[18,512]{1,0:T(8,128)(2,1)S(1)}, bf16[18,512]{1,0:T(8,128)(2,1)S(1)}, u32[]{:S(2)}, u32[]{:S(2)}) collective-permute-start(bf16[18,512]{1,0:T(8,128)(2,1)S(1)} %copy-done.8), channel_id=1, source_target_pairs={{4,8},{12,16},{20,24},{28,32},{36,40},{44,48},{52,56},{60,64},{68,... | collective-permute-start | bytes 55304 | tf_op jit(solution)/shard_map/ppermute | solution.py:382
  54.1 16.5 %copy-start = (bf16[512,512]{1,0:T(8,128)(2,1)S(1)}, bf16[512,512]{1,0:T(8,128)(2,1)}, u32[]{:S(2)}) copy-start(bf16[512,512]{1,0:T(8,128)(2,1)} %w_em_hbm.1) | copy-start | bytes 1572868
  58.4 12.1 %collective-permute-start.7 = (bf16[4,512]{1,0:T(4,128)(2,1)S(1)}, bf16[4,512]{1,0:T(4,128)(2,1)S(1)}, u32[]{:S(2)}, u32[]{:S(2)}) collective-permute-start(bf16[4,512]{1,0:T(4,128)(2,1)S(1)} %get-tuple-element.37), channel_id=1, source_target_pairs={{0,3},{1,2},{2,1},{3,0},{4,7},{5,6},{6,5},{7,4},{8,11},{9,10},{10,... | collective-permute-start | bytes 12296 | tf_op jit(solution)/shard_map/ppermute | solution.py:390
  63.0 7.4 %collective-permute-start.8 = (bf16[4,512]{1,0:T(4,128)(2,1)S(1)}, bf16[4,512]{1,0:T(4,128)(2,1)S(1)}, u32[]{:S(2)}, u32[]{:S(2)}) collective-permute-start(bf16[4,512]{1,0:T(4,128)(2,1)S(1)} %get-tuple-element.38), channel_id=1, source_target_pairs={{0,1},{1,0},{2,3},{3,2},{4,5},{5,4},{6,7},{7,6},{8,9},{9,8},{10,11... | collective-permute-start | bytes 12296 | tf_op jit(solution)/shard_map/ppermute | solution.py:386
  63.1 16.7 %all-to-all-start.1 = ((bf16[8,88,128]{2,1,0:T(8,128)(2,1)}), bf16[8,88,128]{2,1,0:T(8,128)(2,1)S(1)}, u32[]{:S(2)}, u32[]{:S(2)}) async-start(bf16[8,88,128]{2,1,0:T(8,128)(2,1)} %sum_over_near.1), calls=%async_computation.1 | async-start | bytes 360448 | tf_op jit(solution)/shard_map/all_to_all | solution.py:452

commit v6 on v5

--- a/solution.py
+++ b/solution.py
@@ -191,10 +191,15 @@
     edge_sum = edge_sum.astype(BF)
     halves(es_half, edge_sum)
     slot_ref[...] = slots[:64]
-    pair_out[...] = slots[64:82].astype(BF)
-    other_out[...] = slots[88:106].astype(BF)
-    mate_out[...] = slots[112:116]
-    opposite_out[...] = slots[120:124]
+    pair_out[...] = slots[65:81]
+    other_out[...] = slots[89:105]
+    at_mate = [slots[112:116]]
+    at_opposite = [slots[120:124]]
+    for west_end, east_end in ((slots[64:65], slots[81:82]), (slots[88:89], slots[105:106])):
+        at_mate.append(jnp.where(core == 0, east_end, west_end))
+        at_opposite.append(jnp.where(core == 0, west_end, east_end))
+    mate_out[...] = jnp.concatenate(at_mate, axis=0).astype(BF)
+    opposite_out[...] = jnp.concatenate(at_opposite, axis=0).astype(BF)
     sl_high, sl_low = split(slots)
     halves(sl_half, jnp.concatenate([sl_high, sl_low], axis=0))
     grid_ref[...] = mm_nt(node_grad, w_node_ref[:D, :]) + mm_nt(edge_sum, w_eg_ref[...])
@@ -266,10 +271,10 @@
         main_kernel,
         out_shape=(
             shape((64, D), F32),
-            shape((18, D), BF),
-            shape((18, D), BF),
-            shape((4, D), F32),
-            shape((4, D), F32),
+            shape((16, D), F32),
+            shape((16, D), F32),
+            shape((6, D), BF),
+            shape((6, D), BF),
             shape((256, D), F32),
             shape((16, ROWS, 128), BF),
             shape((16, ROWS, 128), BF),
@@ -438,25 +443,22 @@
     )
     got = to_mate(send)
     chunks = (keep.astype(F32) + got.astype(F32)).astype(BF)
-    chunks, pair, other = lax.optimization_barrier((chunks, pair, other))
+    chunks, mate, opposite = lax.optimization_barrier((chunks, mate, opposite))
     chunks = lax.all_to_all(chunks, NEAR, 0, 0, tiled=True)
-    pair = to_pair(pair).astype(F32)
-    other = to_other(other).astype(F32)
-    top = jnp.where(odd == 1, pair, other)
-    bottom = jnp.where(odd == 1, other, pair)
-    ends = jnp.stack([top, jnp.zeros_like(top), jnp.zeros_like(top), bottom])
-    mate = mate + jnp.where(core == 0, ends[:, 17], ends[:, 0])
-    opposite = opposite + jnp.where(core == 0, ends[:, 0], ends[:, 17])
-    mate, opposite = mate.astype(BF), opposite.astype(BF)
-    chunks, mate, opposite = lax.optimization_barrier((near_sum(chunks), mate, opposite))
-    chunks = lax.all_to_all(chunks, FAR, 0, 0, tiled=True)
+    chunks = lax.all_to_all(near_sum(chunks), FAR, 0, 0, tiled=True)
     grads = last(lax.all_gather(far_sum(chunks), "core", axis=0, tiled=False))
+
     mate = to_mate(mate).astype(F32)
     opposite = to_opposite(opposite).astype(F32)
     west = jnp.where(core == 0, opposite, mate)
     east = jnp.where(core == 0, mate, opposite)
-    sides = jnp.concatenate([west[:, None], jnp.zeros((4, 14, D), F32), east[:, None]], axis=1)
-    owned = slots.reshape(4, 16, D) + ends[:, 1:17] + sides
+    sides = jnp.concatenate([west[:, None], jnp.zeros((6, 14, D), F32), east[:, None]], axis=1)
+    pair = to_pair((pair + sides[4]).astype(BF)).astype(F32)
+    other = to_other((other + sides[5]).astype(BF)).astype(F32)
+    top = jnp.where(odd == 1, pair, other)
+    bottom = jnp.where(odd == 1, other, pair)
+    ends = jnp.stack([top, jnp.zeros_like(top), jnp.zeros_like(top), bottom])
+    owned = slots.reshape(4, 16, D) + ends + sides[:4]
     node_sum = owned.reshape(64, D).astype(BF)
     mesh_grad = mm_nt(node_sum, w_em).reshape(4, 16, D)
     return (grid_grad.reshape(1, 1, 256, D), mesh_grad) + tuple(grads)

time: 84.6 us -> 83.8 us (level)
  waiting for transfers between devices: 29.7 us -> 26 us
  starting transfers between devices: 33.6 us -> 35.9 us
    ppermute x2, waiting for transfers between devices: 14.7 us -> 0.11 us  [to_pair(): return lax.ppermute(value, 'x_lo', [(0, 1), (1, 0)])]
    ppermute x2, waiting for transfers between devices: 0.55 us -> 14.6 us  [to_opposite(): return lax.ppermute(value, LON, [(i, 3 - i) for i in range(4)])]
    all_to_all x1, starting transfers between devices: 7.34 us -> 10.7 us  [on_device(): chunks = lax.all_to_all(near_sum(chunks), FAR, 0, 0, tiled=True)]
    all_to_all x1, waiting for transfers between devices: 3.12 us -> 0.01 us  [on_device(): chunks = lax.all_to_all(chunks, NEAR, 0, 0, tiled=True)]
    ppermute x2, starting transfers between devices: 9.03 us -> 7.96 us  [to_opposite(): return lax.ppermute(value, LON, [(i, 3 - i) for i in range(4)])]
  transfers between devices with their start and end apart: 11 -> 11, of which waited for: 6 -> 5; matrix products, arithmetic and copies ran while one was open for 3% -> 2% of each run, Pallas kernels for 0% -> 1%
where the time goes in v6:
time: 83.8 us; the launch traced here: 83 us
  starting transfers between devices  35.9 us (43%)
  waiting for transfers between devices  26 us (31%)
  Pallas kernels  9.07 us (11%)
  blocking collectives  4.11 us (5%)
  other arithmetic  3.09 us (4%)
  local copies, waits for them, and re-layouts  2.36 us (3%)
  between operations  1.5 us (2%)
  matrix products  0.95 us (1%)
    ppermute x2, waiting for transfers between devices, to_opposite(): return lax.ppermute(value, LON, [(i, 3 - i) for i in range(4)])  14.6 us
    all_to_all x1, starting transfers between devices, on_device(): chunks = lax.all_to_all(near_sum(chunks), FAR, 0, 0, tiled=True)  10.7 us
    all_to_all x1, starting transfers between devices, on_device(): chunks = lax.all_to_all(chunks, NEAR, 0, 0, tiled=True)  9.7 us
    all_to_all x1, waiting for transfers between devices, on_device(): chunks = lax.all_to_all(near_sum(chunks), FAR, 0, 0, tiled=True)  8.29 us
    ppermute x2, starting transfers between devices, to_opposite(): return lax.ppermute(value, LON, [(i, 3 - i) for i in range(4)])  7.96 us
    pallas_call x1, Pallas kernels, main_call(): pl.pallas_call(main_kernel, out_shape=(shape((64, D), F32), shape((16, D)...  7.54 us
    all_gather x1, blocking collectives, on_device(): grads = last(lax.all_gather(far_sum(chunks), 'core', axis=0, tiled=False))  4.11 us
    ppermute x3, starting transfers between devices, to_mate(): return lax.ppermute(value, 'core', [(0, 1), (1, 0)])  3.43 us
  transfers between devices with their start and end apart: 11, of which 5 were waited for; matrix products, arithmetic and copies ran while one was open for 2% of the time, Pallas kernels for 1%

profile of v6, /device:TPU:1, one launch (start us, length us, event | category | flops | bytes accessed | tf_op | source)
XLA Modules:
  0.0 83.0 jit_solution(11924401825097897605)
XLA Ops:
  0.6 0.8 fusion.14
  1.5 4.4 %collective-permute-start = (bf16[4,512]{1,0:T(4,128)(2,1)S(1)}, bf16[4,512]{1,0:T(4,128)(2,1)S(1)}, u32[]{:S(2)}, u32[]{:S(2)}) collective-permute-start(bf16[4,512]{1,0:T(4,128)(2,1)S(1)} %get-tuple-element.51), channel_id=1, source_target_pairs={{0,3},{1,2},{2,1},{3,0},{4,7},{5,6},{6,5},{7,4},{8,11},{9,10},{10,... | collective-permute-start | bytes 12296 | tf_op jit(solution)/shard_map/ppermute | solution.py:395
  5.9 0.7 slice_bitcast_fusion.3
  6.6 0.6 collective-permute-done.opposite_hbm
  7.1 0.0 collective-permute-done.1.mate_hbm
  7.2 1.3 %collective-permute-start.2 = (bf16[18,512]{1,0:T(8,128)(2,1)S(1)}, bf16[18,512]{1,0:T(8,128)(2,1)S(1)}, u32[]{:S(2)}, u32[]{:S(2)}) collective-permute-start(bf16[18,512]{1,0:T(8,128)(2,1)S(1)} %get-tuple-element.46), channel_id=1, source_target_pairs={{0,4},{4,0},{1,5},{5,1},{2,6},{6,2},{3,7},{7,3},{8,12},{12,8},{9,1... | collective-permute-start | bytes 55304 | tf_op jit(solution)/shard_map/ppermute | solution.py:382
  8.6 0.7 collective-permute-start.3
  9.9 0.1 collective-permute-done.2.pair_hbm
  10.0 0.6 copy-done.4
  10.6 0.0 copy-done.5
  10.6 7.5 %decoder_grads.1 = (f32[64,512]{1,0:T(8,128)}, f32[16,512]{1,0:T(8,128)}, f32[16,512]{1,0:T(8,128)}, bf16[6,512]{1,0:T(8,128)(2,1)}, bf16[6,512]{1,0:T(8,128)(2,...) custom-call(s32[1]{0:T(128)} %bitcast.core_ref, s32[1]{0:T(128)} %bitcast.1.odd_ref, ...), custom_call_target="tpu_custom_call" | custom-call | tf_op jit(solution)/shard_map/decoder_grads/pallas_call | solution.py:270
  18.1 3.4 %collective-permute-start.4 = (bf16[16,352,128]{2,1,0:T(8,128)(2,1)}, bf16[16,352,128]{2,1,0:T(8,128)(2,1)S(1)}, u32[]{:S(2)}, u32[]{:S(2)}) collective-permute-start(bf16[16,352,128]{2,1,0:T(8,128)(2,1)} %get-tuple-element.27), channel_id=1, source_target_pairs={{0,1},{1,0},{2,3},{3,2},{4,5},{5,4},{6,7},{7,6},{8,9},{9,8},{10,11... | collective-permute-start | bytes 4325384 | tf_op jit(solution)/shard_map/ppermute | solution.py:391
  21.6 3.1 %collective-permute-done.4 = bf16[16,352,128]{2,1,0:T(8,128)(2,1)S(1)} collective-permute-done((bf16[16,352,128]{2,1,0:T(8,128)(2,1)}, bf16[16,352,128]{2,1,0:T(8,128)(2,1)S(1)}, u32[]{:S(2)}, u32[]{:S(2)}) %collective-permute-start.4) | collective-permute-done | bytes 1441824 | tf_op jit(solution)/shard_map/ppermute | solution.py:391
  24.6 2.9 %add_convert_fusion = bf16[16,352,128]{2,1,0:T(8,128)(2,1)} fusion(bf16[16,352,128]{2,1,0:T(8,128)(2,1)S(1)} %collective-permute-done.4, bf16[16,352,128]{2,1,0:T(8,128)(2,1)} %get-tuple-element.26), kind=kLoop, calls=%fused_computation | loop fusion | flops 2883584 | bytes 4325376 | tf_op jit(solution)/shard_map/convert_element_type | solution.py:445
  27.6 9.7 %all-to-all-start = ((bf16[16,352,128]{2,1,0:T(8,128)(2,1)}), bf16[16,352,128]{2,1,0:T(8,128)(2,1)S(1)}, u32[]{:S(2)}, u32[]{:S(2)}) async-start(bf16[16,352,128]{2,1,0:T(8,128)(2,1)} %add_convert_fusion), calls=%async_computation | async-start | bytes 2883584 | tf_op jit(solution)/shard_map/all_to_all | solution.py:447
  37.3 0.0 copy-start
  37.3 0.0 copy-start.1
  37.3 3.6 %collective-permute-start.5 = (bf16[6,512]{1,0:T(8,128)(2,1)S(1)}, bf16[6,512]{1,0:T(8,128)(2,1)S(1)}, u32[]{:S(2)}, u32[]{:S(2)}) collective-permute-start(bf16[6,512]{1,0:T(8,128)(2,1)S(1)} %copy-done.9), channel_id=1, source_target_pairs={{0,3},{1,2},{2,1},{3,0},{4,7},{5,6},{6,5},{7,4},{8,11},{9,10},{10,... | collective-permute-start | bytes 18440 | tf_op jit(solution)/shard_map/ppermute | solution.py:395
  40.9 0.1 pad.4.clone
  41.0 14.0 %collective-permute-done.5 = bf16[6,512]{1,0:T(8,128)(2,1)S(1)} collective-permute-done((bf16[6,512]{1,0:T(8,128)(2,1)S(1)}, bf16[6,512]{1,0:T(8,128)(2,1)S(1)}, u32[]{:S(2)}, u32[]{:S(2)}) %collective-permute-start.5) | collective-permute-done | bytes 6176 | tf_op jit(solution)/shard_map/ppermute | solution.py:395
  55.0 0.0 collective-permute-done.6
  55.0 0.1 pad_maximum_fusion
  55.2 1.5 %collective-permute-start.7 = (bf16[16,512]{1,0:T(8,128)(2,1)S(1)}, bf16[16,512]{1,0:T(8,128)(2,1)S(1)}, u32[]{:S(2)}, u32[]{:S(2)}) collective-permute-start(bf16[16,512]{1,0:T(8,128)(2,1)S(1)} %get-tuple-element.40), channel_id=1, source_target_pairs={{0,4},{4,0},{1,5},{5,1},{2,6},{6,2},{3,7},{7,3},{8,12},{12,8},{9,1... | collective-permute-start | bytes 49160 | tf_op jit(solution)/shard_map/ppermute | solution.py:382
  56.7 0.7 collective-permute-start.8
  57.4 0.1 pad.1.clone
  57.4 0.9 %sum_over_near.1 = bf16[8,88,128]{2,1,0:T(8,128)(2,1)} custom-call(bf16[16,352,128]{2,1,0:T(8,128)(2,1)S(1)} %all-to-all-done.in_ref), custom_call_target="tpu_custom_call" | custom-call | tf_op jit(solution)/shard_map/sum_over_near/pallas_call | solution.py:318
  58.3 10.7 %all-to-all-start.1 = ((bf16[8,88,128]{2,1,0:T(8,128)(2,1)}), bf16[8,88,128]{2,1,0:T(8,128)(2,1)S(1)}, u32[]{:S(2)}, u32[]{:S(2)}) async-start(bf16[8,88,128]{2,1,0:T(8,128)(2,1)} %sum_over_near.1), calls=%async_computation.1 | async-start | bytes 360448 | tf_op jit(solution)/shard_map/all_to_all | solution.py:448
  69.0 0.0 collective-permute-done.7
  69.0 0.9 %fusion = f32[4,16,512]{2,1,0:T(8,128)} fusion(bf16[512,512]{1,0:T(8,128)(2,1)S(1)} %copy-done, f32[6,16,512]{2,1,0:T(8,128)S(1)} %pad_maximum_fusion, f32[4,16,512]{2,1,0:T(8,128)S(1)} %bitcast.51, f32[1,16,512]{2,1,0:T(8,128)S(1)} %get-tuple-element.48, f32[1,16,512]{2,1,0:T(8,128)S(1)} %get-tuple-element.47, f32[4]{0:T(128)S(1)} %pad.1.clone), kind=kOutput, calls=%fused_computation.1 | convolution fusion | flops 33718272 | bytes 983552 | tf_op jit(solution)/shard_map/dot_general | solution.py:27
  70.0 8.3 %all-to-all-done.1.in_ref = bf16[8,88,128]{2,1,0:T(8,128)(2,1)S(1)} async-done(((bf16[8,88,128]{2,1,0:T(8,128)(2,1)}), bf16[8,88,128]{2,1,0:T(8,128)(2,1)S(1)}, u32[]{:S(2)}, u32[]{:S(2)}) %all-to-all-start.1) | async-done | bytes 180256 | tf_op jit(solution)/shard_map/all_to_all | solution.py:448
  78.3 4.1 %all-gather = bf16[176,128]{1,0:T(8,128)(2,1)S(1)} all-gather(bf16[88,128]{1,0:T(8,128)(2,1)S(1)} %sum_over_far.1), channel_id=2, replica_groups=mesh['y_lo'=2,'z_hi'=4,'z_lo'=2,'x_hi'=2,'x_lo'=2,'y_hi'=2,'core'=2] {'c..., dimensions={0}, use_global_device_ids=true | all-gather | bytes 67584 | tf_op jit(solution)/shard_map/all_gather | solution.py:449
  82.4 0.6 share_over_core.1
  (33 shorter events, 0.2 us)
Async XLA Ops:
  1.5 5.7 %collective-permute-start = (bf16[4,512]{1,0:T(4,128)(2,1)S(1)}, bf16[4,512]{1,0:T(4,128)(2,1)S(1)}, u32[]{:S(2)}, u32[]{:S(2)}) collective-permute-start(bf16[4,512]{1,0:T(4,128)(2,1)S(1)} %get-tuple-element.51), channel_id=1, source_target_pairs={{0,3},{1,2},{2,1},{3,0},{4,7},{5,6},{6,5},{7,4},{8,11},{9,10},{10,... | collective-permute-start | bytes 12296 | tf_op jit(solution)/shard_map/ppermute | solution.py:395
  5.8 1.3 %collective-permute-start.1 = (bf16[4,512]{1,0:T(4,128)(2,1)S(1)}, bf16[4,512]{1,0:T(4,128)(2,1)S(1)}, u32[]{:S(2)}, u32[]{:S(2)}) collective-permute-start(bf16[4,512]{1,0:T(4,128)(2,1)S(1)} %get-tuple-element.52), channel_id=1, source_target_pairs={{0,1},{1,0},{2,3},{3,2},{4,5},{5,4},{6,7},{7,6},{8,9},{9,8},{10,11... | collective-permute-start | bytes 12296 | tf_op jit(solution)/shard_map/ppermute | solution.py:391
  7.1 2.9 %copy-start.6 = (bf16[4,512]{1,0:T(4,128)(2,1)}, bf16[4,512]{1,0:T(4,128)(2,1)S(1)}, u32[]{:S(2)}) copy-start(bf16[4,512]{1,0:T(4,128)(2,1)S(1)} %collective-permute-done.opposite_hbm) | copy-start | bytes 12292
  7.1 2.9 %copy-start.7 = (bf16[4,512]{1,0:T(4,128)(2,1)}, bf16[4,512]{1,0:T(4,128)(2,1)S(1)}, u32[]{:S(2)}) copy-start(bf16[4,512]{1,0:T(4,128)(2,1)S(1)} %collective-permute-done.1.mate_hbm) | copy-start | bytes 12292
  7.2 2.8 %collective-permute-start.2 = (bf16[18,512]{1,0:T(8,128)(2,1)S(1)}, bf16[18,512]{1,0:T(8,128)(2,1)S(1)}, u32[]{:S(2)}, u32[]{:S(2)}) collective-permute-start(bf16[18,512]{1,0:T(8,128)(2,1)S(1)} %get-tuple-element.46), channel_id=1, source_target_pairs={{0,4},{4,0},{1,5},{5,1},{2,6},{6,2},{3,7},{7,3},{8,12},{12,8},{9,1... | collective-permute-start | bytes 55304 | tf_op jit(solution)/shard_map/ppermute | solution.py:382
  8.6 1.4 %collective-permute-start.3 = (bf16[18,512]{1,0:T(8,128)(2,1)S(1)}, bf16[18,512]{1,0:T(8,128)(2,1)S(1)}, u32[]{:S(2)}, u32[]{:S(2)}) collective-permute-start(bf16[18,512]{1,0:T(8,128)(2,1)S(1)} %get-tuple-element.45), channel_id=1, source_target_pairs={{4,8},{12,16},{20,24},{28,32},{36,40},{44,48},{52,56},{60,64},{68,... | collective-permute-start | bytes 55304 | tf_op jit(solution)/shard_map/ppermute | solution.py:387
  10.0 0.6 copy-start.4
  10.0 0.6 copy-start.5
  18.1 6.5 %collective-permute-start.4 = (bf16[16,352,128]{2,1,0:T(8,128)(2,1)}, bf16[16,352,128]{2,1,0:T(8,128)(2,1)S(1)}, u32[]{:S(2)}, u32[]{:S(2)}) collective-permute-start(bf16[16,352,128]{2,1,0:T(8,128)(2,1)} %get-tuple-element.27), channel_id=1, source_target_pairs={{0,1},{1,0},{2,3},{3,2},{4,5},{5,4},{6,7},{7,6},{8,9},{9,8},{10,11... | collective-permute-start | bytes 4325384 | tf_op jit(solution)/shard_map/ppermute | solution.py:391
  27.6 9.7 %copy-start.9 = (bf16[6,512]{1,0:T(8,128)(2,1)S(1)}, bf16[6,512]{1,0:T(8,128)(2,1)}, u32[]{:S(2)}) copy-start(bf16[6,512]{1,0:T(8,128)(2,1)} %get-tuple-element.30) | copy-start | bytes 18436
  27.6 13.3 %copy-start.8 = (bf16[6,512]{1,0:T(8,128)(2,1)S(1)}, bf16[6,512]{1,0:T(8,128)(2,1)}, u32[]{:S(2)}) copy-start(bf16[6,512]{1,0:T(8,128)(2,1)} %get-tuple-element.31) | copy-start | bytes 18436
  27.6 27.6 %copy-start.2 = (f32[16,512]{1,0:T(8,128)S(1)}, f32[16,512]{1,0:T(8,128)}, u32[]{:S(2)}) copy-start(f32[16,512]{1,0:T(8,128)} %get-tuple-element.25) | copy-start | bytes 98308
  27.6 27.6 %copy-start.3 = (f32[16,512]{1,0:T(8,128)S(1)}, f32[16,512]{1,0:T(8,128)}, u32[]{:S(2)}) copy-start(f32[16,512]{1,0:T(8,128)} %get-tuple-element.32) | copy-start | bytes 98308
  27.6 29.9 %all-to-all-start = ((bf16[16,352,128]{2,1,0:T(8,128)(2,1)}), bf16[16,352,128]{2,1,0:T(8,128)(2,1)S(1)}, u32[]{:S(2)}, u32[]{:S(2)}) async-start(bf16[16,352,128]{2,1,0:T(8,128)(2,1)} %add_convert_fusion), calls=%async_computation | async-start | bytes 2883584 | tf_op jit(solution)/shard_map/all_to_all | solution.py:447
  37.3 31.7 %copy-start = (bf16[512,512]{1,0:T(8,128)(2,1)S(1)}, bf16[512,512]{1,0:T(8,128)(2,1)}, u32[]{:S(2)}) copy-start(bf16[512,512]{1,0:T(8,128)(2,1)} %w_em_hbm.1) | copy-start | bytes 1572868
  37.3 31.7 %copy-start.1 = (f32[64,512]{1,0:T(8,128)S(1)}, f32[64,512]{1,0:T(8,128)}, u32[]{:S(2)}) copy-start(f32[64,512]{1,0:T(8,128)} %get-tuple-element.24) | copy-start | bytes 393220
  37.3 17.7 %collective-permute-start.5 = (bf16[6,512]{1,0:T(8,128)(2,1)S(1)}, bf16[6,512]{1,0:T(8,128)(2,1)S(1)}, u32[]{:S(2)}, u32[]{:S(2)}) collective-permute-start(bf16[6,512]{1,0:T(8,128)(2,1)S(1)} %copy-done.9), channel_id=1, source_target_pairs={{0,3},{1,2},{2,1},{3,0},{4,7},{5,6},{6,5},{7,4},{8,11},{9,10},{10,... | collective-permute-start | bytes 18440 | tf_op jit(solution)/shard_map/ppermute | solution.py:395
  40.9 14.1 %collective-permute-start.6 = (bf16[6,512]{1,0:T(8,128)(2,1)S(1)}, bf16[6,512]{1,0:T(8,128)(2,1)S(1)}, u32[]{:S(2)}, u32[]{:S(2)}) collective-permute-start(bf16[6,512]{1,0:T(8,128)(2,1)S(1)} %copy-done.8), channel_id=1, source_target_pairs={{0,1},{1,0},{2,3},{3,2},{4,5},{5,4},{6,7},{7,6},{8,9},{9,8},{10,11... | collective-permute-start | bytes 18440 | tf_op jit(solution)/shard_map/ppermute | solution.py:391
  55.2 13.8 %collective-permute-start.7 = (bf16[16,512]{1,0:T(8,128)(2,1)S(1)}, bf16[16,512]{1,0:T(8,128)(2,1)S(1)}, u32[]{:S(2)}, u32[]{:S(2)}) collective-permute-start(bf16[16,512]{1,0:T(8,128)(2,1)S(1)} %get-tuple-element.40), channel_id=1, source_target_pairs={{0,4},{4,0},{1,5},{5,1},{2,6},{6,2},{3,7},{7,3},{8,12},{12,8},{9,1... | collective-permute-start | bytes 49160 | tf_op jit(solution)/shard_map/ppermute | solution.py:382
  56.7 12.3 %collective-permute-start.8 = (bf16[16,512]{1,0:T(8,128)(2,1)S(1)}, bf16[16,512]{1,0:T(8,128)(2,1)S(1)}, u32[]{:S(2)}, u32[]{:S(2)}) collective-permute-start(bf16[16,512]{1,0:T(8,128)(2,1)S(1)} %get-tuple-element.39), channel_id=1, source_target_pairs={{4,8},{12,16},{20,24},{28,32},{36,40},{44,48},{52,56},{60,64},{68,... | collective-permute-start | bytes 49160 | tf_op jit(solution)/shard_map/ppermute | solution.py:387
  58.3 19.9 %all-to-all-start.1 = ((bf16[8,88,128]{2,1,0:T(8,128)(2,1)}), bf16[8,88,128]{2,1,0:T(8,128)(2,1)S(1)}, u32[]{:S(2)}, u32[]{:S(2)}) async-start(bf16[8,88,128]{2,1,0:T(8,128)(2,1)} %sum_over_near.1), calls=%async_computation.1 | async-start | bytes 360448 | tf_op jit(solution)/shard_map/all_to_all | solution.py:448

commit v7 on v6

--- a/solution.py
+++ b/solution.py
@@ -443,18 +443,19 @@
     )
     got = to_mate(send)
     chunks = (keep.astype(F32) + got.astype(F32)).astype(BF)
-    chunks, mate, opposite = lax.optimization_barrier((chunks, mate, opposite))
-    chunks = lax.all_to_all(chunks, NEAR, 0, 0, tiled=True)
-    chunks = lax.all_to_all(near_sum(chunks), FAR, 0, 0, tiled=True)
-    grads = last(lax.all_gather(far_sum(chunks), "core", axis=0, tiled=False))
-
     mate = to_mate(mate).astype(F32)
     opposite = to_opposite(opposite).astype(F32)
     west = jnp.where(core == 0, opposite, mate)
     east = jnp.where(core == 0, mate, opposite)
     sides = jnp.concatenate([west[:, None], jnp.zeros((6, 14, D), F32), east[:, None]], axis=1)
-    pair = to_pair((pair + sides[4]).astype(BF)).astype(F32)
-    other = to_other((other + sides[5]).astype(BF)).astype(F32)
+    pair, other = (pair + sides[4]).astype(BF), (other + sides[5]).astype(BF)
+    chunks, pair, other = lax.optimization_barrier((chunks, pair, other))
+    chunks = lax.all_to_all(chunks, NEAR, 0, 0, tiled=True)
+    chunks = lax.all_to_all(near_sum(chunks), FAR, 0, 0, tiled=True)
+    grads = last(lax.all_gather(far_sum(chunks), "core", axis=0, tiled=False))
+
+    pair = to_pair(pair).astype(F32)
+    other = to_other(other).astype(F32)
     top = jnp.where(odd == 1, pair, other)
     bottom = jnp.where(odd == 1, other, pair)
     ends = jnp.stack([top, jnp.zeros_like(top), jnp.zeros_like(top), bottom])

time: 83.8 us -> 86.8 us (1.036)
  waiting for transfers between devices: 26 us -> 30.9 us
  starting transfers between devices: 35.9 us -> 33.9 us
    all_to_all x1, waiting for transfers between devices: 0.01 us -> 18.8 us  [on_device(): chunks = lax.all_to_all(chunks, NEAR, 0, 0, tiled=True)]
    ppermute x2, waiting for transfers between devices: 14.6 us -> 3.67 us  [to_opposite(): return lax.ppermute(value, LON, [(i, 3 - i) for i in range(4)])]
    ppermute x3, waiting for transfers between devices: 3.06 us -> 0.01 us  [to_mate(): return lax.ppermute(value, 'core', [(0, 1), (1, 0)])]
    ppermute x2, starting transfers between devices: 7.96 us -> 5.57 us  [to_opposite(): return lax.ppermute(value, LON, [(i, 3 - i) for i in range(4)])]
  transfers between devices with their start and end apart: 11 -> 11, of which waited for: 5 -> 5; matrix products, arithmetic and copies ran while one was open for 2% -> 3% of each run, Pallas kernels for 1% -> 1%
where the time goes in v7:
time: 86.8 us; the launch traced here: 86.2 us
  starting transfers between devices  33.9 us (39%)
  waiting for transfers between devices  30.9 us (36%)
  Pallas kernels  9.08 us (10%)
  other arithmetic  3.87 us (4%)
  blocking collectives  3.77 us (4%)
  local copies, waits for them, and re-layouts  2.33 us (3%)
  between operations  1.47 us (2%)
  matrix products  0.94 us (1%)
    all_to_all x1, waiting for transfers between devices, on_device(): chunks = lax.all_to_all(chunks, NEAR, 0, 0, tiled=True)  18.8 us
    all_to_all x1, starting transfers between devices, on_device(): chunks = lax.all_to_all(near_sum(chunks), FAR, 0, 0, tiled=True)  10.8 us
    all_to_all x1, starting transfers between devices, on_device(): chunks = lax.all_to_all(chunks, NEAR, 0, 0, tiled=True)  9.57 us
    all_to_all x1, waiting for transfers between devices, on_device(): chunks = lax.all_to_all(near_sum(chunks), FAR, 0, 0, tiled=True)  8.3 us
    pallas_call x1, Pallas kernels, main_call(): pl.pallas_call(main_kernel, out_shape=(shape((64, D), F32), shape((16, D)...  7.54 us
    ppermute x2, starting transfers between devices, to_opposite(): return lax.ppermute(value, LON, [(i, 3 - i) for i in range(4)])  5.57 us
    ppermute x3, starting transfers between devices, to_mate(): return lax.ppermute(value, 'core', [(0, 1), (1, 0)])  3.84 us
    all_gather x1, blocking collectives, on_device(): grads = last(lax.all_gather(far_sum(chunks), 'core', axis=0, tiled=False))  3.77 us
  transfers between devices with their start and end apart: 11, of which 5 were waited for; matrix products, arithmetic and copies ran while one was open for 3% of the time, Pallas kernels for 1%

profile of v7, /device:TPU:1, one launch (start us, length us, event | category | flops | bytes accessed | tf_op | source)
XLA Modules:
  0.0 86.2 jit_solution(12011176979352767586)
XLA Ops:
  0.6 0.8 fusion.14
  1.5 4.4 %collective-permute-start = (bf16[4,512]{1,0:T(4,128)(2,1)S(1)}, bf16[4,512]{1,0:T(4,128)(2,1)S(1)}, u32[]{:S(2)}, u32[]{:S(2)}) collective-permute-start(bf16[4,512]{1,0:T(4,128)(2,1)S(1)} %get-tuple-element.51), channel_id=1, source_target_pairs={{0,3},{1,2},{2,1},{3,0},{4,7},{5,6},{6,5},{7,4},{8,11},{9,10},{10,... | collective-permute-start | bytes 12296 | tf_op jit(solution)/shard_map/ppermute | solution.py:395
  5.8 0.0 collective-permute-start.1
  5.9 0.7 slice_bitcast_fusion.3
  6.6 0.6 collective-permute-done.opposite_hbm
  7.2 1.3 %collective-permute-start.2 = (bf16[18,512]{1,0:T(8,128)(2,1)S(1)}, bf16[18,512]{1,0:T(8,128)(2,1)S(1)}, u32[]{:S(2)}, u32[]{:S(2)}) collective-permute-start(bf16[18,512]{1,0:T(8,128)(2,1)S(1)} %get-tuple-element.46), channel_id=1, source_target_pairs={{0,4},{4,0},{1,5},{5,1},{2,6},{6,2},{3,7},{7,3},{8,12},{12,8},{9,1... | collective-permute-start | bytes 55304 | tf_op jit(solution)/shard_map/ppermute | solution.py:382
  8.6 0.7 collective-permute-start.3
  9.9 0.1 collective-permute-done.2.pair_hbm
  10.0 0.6 copy-done.2
  10.6 0.0 copy-done.3
  10.6 7.5 %decoder_grads.1 = (f32[64,512]{1,0:T(8,128)}, f32[16,512]{1,0:T(8,128)}, f32[16,512]{1,0:T(8,128)}, bf16[6,512]{1,0:T(8,128)(2,1)}, bf16[6,512]{1,0:T(8,128)(2,...) custom-call(s32[1]{0:T(128)} %bitcast.core_ref, s32[1]{0:T(128)} %bitcast.1.odd_ref, ...), custom_call_target="tpu_custom_call" | custom-call | tf_op jit(solution)/shard_map/decoder_grads/pallas_call | solution.py:270
  18.1 3.4 %collective-permute-start.4 = (bf16[16,352,128]{2,1,0:T(8,128)(2,1)}, bf16[16,352,128]{2,1,0:T(8,128)(2,1)S(1)}, u32[]{:S(2)}, u32[]{:S(2)}) collective-permute-start(bf16[16,352,128]{2,1,0:T(8,128)(2,1)} %get-tuple-element.26), channel_id=1, source_target_pairs={{0,1},{1,0},{2,3},{3,2},{4,5},{5,4},{6,7},{7,6},{8,9},{9,8},{10,11... | collective-permute-start | bytes 4325384 | tf_op jit(solution)/shard_map/ppermute | solution.py:391
  21.6 1.2 %collective-permute-start.5 = (bf16[6,512]{1,0:T(8,128)(2,1)}, bf16[6,512]{1,0:T(8,128)(2,1)S(1)}, u32[]{:S(2)}, u32[]{:S(2)}) collective-permute-start(bf16[6,512]{1,0:T(8,128)(2,1)} %get-tuple-element.28), channel_id=1, source_target_pairs={{0,3},{1,2},{2,1},{3,0},{4,7},{5,6},{6,5},{7,4},{8,11},{9,10},{10,... | collective-permute-start | bytes 18440 | tf_op jit(solution)/shard_map/ppermute | solution.py:395
  22.7 0.4 collective-permute-start.6
  23.2 0.1 pad.4.clone
  23.2 3.1 %collective-permute-done.5 = bf16[6,512]{1,0:T(8,128)(2,1)S(1)} collective-permute-done((bf16[6,512]{1,0:T(8,128)(2,1)}, bf16[6,512]{1,0:T(8,128)(2,1)S(1)}, u32[]{:S(2)}, u32[]{:S(2)}) %collective-permute-start.5) | collective-permute-done | bytes 6176 | tf_op jit(solution)/shard_map/ppermute | solution.py:395
  26.4 0.1 pad_maximum_fusion
  26.5 0.8 fusion.8
  27.3 2.9 %add_convert_fusion = bf16[16,352,128]{2,1,0:T(8,128)(2,1)} fusion(bf16[16,352,128]{2,1,0:T(8,128)(2,1)S(1)} %collective-permute-done.4, bf16[16,352,128]{2,1,0:T(8,128)(2,1)} %get-tuple-element.25), kind=kLoop, calls=%fused_computation | loop fusion | flops 2883584 | bytes 4325376 | tf_op jit(solution)/shard_map/convert_element_type | solution.py:445
  30.2 9.6 %all-to-all-start = ((bf16[16,352,128]{2,1,0:T(8,128)(2,1)}), bf16[16,352,128]{2,1,0:T(8,128)(2,1)S(1)}, u32[]{:S(2)}, u32[]{:S(2)}) async-start(bf16[16,352,128]{2,1,0:T(8,128)(2,1)} %add_convert_fusion), calls=%async_computation | async-start | bytes 2883584 | tf_op jit(solution)/shard_map/all_to_all | solution.py:453
  39.8 0.0 copy-start
  39.8 0.0 copy-start.1
  39.8 1.4 %collective-permute-start.7 = (bf16[16,512]{1,0:T(8,128)(2,1)S(1)}, bf16[16,512]{1,0:T(8,128)(2,1)S(1)}, u32[]{:S(2)}, u32[]{:S(2)}) collective-permute-start(bf16[16,512]{1,0:T(8,128)(2,1)S(1)} %get-tuple-element.31), channel_id=1, source_target_pairs={{0,4},{4,0},{1,5},{5,1},{2,6},{6,2},{3,7},{7,3},{8,12},{12,8},{9,1... | collective-permute-start | bytes 49160 | tf_op jit(solution)/shard_map/ppermute | solution.py:382
  41.3 0.7 collective-permute-start.8
  42.0 0.1 pad.1.clone
  42.0 18.8 %all-to-all-done.in_ref = bf16[16,352,128]{2,1,0:T(8,128)(2,1)S(1)} async-done(((bf16[16,352,128]{2,1,0:T(8,128)(2,1)}), bf16[16,352,128]{2,1,0:T(8,128)(2,1)S(1)}, u32[]{:S(2)}, u32[]{:S(2)}) %all-to-all-start) | async-done | bytes 1441824 | tf_op jit(solution)/shard_map/all_to_all | solution.py:453
  60.8 0.9 %sum_over_near.1 = bf16[8,88,128]{2,1,0:T(8,128)(2,1)} custom-call(bf16[16,352,128]{2,1,0:T(8,128)(2,1)S(1)} %all-to-all-done.in_ref), custom_call_target="tpu_custom_call" | custom-call | tf_op jit(solution)/shard_map/sum_over_near/pallas_call | solution.py:318
  61.7 10.8 %all-to-all-start.1 = ((bf16[8,88,128]{2,1,0:T(8,128)(2,1)}), bf16[8,88,128]{2,1,0:T(8,128)(2,1)S(1)}, u32[]{:S(2)}, u32[]{:S(2)}) async-start(bf16[8,88,128]{2,1,0:T(8,128)(2,1)} %sum_over_near.1), calls=%async_computation.1 | async-start | bytes 360448 | tf_op jit(solution)/shard_map/all_to_all | solution.py:454
  72.5 0.9 %fusion = f32[4,16,512]{2,1,0:T(8,128)} fusion(bf16[512,512]{1,0:T(8,128)(2,1)S(1)} %copy-done, f32[6,16,512]{2,1,0:T(8,128)S(1)} %pad_maximum_fusion, f32[4,16,512]{2,1,0:T(8,128)S(1)} %bitcast.51, f32[1,16,512]{2,1,0:T(8,128)S(1)} %get-tuple-element.48, f32[1,16,512]{2,1,0:T(8,128)S(1)} %get-tuple-element.47, f32[4]{0:T(128)S(1)} %pad.1.clone), kind=kOutput, calls=%fused_computation.1 | convolution fusion | flops 33718272 | bytes 983552 | tf_op jit(solution)/shard_map/dot_general | solution.py:27
  73.5 8.3 %all-to-all-done.1.in_ref = bf16[8,88,128]{2,1,0:T(8,128)(2,1)S(1)} async-done(((bf16[8,88,128]{2,1,0:T(8,128)(2,1)}), bf16[8,88,128]{2,1,0:T(8,128)(2,1)S(1)}, u32[]{:S(2)}, u32[]{:S(2)}) %all-to-all-start.1) | async-done | bytes 180256 | tf_op jit(solution)/shard_map/all_to_all | solution.py:454
  81.8 3.8 %all-gather = bf16[176,128]{1,0:T(8,128)(2,1)S(1)} all-gather(bf16[88,128]{1,0:T(8,128)(2,1)S(1)} %sum_over_far.1), channel_id=2, replica_groups=mesh['y_lo'=2,'z_hi'=4,'z_lo'=2,'x_hi'=2,'x_lo'=2,'y_hi'=2,'core'=2] {'c..., dimensions={0}, use_global_device_ids=true | all-gather | bytes 67584 | tf_op jit(solution)/shard_map/all_gather | solution.py:455
  85.6 0.6 share_over_core.1
  (25 shorter events, 0.2 us)
Async XLA Ops:
  1.5 5.7 %collective-permute-start = (bf16[4,512]{1,0:T(4,128)(2,1)S(1)}, bf16[4,512]{1,0:T(4,128)(2,1)S(1)}, u32[]{:S(2)}, u32[]{:S(2)}) collective-permute-start(bf16[4,512]{1,0:T(4,128)(2,1)S(1)} %get-tuple-element.51), channel_id=1, source_target_pairs={{0,3},{1,2},{2,1},{3,0},{4,7},{5,6},{6,5},{7,4},{8,11},{9,10},{10,... | collective-permute-start | bytes 12296 | tf_op jit(solution)/shard_map/ppermute | solution.py:395
  5.8 1.3 %collective-permute-start.1 = (bf16[4,512]{1,0:T(4,128)(2,1)S(1)}, bf16[4,512]{1,0:T(4,128)(2,1)S(1)}, u32[]{:S(2)}, u32[]{:S(2)}) collective-permute-start(bf16[4,512]{1,0:T(4,128)(2,1)S(1)} %get-tuple-element.52), channel_id=1, source_target_pairs={{0,1},{1,0},{2,3},{3,2},{4,5},{5,4},{6,7},{7,6},{8,9},{9,8},{10,11... | collective-permute-start | bytes 12296 | tf_op jit(solution)/shard_map/ppermute | solution.py:391
  7.1 2.9 %copy-start.4 = (bf16[4,512]{1,0:T(4,128)(2,1)}, bf16[4,512]{1,0:T(4,128)(2,1)S(1)}, u32[]{:S(2)}) copy-start(bf16[4,512]{1,0:T(4,128)(2,1)S(1)} %collective-permute-done.opposite_hbm) | copy-start | bytes 12292
  7.1 2.9 %copy-start.5 = (bf16[4,512]{1,0:T(4,128)(2,1)}, bf16[4,512]{1,0:T(4,128)(2,1)S(1)}, u32[]{:S(2)}) copy-start(bf16[4,512]{1,0:T(4,128)(2,1)S(1)} %collective-permute-done.1.mate_hbm) | copy-start | bytes 12292
  7.2 2.8 %collective-permute-start.2 = (bf16[18,512]{1,0:T(8,128)(2,1)S(1)}, bf16[18,512]{1,0:T(8,128)(2,1)S(1)}, u32[]{:S(2)}, u32[]{:S(2)}) collective-permute-start(bf16[18,512]{1,0:T(8,128)(2,1)S(1)} %get-tuple-element.46), channel_id=1, source_target_pairs={{0,4},{4,0},{1,5},{5,1},{2,6},{6,2},{3,7},{7,3},{8,12},{12,8},{9,1... | collective-permute-start | bytes 55304 | tf_op jit(solution)/shard_map/ppermute | solution.py:382
  8.6 1.4 %collective-permute-start.3 = (bf16[18,512]{1,0:T(8,128)(2,1)S(1)}, bf16[18,512]{1,0:T(8,128)(2,1)S(1)}, u32[]{:S(2)}, u32[]{:S(2)}) collective-permute-start(bf16[18,512]{1,0:T(8,128)(2,1)S(1)} %get-tuple-element.45), channel_id=1, source_target_pairs={{4,8},{12,16},{20,24},{28,32},{36,40},{44,48},{52,56},{60,64},{68,... | collective-permute-start | bytes 55304 | tf_op jit(solution)/shard_map/ppermute | solution.py:387
  10.0 0.6 copy-start.2
  10.0 0.6 copy-start.3
  18.1 9.2 %collective-permute-start.4 = (bf16[16,352,128]{2,1,0:T(8,128)(2,1)}, bf16[16,352,128]{2,1,0:T(8,128)(2,1)S(1)}, u32[]{:S(2)}, u32[]{:S(2)}) collective-permute-start(bf16[16,352,128]{2,1,0:T(8,128)(2,1)} %get-tuple-element.26), channel_id=1, source_target_pairs={{0,1},{1,0},{2,3},{3,2},{4,5},{5,4},{6,7},{7,6},{8,9},{9,8},{10,11... | collective-permute-start | bytes 4325384 | tf_op jit(solution)/shard_map/ppermute | solution.py:391
  21.6 4.8 %collective-permute-start.5 = (bf16[6,512]{1,0:T(8,128)(2,1)}, bf16[6,512]{1,0:T(8,128)(2,1)S(1)}, u32[]{:S(2)}, u32[]{:S(2)}) collective-permute-start(bf16[6,512]{1,0:T(8,128)(2,1)} %get-tuple-element.28), channel_id=1, source_target_pairs={{0,3},{1,2},{2,1},{3,0},{4,7},{5,6},{6,5},{7,4},{8,11},{9,10},{10,... | collective-permute-start | bytes 18440 | tf_op jit(solution)/shard_map/ppermute | solution.py:395
  22.7 3.6 %collective-permute-start.6 = (bf16[6,512]{1,0:T(8,128)(2,1)}, bf16[6,512]{1,0:T(8,128)(2,1)S(1)}, u32[]{:S(2)}, u32[]{:S(2)}) collective-permute-start(bf16[6,512]{1,0:T(8,128)(2,1)} %get-tuple-element.29), channel_id=1, source_target_pairs={{0,1},{1,0},{2,3},{3,2},{4,5},{5,4},{6,7},{7,6},{8,9},{9,8},{10,11... | collective-permute-start | bytes 18440 | tf_op jit(solution)/shard_map/ppermute | solution.py:391
  30.2 30.6 %all-to-all-start = ((bf16[16,352,128]{2,1,0:T(8,128)(2,1)}), bf16[16,352,128]{2,1,0:T(8,128)(2,1)S(1)}, u32[]{:S(2)}, u32[]{:S(2)}) async-start(bf16[16,352,128]{2,1,0:T(8,128)(2,1)} %add_convert_fusion), calls=%async_computation | async-start | bytes 2883584 | tf_op jit(solution)/shard_map/all_to_all | solution.py:453
  39.8 32.7 %copy-start = (bf16[512,512]{1,0:T(8,128)(2,1)S(1)}, bf16[512,512]{1,0:T(8,128)(2,1)}, u32[]{:S(2)}) copy-start(bf16[512,512]{1,0:T(8,128)(2,1)} %w_em_hbm.1) | copy-start | bytes 1572868
  39.8 32.7 %copy-start.1 = (f32[64,512]{1,0:T(8,128)S(1)}, f32[64,512]{1,0:T(8,128)}, u32[]{:S(2)}) copy-start(f32[64,512]{1,0:T(8,128)} %get-tuple-element.24) | copy-start | bytes 393220
  39.8 32.6 %collective-permute-start.7 = (bf16[16,512]{1,0:T(8,128)(2,1)S(1)}, bf16[16,512]{1,0:T(8,128)(2,1)S(1)}, u32[]{:S(2)}, u32[]{:S(2)}) collective-permute-start(bf16[16,512]{1,0:T(8,128)(2,1)S(1)} %get-tuple-element.31), channel_id=1, source_target_pairs={{0,4},{4,0},{1,5},{5,1},{2,6},{6,2},{3,7},{7,3},{8,12},{12,8},{9,1... | collective-permute-start | bytes 49160 | tf_op jit(solution)/shard_map/ppermute | solution.py:382
  41.3 31.2 %collective-permute-start.8 = (bf16[16,512]{1,0:T(8,128)(2,1)S(1)}, bf16[16,512]{1,0:T(8,128)(2,1)S(1)}, u32[]{:S(2)}, u32[]{:S(2)}) collective-permute-start(bf16[16,512]{1,0:T(8,128)(2,1)S(1)} %get-tuple-element.32), channel_id=1, source_target_pairs={{4,8},{12,16},{20,24},{28,32},{36,40},{44,48},{52,56},{60,64},{68,... | collective-permute-start | bytes 49160 | tf_op jit(solution)/shard_map/ppermute | solution.py:387
  61.7 20.1 %all-to-all-start.1 = ((bf16[8,88,128]{2,1,0:T(8,128)(2,1)}), bf16[8,88,128]{2,1,0:T(8,128)(2,1)S(1)}, u32[]{:S(2)}, u32[]{:S(2)}) async-start(bf16[8,88,128]{2,1,0:T(8,128)(2,1)} %sum_over_near.1), calls=%async_computation.1 | async-start | bytes 360448 | tf_op jit(solution)/shard_map/all_to_all | solution.py:454
